TPU v7x, 128 devices: a whole 4x4x4 slice. The times are simulated.
128 devices in a mesh: fsdp: 4 (over z_hi, core), expert: 8 (over y, z_lo), tensor: 4 (over x).
Axes of the slice: x: 4, y: 4, z: 4 (z_hi: 2, z_lo: 2; z = z_hi * 2 + z_lo), core: 2. Of those that a mesh axis runs over, the one named last changes fastest.
Arguments:
- attn_partial: bfloat16 [4, 16384, 7168], P('tensor', ('fsdp', 'expert')), may hold values from -6 to 6
- residual: bfloat16 [16384, 7168], P(('fsdp', 'expert', 'tensor')), may hold values from -6 to 6
- gain: float32 [7168], replicated, may hold values from 0.1 to 1.9
- expert_ids: int32 [16384, 8], P(('fsdp', 'expert', 'tensor')), may hold values from 0 to 255, all different within a row; in each aligned block of 128 rows (0 to 127, 128 to 255, ...) at most 5 rows name the same one
- gate_vals: float32 [16384, 8], P(('fsdp', 'expert', 'tensor')), may hold values from 0.1 to 1
- w_gate: bfloat16 [8, 7168, 2048], P('expert', 'fsdp', 'tensor'), may hold values from -0.0625 to 0.0625
- w_up: bfloat16 [8, 7168, 2048], P('expert', 'fsdp', 'tensor'), may hold values from -0.0625 to 0.0625
- w_down: bfloat16 [8, 2048, 7168], P('expert', 'tensor', 'fsdp'), may hold values from -0.125 to 0.125
Outputs:
- hidden: bfloat16 [16384, 7168], P(('fsdp', 'expert', 'tensor'))
- moe_out: bfloat16 [16384, 7168], P(('fsdp', 'expert', 'tensor'))
Inputs may be any that keep to these rules, and one draw needn't show every extreme that they name: `expert_ids`: each row names 8 different experts. Within the rows of one device an expert is named at most 5 times.
All inputs are finite; a program needn't handle non-finite values.
Results may differ from a plain program's by a relative error of at most 0.03.
Values may be sent and summed in bfloat16 or wider, within the bound.
No kernel may reach another device: no remote copies, remote signals or barrier semaphores. Data moves between devices by JAX's collectives and lax.ppermute only.
A program may use at most 128 MiB of HBM per device.

v0:
```python
import jax
import jax.numpy as jnp
from jax import lax
from jax.sharding import PartitionSpec as P

CAP = 5


quant_range = 240.0


def local(attn_partial, residual, gain, expert_ids, gate_vals, w_gate, w_up, w_down):
    token_count = residual.shape[0]
    width = residual.shape[1]
    nscale = width // 128
    experts_here = lax.axis_size("expert")
    tensor_count = lax.axis_size("tensor")
    own_partial = attn_partial[0]
    head_total = lax.psum_scatter(
        own_partial.astype(jnp.float32).astype(jnp.bfloat16),
        "tensor",
        scatter_dimension=0,
        tiled=True,
    ).astype(jnp.float32)
    hidden = (residual.astype(jnp.float32) + head_total).astype(jnp.bfloat16)
    values = hidden.astype(jnp.float32)
    meansq = jnp.mean(values * values, axis=-1, keepdims=True)
    normed = values * lax.rsqrt(meansq + 1e-06) * gain
    blocks = normed.reshape(token_count, nscale, 128)
    largest = jnp.max(jnp.abs(blocks), axis=-1)
    scales = ((largest + 1e-06) / quant_range).astype(jnp.bfloat16)
    quantized = (
        (blocks / scales.astype(jnp.float32)[..., None])
        .astype(jnp.bfloat16)
        .reshape(token_count, width)
    )
    expert_range = jnp.arange(experts_here, dtype=jnp.int32)
    matched = expert_ids[:, :, None] == expert_range[None, None, :]
    routed = jnp.any(matched, axis=1)
    weight = jnp.sum(jnp.where(matched, gate_vals[:, :, None], jnp.float32(0.0)), axis=1)
    slots = jnp.cumsum(routed.astype(jnp.int32), axis=0) - 1
    slot_range = jnp.arange(CAP, dtype=jnp.int32)
    placing = (slots.T[:, None, :] == slot_range[None, :, None]) & routed.T[:, None, :]
    placing_bf = placing.astype(jnp.bfloat16)
    send_rows = jnp.einsum(
        "ecr,rd->ecd", placing_bf, quantized, preferred_element_type=jnp.float32
    ).astype(jnp.bfloat16)
    send_scales = jnp.einsum(
        "ecr,rb->ecb", placing_bf, scales, preferred_element_type=jnp.float32
    ).astype(jnp.bfloat16)
    wide_rows = jnp.broadcast_to(
        send_rows[:, None], (experts_here, tensor_count, CAP, width)
    ).reshape(experts_here * tensor_count, CAP, width)
    wide_scales = jnp.broadcast_to(
        send_scales[:, None], (experts_here, tensor_count, CAP, nscale)
    ).reshape(experts_here * tensor_count, CAP, nscale)
    got_rows, got_scales = (
        lax.all_to_all(wide_rows, ("expert", "tensor"), split_axis=0, concat_axis=0, tiled=True),
        lax.all_to_all(wide_scales, ("expert", "tensor"), split_axis=0, concat_axis=0, tiled=True),
    )
    sources = got_rows.shape[0]
    row_total = sources * CAP
    dequant = (
        got_rows.reshape(row_total, nscale, 128).astype(jnp.float32)
        * got_scales.reshape(row_total, nscale).astype(jnp.float32)[..., None]
    )
    inputs = dequant.reshape(row_total, width).astype(jnp.bfloat16)
    gate_next = jnp.dot(
        inputs,
        lax.all_gather(w_gate[0], "fsdp", axis=0, tiled=True),
        preferred_element_type=jnp.float32,
    )
    up_next = jnp.dot(
        inputs,
        lax.all_gather(w_up[0], "fsdp", axis=0, tiled=True),
        preferred_element_type=jnp.float32,
    )
    middle = (jax.nn.silu(gate_next) * up_next).astype(jnp.bfloat16)
    partial_value = jnp.dot(
        middle,
        lax.all_gather(w_down[0], "fsdp", axis=1, tiled=True),
        preferred_element_type=jnp.float32,
    ).astype(jnp.bfloat16)
    partial_value = partial_value.reshape(sources, CAP, width)
    returned = lax.all_to_all(
        partial_value, ("expert", "tensor"), split_axis=0, concat_axis=0, tiled=True
    )
    expert_out = jnp.sum(
        returned.reshape(experts_here, tensor_count, CAP, width).astype(jnp.float32), axis=1
    )
    slot_index = jnp.clip(slots, 0, CAP - 1)
    taken = expert_out[expert_range[None, :], slot_index]
    factor = weight * routed.astype(jnp.float32)
    mixture = jnp.sum(factor[:, :, None] * taken, axis=1)
    return (hidden, mixture.astype(jnp.bfloat16))


def solution(mesh):
    placed = (
        P("tensor", ("fsdp", "expert"), None),
        P(("fsdp", "expert", "tensor"), None),
        P(),
        P(("fsdp", "expert", "tensor"), None),
        P(("fsdp", "expert", "tensor"), None),
        P("expert", "fsdp", "tensor"),
        P("expert", "fsdp", "tensor"),
        P("expert", "tensor", "fsdp"),
    )
    return jax.shard_map(
        local,
        mesh=mesh,
        in_specs=placed,
        out_specs=(P(("fsdp", "expert", "tensor"), None), P(("fsdp", "expert", "tensor"), None)),
        check_vma=False,
    )
```

profile of v0, /device:TPU:0, one launch (start us, length us, event | category | flops | bytes accessed | tf_op | source)
XLA Modules:
  0.0 356.0 jit_solution(11269773046969324359)
XLA Ops:
  8.0 0.0 reduce-scatter.2.cloned.1.call-start
  8.0 0.7 reduce-scatter.2.cloned.1.call-update
  8.7 0.0 all-gather.7.cloned.1.call-start
  8.8 0.5 all-gather.7.cloned.1.call-update
  9.3 0.0 all-gather.11.cloned.1.call-start
  9.4 0.5 all-gather.11.cloned.1.call-update
  9.9 0.0 all-gather.9.cloned.1.call-start
  10.0 0.5 all-gather.9.cloned.1.call-update
  10.5 0.1 copy.40
  10.6 0.2 reduce_window_sum.11
  10.9 75.4 %reduce-scatter.2.cloned.1.call-done = bf16[128,7168]{1,0:T(8,128)(2,1)} async-done(((bf16[512,7168]{1,0:T(8,128)(2,1)}), bf16[128,7168]{1,0:T(8,128)(2,1)}) %reduce-scatter.2.cloned.1.call-update) | async-done | bytes 1835024 | tf_op jit(solution)/shard_map/reduce_scatter | solution.py:19
  86.2 2.8 fusion.7
  89.0 0.0 copy-start.1
  89.1 0.6 fusion.11
  89.7 2.5 copy.47
  92.2 3.1 reduce_max.9
  95.2 0.1 copy.42
  95.3 0.1 copy.43
  95.4 0.1 convolution_convert_fusion.2
  95.6 0.7 reshape.104
  96.3 6.7 %all-to-all-start.1 = ((bf16[32,2,140]{2,1,0:T(2,128)(2,1)}), bf16[32,2,140]{2,1,0:T(2,128)(2,1)S(1)}, u32[]{:S(2)}, u32[]{:S(2)}) async-start(bf16[32,2,140]{2,1,0:T(2,128)(2,1)} %reshape.104), calls=%async_computation.2 | async-start | bytes 65536 | tf_op jit(solution)/shard_map/all_to_all | solution.py:59
  103.0 1.0 div.31
  104.1 1.1 convolution_convert_fusion.1
  105.1 0.3 copy.44
  105.5 5.9 %all-to-all-done.1 = bf16[32,2,140]{2,1,0:T(2,128)(2,1)S(1)} async-done(((bf16[32,2,140]{2,1,0:T(2,128)(2,1)}), bf16[32,2,140]{2,1,0:T(2,128)(2,1)S(1)}, u32[]{:S(2)}, u32[]{:S(2)}) %all-to-all-start.1) | async-done | bytes 17952 | tf_op jit(solution)/shard_map/all_to_all | solution.py:59
  111.4 2.3 broadcast_in_dim.20
  113.7 5.0 %all-to-all-start = ((bf16[32,5,7168]{2,1,0:T(8,128)(2,1)}), bf16[32,5,7168]{2,1,0:T(8,128)(2,1)}, u32[]{:S(2)}, u32[]{:S(2)}) async-start(bf16[32,5,7168]{2,1,0:T(8,128)(2,1)} %bitcast.55), calls=%async_computation.1 | async-start | bytes 7340032 | tf_op jit(solution)/shard_map/all_to_all | solution.py:58
  118.8 0.1 reshape.105
  118.9 44.9 %all-to-all-done = bf16[32,5,7168]{2,1,0:T(8,128)(2,1)} async-done(((bf16[32,5,7168]{2,1,0:T(8,128)(2,1)}), bf16[32,5,7168]{2,1,0:T(8,128)(2,1)}, u32[]{:S(2)}, u32[]{:S(2)}) %all-to-all-start) | async-done | bytes 2293792 | tf_op jit(solution)/shard_map/all_to_all | solution.py:58
  163.8 5.1 %reshape.90 = f32[160,7168]{1,0:T(8,128)} reshape(bf16[32,5,7168]{2,1,0:T(8,128)(2,1)} %all-to-all-done) | data formatting | bytes 6881280 | tf_op jit(solution)/shard_map/convert_element_type | solution.py:64
  168.9 1.3 mul.55
  170.2 1.0 copy-done
  171.2 1.0 fusion.6
  172.2 0.0 all-gather.7.cloned.1.call-done
  172.3 4.4 %fusion.4 = f32[160,512]{1,0:T(8,128)S(1)} fusion(bf16[160,7168]{1,0:T(8,128)(2,1)S(1)} %fusion.6, bf16[1,7168,512]{2,1,0:T(8,128)(2,1)} %all-gather.7.cloned.1.call-done), kind=kOutput, calls=%fused_computation.9 | convolution fusion | flops 1174405120 | bytes 9961472 | tf_op jit(solution)/shard_map/dot_general | solution.py:68
  176.7 0.0 all-gather.11.cloned.1.call-done
  176.7 46.7 %all-gather.9.cloned.1.call-done = bf16[1,7168,512]{2,1,0:T(8,128)(2,1)} async-done(((bf16[1,1792,512]{2,1,0:T(8,128)(2,1)}), bf16[1,7168,512]{2,1,0:T(8,128)(2,1)}) %all-gather.9.cloned.1.call-update) | async-done | bytes 7340048 | tf_op jit(solution)/shard_map/all_gather | solution.py:75
  223.4 9.2 %convolution_convert_fusion = bf16[160,7168]{1,0:T(8,128)(2,1)} fusion(bf16[1,512,7168]{2,1,0:T(8,128)(2,1)} %all-gather.11.cloned.1.call-done, bf16[160,7168]{1,0:T(8,128)(2,1)S(1)} %fusion.6, bf16[1,7168,512]{2,1,0:T(8,128)(2,1)} %all-gather.9.cloned.1.call-done, f32[160,512]{1,0:T(8,128)S(1)} %fusion.4), kind=kOutput, calls=%fused_computation.3 | convolution fusion | flops 2350448640 | bytes 19595264 | tf_op jit(solution)/shard_map/dot_general | solution.py:79
  232.6 4.5 %reshape.89 = bf16[32,5,7168]{2,1,0:T(8,128)(2,1)} reshape(bf16[160,7168]{1,0:T(8,128)(2,1)} %convolution_convert_fusion) | data formatting | bytes 4587520 | tf_op jit(solution)/shard_map/reshape | solution.py:84
  237.2 7.6 %all-to-all-start.2 = ((bf16[32,5,7168]{2,1,0:T(8,128)(2,1)}), bf16[32,5,7168]{2,1,0:T(8,128)(2,1)}, u32[]{:S(2)}, u32[]{:S(2)}) async-start(bf16[32,5,7168]{2,1,0:T(8,128)(2,1)} %reshape.89), calls=%async_computation.3 | async-start | bytes 7340032 | tf_op jit(solution)/shard_map/all_to_all | solution.py:85
  244.9 0.1 reshape.93
  245.0 0.0 copy-done.4
  245.0 0.1 copy.39
  245.1 46.3 %all-to-all-done.2 = bf16[32,5,7168]{2,1,0:T(8,128)(2,1)} async-done(((bf16[32,5,7168]{2,1,0:T(8,128)(2,1)}), bf16[32,5,7168]{2,1,0:T(8,128)(2,1)}, u32[]{:S(2)}, u32[]{:S(2)}) %all-to-all-start.2) | async-done | bytes 2293792 | tf_op jit(solution)/shard_map/all_to_all | solution.py:85
  291.4 3.0 convert_reduce_fusion
  294.4 0.7 copy.46
  295.1 37.8 %gather_fusion = f32[1024,7168]{1,0:T(8,128)} fusion(f32[8,5,7168]{2,0,1:T(8,128)S(1)} %copy.46, s32[1024]{0:T(1024)S(1)} %reshape.93), kind=kCustom, calls=%fused_computation | custom fusion | bytes 58728448 | tf_op jit(solution)/shard_map/gather | solution.py:92
  332.9 15.5 %fusion = bf16[128,7168]{1,0:T(8,128)(2,1)} fusion(f32[1024,7168]{1,0:T(8,128)} %gather_fusion, f32[128,8]{1,0:T(8,128)S(1)} %copy.39), kind=kLoop, calls=%fused_computation.2 | loop fusion | flops 13762560 | bytes 31199232 | tf_op jit(solution)/shard_map/reduce_sum | solution.py:94
  (19 shorter events, 0.2 us)
Async XLA Ops:
  8.0 78.2 %reduce-scatter.2.cloned.1.call-start = ((), (), s32[]{:S(2)}) async-start(), calls=%async_computation.4 | async-start | bytes 9175040 | tf_op jit(solution)/shard_map/reduce_scatter | solution.py:19
  8.7 1.8 copy-start.3
  8.7 163.5 %all-gather.7.cloned.1.call-start = ((), (), s32[]{:S(2)}) async-start(), calls=%async_computation.5 | async-start | bytes 9175040 | tf_op jit(solution)/shard_map/all_gather | solution.py:70
  9.3 167.4 %all-gather.11.cloned.1.call-start = ((), (), s32[]{:S(2)}) async-start(), calls=%async_computation.7 | async-start | bytes 9175040 | tf_op jit(solution)/shard_map/all_gather | solution.py:81
  9.9 79.1 %copy-start.2 = (f32[7168]{0:T(1024)S(1)}, f32[7168]{0:T(1024)}, u32[]{:S(2)}) copy-start(f32[7168]{0:T(1024)} %param.10) | copy-start | bytes 86020
  9.9 213.5 %all-gather.9.cloned.1.call-start = ((), (), s32[]{:S(2)}) async-start(), calls=%async_computation.6 | async-start | bytes 9175040 | tf_op jit(solution)/shard_map/all_gather | solution.py:75
  89.0 15.0 %copy-start.1 = (bf16[128,7168]{1,0:T(8,128)(2,1)}, bf16[128,7168]{1,0:T(8,128)(2,1)S(1)}, u32[]{:S(2)}) copy-start(bf16[128,7168]{1,0:T(8,128)(2,1)S(1)} %get-tuple-element.3) | copy-start | bytes 5505028
  96.3 15.1 %all-to-all-start.1 = ((bf16[32,2,140]{2,1,0:T(2,128)(2,1)}), bf16[32,2,140]{2,1,0:T(2,128)(2,1)S(1)}, u32[]{:S(2)}, u32[]{:S(2)}) async-start(bf16[32,2,140]{2,1,0:T(2,128)(2,1)} %reshape.104), calls=%async_computation.2 | async-start | bytes 65536 | tf_op jit(solution)/shard_map/all_to_all | solution.py:59
  113.7 50.1 %all-to-all-start = ((bf16[32,5,7168]{2,1,0:T(8,128)(2,1)}), bf16[32,5,7168]{2,1,0:T(8,128)(2,1)}, u32[]{:S(2)}, u32[]{:S(2)}) async-start(bf16[32,5,7168]{2,1,0:T(8,128)(2,1)} %bitcast.55), calls=%async_computation.1 | async-start | bytes 7340032 | tf_op jit(solution)/shard_map/all_to_all | solution.py:58
  168.9 2.3 copy-start
  237.2 7.8 %copy-start.4 = (f32[128,8]{0,1:T(8,128)S(1)}, f32[128,8]{0,1:T(8,128)}, u32[]{:S(2)}) copy-start(f32[128,8]{0,1:T(8,128)} %param.12) | copy-start | bytes 12292
  237.2 54.2 %all-to-all-start.2 = ((bf16[32,5,7168]{2,1,0:T(8,128)(2,1)}), bf16[32,5,7168]{2,1,0:T(8,128)(2,1)}, u32[]{:S(2)}, u32[]{:S(2)}) async-start(bf16[32,5,7168]{2,1,0:T(8,128)(2,1)} %reshape.89), calls=%async_computation.3 | async-start | bytes 7340032 | tf_op jit(solution)/shard_map/all_to_all | solution.py:85
Sparse Core Ops, SparseCore 0:
  11.2 74.9 reduce-scatter.1
Sparse Core Ops, SparseCore 1:
  10.9 58.8 all-gather.6
  71.3 95.2 all-gather.10
  168.1 55.2 all-gather.8
where the time goes:
time: 362 us; the launch traced here: 356 us
  waiting for transfers between devices  221 us (61%)
  local copies, waits for them, and re-layouts  57.9 us (16%)
  other arithmetic  26.2 us (7%)
  starting transfers between devices  19.6 us (5%)
  between operations  15.9 us (4%)
  matrix products  14.8 us (4%)
    reduce_scatter x1, waiting for transfers between devices, local(): lax.psum_scatter(own_partial.astype(jnp.float32).astype(jnp.bfloat16), 't...  75.4 us
    all_gather x1, waiting for transfers between devices, local(): lax.all_gather(w_up[0], 'fsdp', axis=0, tiled=True)  46.7 us
    all_to_all x1, waiting for transfers between devices, local(): lax.all_to_all(partial_value, ('expert', 'tensor'), split_axis=0, concat_...  46.3 us
    all_to_all x1, waiting for transfers between devices, local(): lax.all_to_all(wide_rows, ('expert', 'tensor'), split_axis=0, concat_axis...  44.9 us
    gather x1, local copies, waits for them, and re-layouts, local(): taken = expert_out[expert_range[None, :], slot_index]  37.8 us
    reduce_sum x1, other arithmetic, local(): mixture = jnp.sum(factor[:, :, None] * taken, axis=1)  15.5 us
    dot_general x1, matrix products, local(): jnp.dot(middle, lax.all_gather(w_down[0], 'fsdp', axis=1, tiled=True), pr...  9.2 us
    all_to_all x1, starting transfers between devices, local(): lax.all_to_all(partial_value, ('expert', 'tensor'), split_axis=0, concat_...  7.65 us
  transfers between devices with their start and end apart: 7, of which 5 were waited for; matrix products, arithmetic and copies ran while one was open for 8% of the time, Pallas kernels for 0%

commit v1 on v0

v1 whole, which is shorter than its diff:
```python
import jax
import jax.numpy as jnp
from jax import lax
from jax.sharding import Mesh, PartitionSpec as P

CAP = 5
FRONT = 40
RING = 4
SWAP = [(0, 1), (1, 0)]


def shift(value, steps):
    return lax.ppermute(value, "x", [(j, (j + steps) % RING) for j in range(RING)])


def pick(onehot, rows):
    return jnp.dot(onehot, rows, preferred_element_type=jnp.float32)


def local(attn_partial, residual, gain, expert_ids, gate_vals, w_gate, w_up, w_down):
    count, width = residual.shape
    half = width // 2
    quarter = width // 4
    f32, bf = jnp.float32, jnp.bfloat16
    x = lax.axis_index("x")
    core = lax.axis_index("core")
    zh = lax.axis_index("zh")
    attn = attn_partial[0].reshape(RING, count, width)
    wg, wu, wd = w_gate[0], w_up[0], w_down[0]
    wg2 = lax.ppermute(wg, "core", SWAP)
    wu2 = lax.ppermute(wu, "core", SWAP)
    wd2 = lax.ppermute(wd, "core", SWAP)

    with jax.named_scope("routing"):
        experts = jnp.arange(8, dtype=jnp.int32)
        matched = expert_ids[:, :, None] == experts[None, None, :]
        routed = jnp.any(matched, axis=1)
        weight = jnp.sum(jnp.where(matched, gate_vals[:, :, None], 0.0), axis=1)
        anyone = jnp.any(routed, axis=1)
        flags = jnp.concatenate([routed, anyone[:, None]], axis=1).astype(bf)
        token = jnp.arange(count, dtype=jnp.int32)
        tri = (token[:, None] >= token[None, :]).astype(bf)
        upto = pick(tri, flags).astype(jnp.int32)
        slots = upto[:, :8] - 1
        ahead = upto[:, 8]
        pos = jnp.where(anyone, ahead - 1, ahead[-1] + token - ahead)
        poses = [pos] + [shift(pos, -k) for k in (1, 2, 3)]
        places = [
            (p[None, :] == jnp.arange(count, dtype=jnp.int32)[:, None]).astype(bf) for p in poses
        ]
        placing = (
            (slots.T[:, None, :] == jnp.arange(CAP, dtype=jnp.int32)[None, :, None])
            & routed.T[:, None, :]
        ).reshape(8 * CAP, count)

    def head_sum(rows, source, keep):
        sent = [
            pick(places[k][rows], lax.dynamic_index_in_dim(source, (x + k) % RING, 0, False)).astype(bf)
            for k in (1, 2, 3)
        ]
        got = [shift(sent[k - 1], k) for k in (1, 2, 3)]
        own = pick(places[0][rows], lax.dynamic_index_in_dim(source, x, 0, False))
        total = own + got[0].astype(f32) + got[1].astype(f32) + got[2].astype(f32)
        return (pick(places[0][rows], keep) + total).astype(bf)

    front, back = slice(0, FRONT), slice(FRONT, count)
    with jax.named_scope("front_sum"):
        hidden_front = head_sum(front, attn, residual)
    with jax.named_scope("norm_dispatch"):
        values = hidden_front.astype(f32)
        meansq = jnp.mean(values * values, axis=-1, keepdims=True)
        normed = (values * lax.rsqrt(meansq + 1e-06) * gain).astype(bf)
        select = pick(placing.astype(bf), places[0][front].T).astype(bf)
        rows = pick(select, normed).astype(bf)
        rows = rows.reshape(4, 2, CAP, 2, 2, quarter)
        rows = jnp.where(core == 0, rows, rows[:, :, :, :, ::-1])
        rows = rows.transpose(3, 0, 1, 2, 4, 5).reshape(16, CAP, half)
    grid = ("zh", "y", "zl")
    with jax.named_scope("rows_out"):
        got = lax.all_to_all(rows, grid, split_axis=0, concat_axis=0, tiled=True)
        got = got.reshape(16 * CAP, half)
        inputs = jnp.concatenate([got] + [shift(got, k) for k in (1, 2, 3)], axis=0)
    with jax.named_scope("gate_up"):
        first, second = inputs[:, :quarter], inputs[:, quarter:]
        both = jnp.concatenate(
            [pick(first, wg) + pick(second, wg2), pick(first, wu) + pick(second, wu2)], axis=1
        )
        both = both.reshape(2, 8 * 16 * CAP // 4, -1)
        away = lax.ppermute(
            lax.dynamic_index_in_dim(both, 1 - zh, 0, False).astype(bf), "zh", SWAP
        )
        mine = lax.dynamic_index_in_dim(both, zh, 0, False) + away.astype(f32)
        ff = wg.shape[1]
        middle = (jax.nn.silu(mine[:, :ff]) * mine[:, ff:]).astype(bf)
    with jax.named_scope("down"):
        other = lax.ppermute(middle, "zh", SWAP)
        middle = jnp.where(
            zh == 0,
            jnp.concatenate([middle, other], axis=0),
            jnp.concatenate([other, middle], axis=0),
        )
        out = jnp.concatenate([pick(middle, wd), pick(middle, wd2)], axis=1).reshape(RING, 16 * CAP, half)
        total = out[0].astype(bf).astype(f32)
        for k in (1, 2, 3):
            total = total + shift(out[k].astype(bf), -k).astype(f32)
    with jax.named_scope("rows_back"):
        back_rows = lax.all_to_all(
            total.astype(bf).reshape(16, CAP, half), grid, split_axis=0, concat_axis=0, tiled=True
        )
        back_rows = back_rows.reshape(2, 8, CAP, 2, quarter)
        back_rows = jnp.where(core == 0, back_rows, back_rows[:, :, :, ::-1])
        back_rows = back_rows.transpose(1, 2, 0, 3, 4).reshape(8 * CAP, width)
    with jax.named_scope("mix"):
        factor = (
            placing.reshape(8, CAP, count).astype(f32) * weight.T[:, None, :]
        ).reshape(8 * CAP, count).T
        high = factor.astype(bf)
        low = (factor - high.astype(f32)).astype(bf)
        moe_out = (pick(high, back_rows) + pick(low, back_rows)).astype(bf)

    with jax.named_scope("back_sum"):
        late, late_residual, _ = lax.optimization_barrier((attn, residual, rows))
        hidden_back = head_sum(back, late, late_residual)
        hidden = pick(places[0].T, jnp.concatenate([hidden_front, hidden_back], axis=0)).astype(bf)
    return hidden, moe_out


def solution(mesh):
    grid = Mesh(mesh.devices.reshape(2, 2, 4, 2, 4), ("zh", "core", "y", "zl", "x"))
    group = ("zh", "core", "y", "zl")
    token = P(group + ("x",), None)
    placed = (
        P("x", group, None),
        token,
        P(),
        token,
        token,
        P(("y", "zl"), ("zh", "core"), "x"),
        P(("y", "zl"), ("zh", "core"), "x"),
        P(("y", "zl"), "x", ("zh", "core")),
    )
    return jax.shard_map(
        local, mesh=grid, in_specs=placed, out_specs=(token, token), check_vma=False
    )
```

time: 362 us -> 234 us (0.65)
  waiting for transfers between devices: 221 us -> 110 us
  local copies, waits for them, and re-layouts: 57.9 us -> 23.7 us
  blocking collectives: 0 us -> 23.5 us
  matrix products: 14.8 us -> 34.8 us
  between operations: 15.9 us -> 1.17 us
  other arithmetic: 26.2 us -> 14.2 us
    ppermute x0 -> x20, waiting for transfers between devices: none -> 110 us  [the longest x15 98.6 us: shift(): lax.ppermute(value, 'x', [(j, (j + steps) % RING) for j in range(RING)])]
    all_to_all x3 -> x1, waiting for transfers between devices: 97.1 us -> 0.01 us  [local(): lax.all_to_all(total.astype(bf).reshape(16, CAP, half), grid, split_axis=...]
    reduce_scatter x1 -> x0, waiting for transfers between devices: 75.4 us -> none  [local(): lax.psum_scatter(own_partial.astype(jnp.float32).astype(jnp.bfloat16), 't...]
    all_gather x3 -> x0, waiting for transfers between devices: 46.8 us -> none  [the longest x1 46.7 us: local(): lax.all_gather(w_up[0], 'fsdp', axis=0, tiled=True)]
    gather x1 -> x0, local copies, waits for them, and re-layouts: 37.8 us -> none  [local(): taken = expert_out[expert_range[None, :], slot_index]]
    all_to_all x0 -> x1, blocking collectives: none -> 23.5 us  [local(): got = lax.all_to_all(rows, grid, split_axis=0, concat_axis=0, tiled=True)]
    dot_general x4 -> x21, matrix products: 14.8 us -> 34.8 us  [pick(): return jnp.dot(onehot, rows, preferred_element_type=jnp.float32)]
    ppermute x0 -> x20, starting transfers between devices: none -> 19 us  [the longest x15 16.1 us: shift(): lax.ppermute(value, 'x', [(j, (j + steps) % RING) for j in range(RING)])]
  transfers between devices with their start and end apart: 7 -> 21, of which waited for: 5 -> 10; matrix products, arithmetic and copies ran while one was open for 8% -> 17% of each run, Pallas kernels for 0% -> 0%
where the time goes in v1:
time: 234 us; the launch traced here: 230 us
  waiting for transfers between devices  110 us (47%)
  matrix products  34.8 us (15%)
  local copies, waits for them, and re-layouts  23.7 us (10%)
  blocking collectives  23.5 us (10%)
  starting transfers between devices  22.8 us (10%)
  other arithmetic  14.2 us (6%)
    ppermute x15, waiting for transfers between devices, shift(): lax.ppermute(value, 'x', [(j, (j + steps) % RING) for j in range(RING)])  98.6 us
    dot_general x21, matrix products, pick(): return jnp.dot(onehot, rows, preferred_element_type=jnp.float32)  34.8 us
    all_to_all x1, blocking collectives, local(): got = lax.all_to_all(rows, grid, split_axis=0, concat_axis=0, tiled=True)  23.5 us
    ppermute x15, starting transfers between devices, shift(): lax.ppermute(value, 'x', [(j, (j + steps) % RING) for j in range(RING)])  16.1 us
    ppermute x1, waiting for transfers between devices, local(): lax.ppermute(lax.dynamic_index_in_dim(both, 1 - zh, 0, False).astype(bf),...  7.55 us
    rev x1, local copies, waits for them, and re-layouts, local(): rows = jnp.where(core == 0, rows, rows[:, :, :, :, ::-1])  6.96 us
    unnamed x41, local copies, waits for them, and re-layouts  5.52 us
  transfers between devices with their start and end apart: 21, of which 10 were waited for; matrix products, arithmetic and copies ran while one was open for 17% of the time, Pallas kernels for 0%

profile of v1, /device:TPU:0, one launch (start us, length us, event | category | flops | bytes accessed | tf_op | source)
XLA Modules:
  0.0 230.2 jit_solution(13604149945248517359)
XLA Ops:
  2.2 1.2 subtract_select_fusion
  3.4 1.6 collective-permute-start.4
  5.0 2.7 %collective-permute-start.2 = (s32[128]{0:T(128)}, s32[128]{0:T(128)S(1)}, u32[]{:S(2)}, u32[]{:S(2)}) collective-permute-start(s32[128]{0:T(128)} %subtract_select_fusion), channel_id=1, source_target_pairs={{0,2},{1,3},{2,0},{3,1},{4,6},{5,7},{6,4},{7,5},{8,10},{9,11},{10,... | collective-permute-start | bytes 1544 | tf_op jit(solution)/shard_map/routing/ppermute | solution.py:13
  7.7 1.4 collective-permute-start
  10.0 1.9 convolution_convert_fusion.5
  12.0 2.7 %convolution_convert_fusion.6 = bf16[40,7168]{1,0:T(8,128)(2,1)} fusion(bf16[4,128,7168]{2,1,0:T(8,128)(2,1)} %bitcast.73, s32[]{:T(128)S(6)} %select_n.86, pred[128,128]{1,0:T(8,128)(4,1)S(1)} %iota_compare_fusion.1), kind=kOutput, calls=%fused_computation.8 | convolution fusion | flops 73687040 | bytes 2413572 | tf_op jit(solution)/shard_map/front_sum/dot_general | solution.py:17
  14.7 2.6 %collective-permute-start.3 = (bf16[40,7168]{1,0:T(8,128)(2,1)}, bf16[40,7168]{1,0:T(8,128)(2,1)S(1)}, u32[]{:S(2)}, u32[]{:S(2)}) collective-permute-start(bf16[40,7168]{1,0:T(8,128)(2,1)} %convolution_convert_fusion.6), channel_id=1, source_target_pairs={{0,2},{1,3},{2,0},{3,1},{4,6},{5,7},{6,4},{7,5},{8,10},{9,11},{10,... | collective-permute-start | bytes 1720328 | tf_op jit(solution)/shard_map/front_sum/ppermute | solution.py:13
  18.6 2.7 %convolution_convert_fusion.7 = bf16[40,7168]{1,0:T(8,128)(2,1)} fusion(bf16[4,128,7168]{2,1,0:T(8,128)(2,1)} %bitcast.74, s32[]{:T(128)S(6)} %select_n.84, pred[128,128]{1,0:T(8,128)(4,1)S(1)} %iota_compare_fusion.2), kind=kOutput, calls=%fused_computation.9 | convolution fusion | flops 73687040 | bytes 2413572 | tf_op jit(solution)/shard_map/front_sum/dot_general | solution.py:17
  21.3 1.2 iota_compare_fusion.3
  22.5 1.9 fusion.12
  25.5 2.4 %collective-permute-done.5 = bf16[40,7168]{1,0:T(8,128)(2,1)S(1)} collective-permute-done((bf16[40,7168]{1,0:T(8,128)(2,1)S(1)}, bf16[40,7168]{1,0:T(8,128)(2,1)S(1)}, u32[]{:S(2)}, u32[]{:S(2)}) %collective-permute-start.5) | collective-permute-done | bytes 573472 | tf_op jit(solution)/shard_map/front_sum/ppermute | solution.py:13
  27.9 4.5 %collective-permute-done.3 = bf16[40,7168]{1,0:T(8,128)(2,1)S(1)} collective-permute-done((bf16[40,7168]{1,0:T(8,128)(2,1)}, bf16[40,7168]{1,0:T(8,128)(2,1)S(1)}, u32[]{:S(2)}, u32[]{:S(2)}) %collective-permute-start.3) | collective-permute-done | bytes 573472 | tf_op jit(solution)/shard_map/front_sum/ppermute | solution.py:13
  32.4 10.3 %collective-permute-done.1 = bf16[40,7168]{1,0:T(8,128)(2,1)} collective-permute-done((bf16[40,7168]{1,0:T(8,128)(2,1)}, bf16[40,7168]{1,0:T(8,128)(2,1)}, u32[]{:S(2)}, u32[]{:S(2)}) %collective-permute-start.1) | collective-permute-done | bytes 573472 | tf_op jit(solution)/shard_map/front_sum/ppermute | solution.py:13
  42.7 1.6 fusion.22
  44.3 1.2 convolution_convert_fusion.4
  46.0 1.2 copy.29
  47.2 7.0 %rev.6 = bf16[4,2,5,2,2,1792]{5,4,1,0,3,2:T(2,128)(2,1)S(1)} reverse(bf16[4,2,5,2,2,1792]{5,4,1,0,3,2:T(2,128)(2,1)} %copy.29), dimensions={4} | reverse | bytes 1146880 | tf_op jit(solution)/shard_map/norm_dispatch/rev | solution.py:76
  54.1 1.4 fusion.31
  55.5 1.4 reshape.80
  57.3 23.5 %all_to_all.10 = bf16[16,5,3584]{2,1,0:T(8,128)(2,1)S(1)} all-to-all(bf16[16,5,3584]{2,1,0:T(8,128)(2,1)S(1)} %copy.30), channel_id=1, replica_groups=mesh['zh'=2,'core'=2,'y'=4,'zl'=2,'x'=4] {'zh','y','zl'}, dimensions={0} | all-to-all | bytes 1146880 | tf_op jit(solution)/shard_map/rows_out/all_to_all | solution.py:80
  82.3 2.4 %collective-permute-start.10 = (bf16[80,3584]{1,0:T(8,128)(2,1)}, bf16[80,3584]{1,0:T(8,128)(2,1)S(1)}, u32[]{:S(2)}, u32[]{:S(2)}) collective-permute-start(bf16[80,3584]{1,0:T(8,128)(2,1)} %reshape.81), channel_id=1, source_target_pairs={{0,2},{1,3},{2,0},{3,1},{4,6},{5,7},{6,4},{7,5},{8,10},{9,11},{10,... | collective-permute-start | bytes 1720328 | tf_op jit(solution)/shard_map/rows_out/ppermute | solution.py:13
  85.8 23.4 %collective-permute-done.9 = bf16[80,3584]{1,0:T(8,128)(2,1)S(1)} collective-permute-done((bf16[80,3584]{1,0:T(8,128)(2,1)}, bf16[80,3584]{1,0:T(8,128)(2,1)S(1)}, u32[]{:S(2)}, u32[]{:S(2)}) %collective-permute-start.9) | collective-permute-done | bytes 573472 | tf_op jit(solution)/shard_map/rows_out/ppermute | solution.py:13
  109.3 9.8 %collective-permute-done.11 = bf16[80,3584]{1,0:T(8,128)(2,1)S(1)} collective-permute-done((bf16[80,3584]{1,0:T(8,128)(2,1)}, bf16[80,3584]{1,0:T(8,128)(2,1)S(1)}, u32[]{:S(2)}, u32[]{:S(2)}) %collective-permute-start.11) | collective-permute-done | bytes 573472 | tf_op jit(solution)/shard_map/rows_out/ppermute | solution.py:13
  119.2 2.4 %fusion.25 = f32[320,512]{1,0:T(8,128)S(1)} fusion(bf16[1792,512]{1,0:T(8,128)(2,1)} %collective-permute-done.13, bf16[320,3584]{1,0:T(8,128)(2,1)S(1)} %constant_dynamic-update-slice_fusion), kind=kOutput, calls=%fused_computation.47 | convolution fusion | flops 587202560 | bytes 3637248 | tf_op jit(solution)/shard_map/gate_up/dot_general | solution.py:17
  122.3 2.4 %fusion.27 = f32[320,512]{1,0:T(8,128)S(1)} fusion(bf16[1792,512]{1,0:T(8,128)(2,1)} %collective-permute-done.12, bf16[320,3584]{1,0:T(8,128)(2,1)S(1)} %constant_dynamic-update-slice_fusion), kind=kOutput, calls=%fused_computation.49 | convolution fusion | flops 587202560 | bytes 3637248 | tf_op jit(solution)/shard_map/gate_up/dot_general | solution.py:17
  126.8 1.2 collective-permute-start.14
  128.0 7.6 %collective-permute-done.14 = bf16[160,1024]{1,0:T(8,128)(2,1)S(1)} collective-permute-done((bf16[160,1024]{1,0:T(8,128)(2,1)S(1)}, bf16[160,1024]{1,0:T(8,128)(2,1)S(1)}, u32[]{:S(2)}, u32[]{:S(2)}) %collective-permute-start.14) | collective-permute-done | bytes 327712 | tf_op jit(solution)/shard_map/gate_up/ppermute | solution.py:89
  135.6 1.2 bitcast_add_fusion
  138.0 2.0 fusion.44
  139.9 3.9 %collective-permute-done.15 = bf16[160,512]{1,0:T(8,128)(2,1)S(1)} collective-permute-done((bf16[160,512]{1,0:T(8,128)(2,1)S(1)}, bf16[160,512]{1,0:T(8,128)(2,1)S(1)}, u32[]{:S(2)}, u32[]{:S(2)}) %collective-permute-start.15) | collective-permute-done | bytes 163872 | tf_op jit(solution)/shard_map/down/ppermute | solution.py:96
  144.6 2.4 %fusion.38 = bf16[320,1792]{1,0:T(8,128)(2,1)S(1)} fusion(bf16[512,1792]{1,0:T(8,128)(2,1)} %collective-permute-done.16, bf16[160,512]{1,0:T(8,128)(2,1)S(1)} %collective-permute-done.15, bf16[160,512]{1,0:T(8,128)(2,1)S(1)} %fusion.37, pred[]{:T(512)S(6)} %eq.110), kind=kOutput, calls=%fused_computation.68 | convolution fusion | flops 588677120 | bytes 3309569 | tf_op jit(solution)/shard_map/down/dot_general | solution.py:17
  147.4 1.6 slice-done.1
  149.0 1.5 convolution_convert_fusion.1
  150.5 1.2 collective-permute-start.18
  151.7 1.2 collective-permute-start.17
  152.9 1.5 convolution_convert_fusion.2
  154.4 1.8 collective-permute-start.8
  156.1 1.2 collective-permute-start.7
  157.3 1.6 convolution_convert_fusion.3
  158.9 27.2 %collective-permute-done.19 = bf16[80,3584]{1,0:T(8,128)(2,1)S(1)} collective-permute-done((bf16[80,3584]{1,0:T(8,128)(2,1)S(1)}, bf16[80,3584]{1,0:T(8,128)(2,1)S(1)}, u32[]{:S(2)}, u32[]{:S(2)}) %collective-permute-start.19) | collective-permute-done | bytes 573472 | tf_op jit(solution)/shard_map/down/ppermute | solution.py:13
  186.2 2.0 fusion.7
  189.6 3.9 %all-to-all-start.1 = ((bf16[16,5,3584]{2,1,0:T(8,128)(2,1)}), bf16[16,5,3584]{2,1,0:T(8,128)(2,1)S(1)}, u32[]{:S(2)}, u32[]{:S(2)}) async-start(bf16[16,5,3584]{2,1,0:T(8,128)(2,1)} %reshape.83), calls=%async_computation.1 | async-start | bytes 1835008 | tf_op jit(solution)/shard_map/rows_back/all_to_all | solution.py:107
  193.4 10.9 %collective-permute-done.8 = bf16[88,7168]{1,0:T(8,128)(2,1)S(1)} collective-permute-done((bf16[88,7168]{1,0:T(8,128)(2,1)}, bf16[88,7168]{1,0:T(8,128)(2,1)S(1)}, u32[]{:S(2)}, u32[]{:S(2)}) %collective-permute-start.8) | collective-permute-done | bytes 1261600 | tf_op jit(solution)/shard_map/back_sum/ppermute | solution.py:13
  205.4 10.0 %collective-permute-done.6 = bf16[88,7168]{1,0:T(8,128)(2,1)} collective-permute-done((bf16[88,7168]{1,0:T(8,128)(2,1)}, bf16[88,7168]{1,0:T(8,128)(2,1)}, u32[]{:S(2)}, u32[]{:S(2)}) %collective-permute-start.6) | collective-permute-done | bytes 1261600 | tf_op jit(solution)/shard_map/back_sum/ppermute | solution.py:13
  215.4 4.2 %add_convert_fusion = bf16[88,7168]{1,0:T(8,128)(2,1)S(1)} fusion(f32[88,7168]{1,0:T(8,128)} %fusion.44, bf16[88,7168]{1,0:T(8,128)(2,1)} %copy-done.3, bf16[88,7168]{1,0:T(8,128)(2,1)} %collective-permute-done.7, f32[88,7168]{1,0:T(8,128)} %fusion.7, bf16[88,7168]{1,0:T(8,128)(2,1)} %collective-permute-done.6), kind=kLoop, calls=%fused_computation.11 | loop fusion | flops 5046272 | bytes 10092544 | tf_op jit(solution)/shard_map/back_sum/convert_element_type | solution.py:64
  219.7 2.5 %convolution_convert_fusion = bf16[128,7168]{1,0:T(8,128)(2,1)} fusion(bf16[88,7168]{1,0:T(8,128)(2,1)S(1)} %add_convert_fusion, bf16[40,7168]{1,0:T(8,128)(2,1)S(1)} %get-tuple-element.9, s32[128]{0:T(128)} %subtract_select_fusion), kind=kOutput, calls=%fused_computation.2 | convolution fusion | flops 239484928 | bytes 3670528 | tf_op jit(solution)/shard_map/back_sum/dot_general | solution.py:17
  223.0 3.1 %rev.7 = bf16[2,8,5,2,1792]{4,3,1,0,2:T(2,128)(2,1)S(1)} reverse(bf16[2,8,5,2,1792]{4,3,1,0,2:T(2,128)(2,1)S(1)} %copy.33), dimensions={3} | reverse | bytes 1146880 | tf_op jit(solution)/shard_map/rows_back/rev | solution.py:111
  228.3 1.9 fusion
  (101 shorter events, 18.8 us)
Async XLA Ops:
  0.6 23.8 %copy-start = (bf16[128,7168]{1,0:T(8,128)(2,1)S(1)}, bf16[128,7168]{1,0:T(8,128)(2,1)}, u32[]{:S(2)}) copy-start(bf16[128,7168]{1,0:T(8,128)(2,1)} %param.9) | copy-start | bytes 5505028
  3.4 6.6 %collective-permute-start.4 = (s32[128]{0:T(128)}, s32[128]{0:T(128)S(1)}, u32[]{:S(2)}, u32[]{:S(2)}) collective-permute-start(s32[128]{0:T(128)} %subtract_select_fusion), channel_id=1, source_target_pairs={{0,1},{1,2},{2,3},{3,0},{4,5},{5,6},{6,7},{7,4},{8,9},{9,10},{10,1... | collective-permute-start | bytes 1544 | tf_op jit(solution)/shard_map/routing/ppermute | solution.py:13
  5.0 7.0 %collective-permute-start.2 = (s32[128]{0:T(128)}, s32[128]{0:T(128)S(1)}, u32[]{:S(2)}, u32[]{:S(2)}) collective-permute-start(s32[128]{0:T(128)} %subtract_select_fusion), channel_id=1, source_target_pairs={{0,2},{1,3},{2,0},{3,1},{4,6},{5,7},{6,4},{7,5},{8,10},{9,11},{10,... | collective-permute-start | bytes 1544 | tf_op jit(solution)/shard_map/routing/ppermute | solution.py:13
  7.7 9.6 %collective-permute-start = (s32[128]{0:T(128)}, s32[128]{0:T(128)}, u32[]{:S(2)}, u32[]{:S(2)}) collective-permute-start(s32[128]{0:T(128)} %subtract_select_fusion), channel_id=1, source_target_pairs={{0,3},{1,0},{2,1},{3,2},{4,7},{5,4},{6,5},{7,6},{8,11},{9,8},{10,9... | collective-permute-start | bytes 1544 | tf_op jit(solution)/shard_map/routing/ppermute | solution.py:13
  10.0 2.0 copy-start.10
  11.9 16.0 %collective-permute-start.5 = (bf16[40,7168]{1,0:T(8,128)(2,1)S(1)}, bf16[40,7168]{1,0:T(8,128)(2,1)S(1)}, u32[]{:S(2)}, u32[]{:S(2)}) collective-permute-start(bf16[40,7168]{1,0:T(8,128)(2,1)S(1)} %convolution_convert_fusion.5), channel_id=1, source_target_pairs={{0,3},{1,0},{2,1},{3,2},{4,7},{5,4},{6,5},{7,6},{8,11},{9,8},{10,9... | collective-permute-start | bytes 1720328 | tf_op jit(solution)/shard_map/front_sum/ppermute | solution.py:13
  12.0 5.3 %copy-start.8 = (pred[128,128]{1,0:T(8,128)(4,1)}, pred[128,128]{1,0:T(8,128)(4,1)S(1)}, u32[]{:S(2)}) copy-start(pred[128,128]{1,0:T(8,128)(4,1)S(1)} %iota_compare_fusion.1) | copy-start | bytes 49156
  14.7 17.7 %collective-permute-start.3 = (bf16[40,7168]{1,0:T(8,128)(2,1)}, bf16[40,7168]{1,0:T(8,128)(2,1)S(1)}, u32[]{:S(2)}, u32[]{:S(2)}) collective-permute-start(bf16[40,7168]{1,0:T(8,128)(2,1)} %convolution_convert_fusion.6), channel_id=1, source_target_pairs={{0,2},{1,3},{2,0},{3,1},{4,6},{5,7},{6,4},{7,5},{8,10},{9,11},{10,... | collective-permute-start | bytes 1720328 | tf_op jit(solution)/shard_map/front_sum/ppermute | solution.py:13
  18.0 0.6 copy-start.6
  21.3 21.4 %collective-permute-start.1 = (bf16[40,7168]{1,0:T(8,128)(2,1)}, bf16[40,7168]{1,0:T(8,128)(2,1)}, u32[]{:S(2)}, u32[]{:S(2)}) collective-permute-start(bf16[40,7168]{1,0:T(8,128)(2,1)} %convolution_convert_fusion.7), channel_id=1, source_target_pairs={{0,1},{1,2},{2,3},{3,0},{4,5},{5,6},{6,7},{7,4},{8,9},{9,10},{10,1... | collective-permute-start | bytes 1720328 | tf_op jit(solution)/shard_map/front_sum/ppermute | solution.py:13
  81.8 27.4 %collective-permute-start.9 = (bf16[80,3584]{1,0:T(8,128)(2,1)}, bf16[80,3584]{1,0:T(8,128)(2,1)S(1)}, u32[]{:S(2)}, u32[]{:S(2)}) collective-permute-start(bf16[80,3584]{1,0:T(8,128)(2,1)} %reshape.81), channel_id=1, source_target_pairs={{0,1},{1,2},{2,3},{3,0},{4,5},{5,6},{6,7},{7,4},{8,9},{9,10},{10,1... | collective-permute-start | bytes 1720328 | tf_op jit(solution)/shard_map/rows_out/ppermute | solution.py:13
  81.8 62.8 %collective-permute-start.16 = (bf16[512,1792]{1,0:T(8,128)(2,1)}, bf16[512,1792]{1,0:T(8,128)(2,1)}, u32[]{:S(2)}, u32[]{:S(2)}) collective-permute-start(bf16[512,1792]{1,0:T(8,128)(2,1)} %bitcast.89), channel_id=1, source_target_pairs={{0,32},{32,0},{1,33},{33,1},{2,34},{34,2},{3,35},{35,3},{4,36},{36... | collective-permute-start | bytes 5505032 | tf_op jit(solution)/shard_map/ppermute | solution.py:32
  81.8 37.3 %collective-permute-start.13 = (bf16[1792,512]{1,0:T(8,128)(2,1)}, bf16[1792,512]{1,0:T(8,128)(2,1)}, u32[]{:S(2)}, u32[]{:S(2)}) collective-permute-start(bf16[1792,512]{1,0:T(8,128)(2,1)} %bitcast.87), channel_id=1, source_target_pairs={{0,32},{32,0},{1,33},{33,1},{2,34},{34,2},{3,35},{35,3},{4,36},{36... | collective-permute-start | bytes 5505032 | tf_op jit(solution)/shard_map/ppermute | solution.py:31
  82.3 40.0 %collective-permute-start.12 = (bf16[1792,512]{1,0:T(8,128)(2,1)}, bf16[1792,512]{1,0:T(8,128)(2,1)}, u32[]{:S(2)}, u32[]{:S(2)}) collective-permute-start(bf16[1792,512]{1,0:T(8,128)(2,1)} %bitcast.88), channel_id=1, source_target_pairs={{0,32},{32,0},{1,33},{33,1},{2,34},{34,2},{3,35},{35,3},{4,36},{36... | collective-permute-start | bytes 5505032 | tf_op jit(solution)/shard_map/ppermute | solution.py:30
  82.3 26.9 %collective-permute-start.10 = (bf16[80,3584]{1,0:T(8,128)(2,1)}, bf16[80,3584]{1,0:T(8,128)(2,1)S(1)}, u32[]{:S(2)}, u32[]{:S(2)}) collective-permute-start(bf16[80,3584]{1,0:T(8,128)(2,1)} %reshape.81), channel_id=1, source_target_pairs={{0,2},{1,3},{2,0},{3,1},{4,6},{5,7},{6,4},{7,5},{8,10},{9,11},{10,... | collective-permute-start | bytes 1720328 | tf_op jit(solution)/shard_map/rows_out/ppermute | solution.py:13
  109.2 9.9 %collective-permute-start.11 = (bf16[80,3584]{1,0:T(8,128)(2,1)}, bf16[80,3584]{1,0:T(8,128)(2,1)S(1)}, u32[]{:S(2)}, u32[]{:S(2)}) collective-permute-start(bf16[80,3584]{1,0:T(8,128)(2,1)} %reshape.81), channel_id=1, source_target_pairs={{0,3},{1,0},{2,1},{3,2},{4,7},{5,4},{6,5},{7,6},{8,11},{9,8},{10,9... | collective-permute-start | bytes 1720328 | tf_op jit(solution)/shard_map/rows_out/ppermute | solution.py:13
  119.1 2.4 %copy-start.14 = (bf16[1,1792,512]{2,1,0:T(8,128)(2,1)S(1)}, bf16[1,1792,512]{2,1,0:T(8,128)(2,1)}, u32[]{:S(2)}) copy-start(bf16[1,1792,512]{2,1,0:T(8,128)(2,1)} %param.14) | copy-start | bytes 5505028
  122.3 2.4 %copy-start.15 = (bf16[1,1792,512]{2,1,0:T(8,128)(2,1)S(1)}, bf16[1,1792,512]{2,1,0:T(8,128)(2,1)}, u32[]{:S(2)}) copy-start(bf16[1,1792,512]{2,1,0:T(8,128)(2,1)} %param.13) | copy-start | bytes 5505028
  125.5 2.5 %copy-start.12 = (s32[128,8]{0,1:T(8,128)S(1)}, s32[128,8]{0,1:T(8,128)}, u32[]{:S(2)}) copy-start(s32[128,8]{0,1:T(8,128)} %param.11) | copy-start | bytes 12292
  125.5 2.5 %copy-start.13 = (f32[128,8]{0,1:T(8,128)S(1)}, f32[128,8]{0,1:T(8,128)}, u32[]{:S(2)}) copy-start(f32[128,8]{0,1:T(8,128)} %param.12) | copy-start | bytes 12292
  125.6 1.1 copy-start.2
  125.7 12.3 %copy-start.4 = (pred[128,128]{1,0:T(8,128)(4,1)S(1)}, pred[128,128]{1,0:T(8,128)(4,1)}, u32[]{:S(2)}) copy-start(pred[128,128]{1,0:T(8,128)(4,1)} %iota_compare_fusion.3) | copy-start | bytes 49156
  126.8 8.8 %collective-permute-start.14 = (bf16[160,1024]{1,0:T(8,128)(2,1)S(1)}, bf16[160,1024]{1,0:T(8,128)(2,1)S(1)}, u32[]{:S(2)}, u32[]{:S(2)}) collective-permute-start(bf16[160,1024]{1,0:T(8,128)(2,1)S(1)} %fusion.36), channel_id=1, source_target_pairs={{0,64},{64,0},{1,65},{65,1},{2,66},{66,2},{3,67},{67,3},{4,68},{68... | collective-permute-start | bytes 983048 | tf_op jit(solution)/shard_map/gate_up/ppermute | solution.py:89
  136.9 6.9 %copy-start.16 = (bf16[1,512,1792]{2,1,0:T(8,128)(2,1)S(1)}, bf16[1,512,1792]{2,1,0:T(8,128)(2,1)}, u32[]{:S(2)}) copy-start(bf16[1,512,1792]{2,1,0:T(8,128)(2,1)} %param.15) | copy-start | bytes 5505028
  136.9 6.9 %collective-permute-start.15 = (bf16[160,512]{1,0:T(8,128)(2,1)S(1)}, bf16[160,512]{1,0:T(8,128)(2,1)S(1)}, u32[]{:S(2)}, u32[]{:S(2)}) collective-permute-start(bf16[160,512]{1,0:T(8,128)(2,1)S(1)} %fusion.37), channel_id=1, source_target_pairs={{0,64},{64,0},{1,65},{65,1},{2,66},{66,2},{3,67},{67,3},{4,68},{68... | collective-permute-start | bytes 491528 | tf_op jit(solution)/shard_map/down/ppermute | solution.py:96
  144.6 2.8 %slice-start = ((s8[7340032]{0:T(1024)(128)(4,1)}), s8[4194304]{0:T(1024)(128)(4,1)S(1)}, s32[]{:S(2)}) async-start(s8[7340032]{0:T(1024)(128)(4,1)} %bitcast.76), calls=%async_computation.2 | async-start | bytes 8388608
  147.0 2.0 slice-start.1
  147.2 1.8 copy-start.11
  147.3 5.5 %copy-start.9 = (pred[128,128]{1,0:T(8,128)(4,1)S(1)}, pred[128,128]{1,0:T(8,128)(4,1)}, u32[]{:S(2)}) copy-start(pred[128,128]{1,0:T(8,128)(4,1)} %copy-done.8) | copy-start | bytes 49156
  147.3 38.8 %collective-permute-start.19 = (bf16[80,3584]{1,0:T(8,128)(2,1)S(1)}, bf16[80,3584]{1,0:T(8,128)(2,1)S(1)}, u32[]{:S(2)}, u32[]{:S(2)}) collective-permute-start(bf16[80,3584]{1,0:T(8,128)(2,1)S(1)} %get-tuple-element.11), channel_id=1, source_target_pairs={{0,1},{1,2},{2,3},{3,0},{4,5},{5,6},{6,7},{7,4},{8,9},{9,10},{10,1... | collective-permute-start | bytes 1720328 | tf_op jit(solution)/shard_map/down/ppermute | solution.py:13
  150.5 6.8 %copy-start.7 = (pred[128,128]{1,0:T(8,128)(4,1)S(1)}, pred[128,128]{1,0:T(8,128)(4,1)}, u32[]{:S(2)}) copy-start(pred[128,128]{1,0:T(8,128)(4,1)} %copy-done.6) | copy-start | bytes 49156
  150.5 37.6 %collective-permute-start.18 = (bf16[80,3584]{1,0:T(8,128)(2,1)S(1)}, bf16[80,3584]{1,0:T(8,128)(2,1)S(1)}, u32[]{:S(2)}, u32[]{:S(2)}) collective-permute-start(bf16[80,3584]{1,0:T(8,128)(2,1)S(1)} %get-tuple-element.12), channel_id=1, source_target_pairs={{0,2},{1,3},{2,0},{3,1},{4,6},{5,7},{6,4},{7,5},{8,10},{9,11},{10,... | collective-permute-start | bytes 1720328 | tf_op jit(solution)/shard_map/down/ppermute | solution.py:13
  151.7 36.5 %collective-permute-start.17 = (bf16[80,3584]{1,0:T(8,128)(2,1)S(1)}, bf16[80,3584]{1,0:T(8,128)(2,1)S(1)}, u32[]{:S(2)}, u32[]{:S(2)}) collective-permute-start(bf16[80,3584]{1,0:T(8,128)(2,1)S(1)} %get-tuple-element.10), channel_id=1, source_target_pairs={{0,3},{1,0},{2,1},{3,2},{4,7},{5,4},{6,5},{7,6},{8,11},{9,8},{10,9... | collective-permute-start | bytes 1720328 | tf_op jit(solution)/shard_map/down/ppermute | solution.py:13
  154.4 50.0 %collective-permute-start.8 = (bf16[88,7168]{1,0:T(8,128)(2,1)}, bf16[88,7168]{1,0:T(8,128)(2,1)S(1)}, u32[]{:S(2)}, u32[]{:S(2)}) collective-permute-start(bf16[88,7168]{1,0:T(8,128)(2,1)} %convolution_convert_fusion.1), channel_id=1, source_target_pairs={{0,3},{1,0},{2,1},{3,2},{4,7},{5,4},{6,5},{7,6},{8,11},{9,8},{10,9... | collective-permute-start | bytes 3784712 | tf_op jit(solution)/shard_map/back_sum/ppermute | solution.py:13
  156.1 48.2 %collective-permute-start.7 = (bf16[88,7168]{1,0:T(8,128)(2,1)}, bf16[88,7168]{1,0:T(8,128)(2,1)}, u32[]{:S(2)}, u32[]{:S(2)}) collective-permute-start(bf16[88,7168]{1,0:T(8,128)(2,1)} %convolution_convert_fusion.2), channel_id=1, source_target_pairs={{0,2},{1,3},{2,0},{3,1},{4,6},{5,7},{6,4},{7,5},{8,10},{9,11},{10,... | collective-permute-start | bytes 3784712 | tf_op jit(solution)/shard_map/back_sum/ppermute | solution.py:13
  186.1 29.3 %collective-permute-start.6 = (bf16[88,7168]{1,0:T(8,128)(2,1)}, bf16[88,7168]{1,0:T(8,128)(2,1)}, u32[]{:S(2)}, u32[]{:S(2)}) collective-permute-start(bf16[88,7168]{1,0:T(8,128)(2,1)} %convolution_convert_fusion.3), channel_id=1, source_target_pairs={{0,1},{1,2},{2,3},{3,0},{4,5},{5,6},{6,7},{7,4},{8,9},{9,10},{10,1... | collective-permute-start | bytes 3784712 | tf_op jit(solution)/shard_map/back_sum/ppermute | solution.py:13
  189.6 32.6 %all-to-all-start.1 = ((bf16[16,5,3584]{2,1,0:T(8,128)(2,1)}), bf16[16,5,3584]{2,1,0:T(8,128)(2,1)S(1)}, u32[]{:S(2)}, u32[]{:S(2)}) async-start(bf16[16,5,3584]{2,1,0:T(8,128)(2,1)} %reshape.83), calls=%async_computation.1 | async-start | bytes 1835008 | tf_op jit(solution)/shard_map/rows_back/all_to_all | solution.py:107
  204.4 1.0 copy-start.3
  226.1 1.5 copy-start.5
  227.6 2.6 %copy-start.1 = (bf16[128,7168]{1,0:T(8,128)(2,1)S(1)}, bf16[128,7168]{1,0:T(8,128)(2,1)}, u32[]{:S(2)}) copy-start(bf16[128,7168]{1,0:T(8,128)(2,1)} %param.9) | copy-start | bytes 5505028

commit v2 on v1

v2 whole, which is shorter than its diff:
```python
import jax
import jax.numpy as jnp
from jax import lax
from jax.experimental import pallas as pl
from jax.experimental.pallas import tpu as pltpu
from jax.sharding import Mesh, PartitionSpec as P

CAP = 5
EXPERTS = 8
FRONT = EXPERTS * CAP
RING = 4
SWAP = [(0, 1), (1, 0)]
TILE = 896
SEAT = 8
PIECES = (2, 3, 3)
F32, BF = jnp.float32, jnp.bfloat16
VMEM_LIMIT = 14 * 1024 * 1024
VMEM_ALL = 57 * 1024 * 1024


def shift(value, steps):
    return lax.ppermute(value, "x", [(j, (j + steps) % RING) for j in range(RING)])


def ring_sum(far, up, down, beside=None):
    far_first, far_last = shift(far[0], 1), shift(far[1], -1)
    up_last, down_first = shift(up[1], 1), shift(down[0], -1)
    if beside is not None:
        far_first, far_last, beside = lax.optimization_barrier((far_first, far_last, beside))
    up_first = shift((up[0].astype(F32) + far_first.astype(F32)).astype(BF), 1)
    down_last = shift((down[1].astype(F32) + far_last.astype(F32)).astype(BF), -1)
    return (up_first, up_last), (down_first, down_last), beside


def ring_gather(first, last):
    first_up, last_down = shift(first, 1), shift(last, -1)
    last_up, first_down = shift(last, 1), shift(first, -1)
    first_far, last_far = shift(first_up, 1), shift(last_down, -1)
    return [(first, last), (first_up, last_up), (first_far, last_far), (first_down, last_down)]


def dot(a, b):
    return jnp.dot(a, b, preferred_element_type=F32)


def params(limit=VMEM_LIMIT):
    return pltpu.CompilerParams(vmem_limit_bytes=limit)


def cost(flops, size):
    return pl.CostEstimate(flops=int(flops), bytes_accessed=int(size), transcendentals=0)


def onehot(first, rows, pos):
    index = lax.broadcasted_iota(jnp.int32, (rows, pos.shape[1]), 0) + first
    return (index == pos).astype(BF)


def fetch(source, target, sem):
    copy = pltpu.make_async_copy(source, target, sem)
    copy.start()
    return copy


def select_rows(where, attn, poses, rows, distances):
    count = poses.shape[1]
    width = attn.shape[1]
    number = len(distances)
    half = width // 2

    def kernel(where_ref, attn_ref, poses, *refs):
        held, sems = refs[-2:]
        copies = []
        for n, k in enumerate(distances):
            block = pl.multiple_of(lax.rem(where_ref[0] + k, RING) * count, count)
            for c in range(2):
                at = pl.ds(c * half, half)
                copies.append(
                    fetch(attn_ref.at[pl.ds(block, count), at], held.at[n, :, at], sems.at[n, c])
                )
        for n, k in enumerate(distances):
            pick = onehot(0, rows, poses[k : k + 1, :])
            for c in range(2):
                copies[2 * n + c].wait()
                at = slice(c * half, (c + 1) * half)
                refs[2 * n + c][...] = dot(pick, held[n, :, at]).astype(BF)

    vmem = pl.BlockSpec(memory_space=pltpu.VMEM)
    return pl.pallas_call(
        kernel,
        in_specs=[pl.BlockSpec(memory_space=pltpu.SMEM), pl.BlockSpec(memory_space=pl.ANY), vmem],
        out_specs=[vmem] * (2 * number),
        out_shape=[jax.ShapeDtypeStruct((rows, half), BF)] * (2 * number),
        scratch_shapes=[
            pltpu.VMEM((number, count, width), BF),
            pltpu.SemaphoreType.DMA((number, 2)),
        ],
        compiler_params=params(VMEM_ALL),
        cost_estimate=cost(2 * number * rows * count * width, 4 * number * count * width),
        name="select_rows",
    )(where, attn, poses)


def own_rows(where, attn, residual, pos, rows):
    count = pos.shape[1]
    width = attn.shape[1]
    quarter = width // 4

    def kernel(where_ref, attn_ref, residual_ref, pos, out, held, sems):
        block = pl.multiple_of(where_ref[0] * count, count)
        copies = []
        for c in range(4):
            at = pl.ds(c * quarter, quarter)
            copies.append(fetch(attn_ref.at[pl.ds(block, count), at], held.at[0, :, at], sems.at[0, c]))
            copies.append(fetch(residual_ref.at[:, at], held.at[1, :, at], sems.at[1, c]))
        pick = onehot(0, rows, pos[:1, :])
        for c in range(4):
            at = slice(c * quarter, (c + 1) * quarter)
            copies[2 * c].wait()
            copies[2 * c + 1].wait()
            out[:, at] = dot(pick, held[0, :, at]) + dot(pick, held[1, :, at])

    vmem = pl.BlockSpec(memory_space=pltpu.VMEM)
    hbm = pl.BlockSpec(memory_space=pl.ANY)
    return pl.pallas_call(
        kernel,
        in_specs=[pl.BlockSpec(memory_space=pltpu.SMEM), hbm, hbm, vmem],
        out_specs=vmem,
        out_shape=jax.ShapeDtypeStruct((rows, width), F32),
        scratch_shapes=[pltpu.VMEM((2, count, width), BF), pltpu.SemaphoreType.DMA((2, 4))],
        compiler_params=params(VMEM_ALL),
        cost_estimate=cost(4 * rows * count * width, 4 * count * width + 4 * rows * width),
        name="own_rows",
    )(where, attn, residual, pos)


def back_rows(where, attn, poses, first, left, width):
    count = poses.shape[1]
    rows = count - first

    def kernel(where_ref, attn_ref, poses, out, held, sems):
        blocks, copies = [], []
        for k in range(RING):
            blocks.append(lax.rem(where_ref[0] + k, RING))
            at = pl.multiple_of(blocks[k] * count, count)
            copies.append(
                fetch(attn_ref.at[pl.ds(at, count), pl.ds(left, width)], held.at[k], sems.at[k])
            )
        for k in range(RING):
            copies[k].wait()
            out[blocks[k]] = dot(onehot(first, rows, poses[k : k + 1, :]), held[k]).astype(BF)

    vmem = pl.BlockSpec(memory_space=pltpu.VMEM)
    return pl.pallas_call(
        kernel,
        in_specs=[pl.BlockSpec(memory_space=pltpu.SMEM), pl.BlockSpec(memory_space=pl.ANY), vmem],
        out_specs=vmem,
        out_shape=jax.ShapeDtypeStruct((RING, rows, width), BF),
        scratch_shapes=[pltpu.VMEM((RING, count, width), BF), pltpu.SemaphoreType.DMA((RING,))],
        compiler_params=params(VMEM_ALL),
        cost_estimate=cost(8 * rows * count * width, 8 * count * width + 8 * rows * width),
        name="back_rows",
    )(where, attn, poses)


def finish_hidden(where, front, residual, summed, pos, left, earlier=None):
    count, width = residual.shape
    first = front.shape[0]
    rest, wide = summed.shape
    skip = left // TILE

    def kernel(front, residual, summed, pos, *refs):
        back = onehot(first, rest, pos[:1, :])
        tail = (dot(back, residual[...]) + summed[...].astype(F32)).astype(BF)
        total = None
        for place, rows in ((onehot(0, first, pos[:1, :]), front[...]), (back, tail)):
            got = lax.dot_general(place, rows, (((0,), (0,)), ((), ())), preferred_element_type=F32)
            total = got if total is None else total + got
        refs[-1][...] = total.astype(BF)

    in_specs = [
        pl.BlockSpec((first, TILE), lambda i: (0, i + skip)),
        pl.BlockSpec((count, TILE), lambda i: (0, i + skip)),
        pl.BlockSpec((rest, TILE), lambda i: (0, i)),
        pl.BlockSpec((RING, count), lambda i: (0, 0)),
    ]
    operands = [front, residual, summed, pos]
    aliases = {}
    if earlier is not None:
        in_specs.append(pl.BlockSpec(memory_space=pl.ANY))
        operands.append(earlier)
        aliases = {4: 0}
    return pl.pallas_call(
        kernel,
        grid=(wide // TILE,),
        in_specs=in_specs,
        out_specs=pl.BlockSpec((count, TILE), lambda i: (0, i + skip)),
        out_shape=jax.ShapeDtypeStruct((count, width), BF),
        input_output_aliases=aliases,
        compiler_params=params(),
        cost_estimate=cost(4 * count * count * wide, 8 * count * wide),
        name="finish_hidden",
    )(*operands)


def dispatch(where, base, recv, gain, pos, placing):
    rows, width = base.shape
    quarter = width // 4
    seats = placing.shape[0]

    half = width // 2

    def kernel(where_ref, base, r0, r1, r2, r3, gain, pos, placing, front, out, held, came, sems):
        copies = [fetch(r, came.at[n], sems.at[n]) for n, r in enumerate((r0, r1, r2, r3))]
        pick = onehot(0, rows, pos[:1, :])
        square = jnp.zeros((rows, 1), F32)
        for n in range(2):
            copies[n].wait()
            copies[n + 2].wait()
            at = slice(n * half, (n + 1) * half)
            total = base[:, at] + came[n].astype(F32) + came[n + 2].astype(F32)
            rounded = total.astype(BF)
            front[:, at] = rounded
            total = rounded.astype(F32)
            square = square + jnp.sum(total * total, axis=1, keepdims=True)
        scale = lax.rsqrt(square * (1.0 / width) + 1e-06)
        held[...] = (front[...].astype(F32) * scale * gain[...]).astype(BF)
        seat = lax.dot_general(
            placing[...], pick, (((1,), (1,)), ((), ())), preferred_element_type=F32
        ).astype(BF)
        for side in range(2):
            for n in range(2):
                at = pl.multiple_of((side * 2 + lax.rem(where_ref[1] + n, 2)) * quarter, 128)
                got = dot(seat, held[:, pl.ds(at, quarter)])
                out[side * seats : (side + 1) * seats, n * quarter : (n + 1) * quarter] = got.astype(BF)

    vmem = pl.BlockSpec(memory_space=pltpu.VMEM)
    return pl.pallas_call(
        kernel,
        in_specs=[pl.BlockSpec(memory_space=pltpu.SMEM), vmem]
        + [pl.BlockSpec(memory_space=pl.ANY)] * 4
        + [vmem] * 3,
        out_specs=[vmem] * 2,
        out_shape=[
            jax.ShapeDtypeStruct((rows, width), BF),
            jax.ShapeDtypeStruct((2 * seats, width // 2), BF),
        ],
        scratch_shapes=[
            pltpu.VMEM((rows, width), BF),
            pltpu.VMEM((4, rows, half), BF),
            pltpu.SemaphoreType.DMA((4,)),
        ],
        compiler_params=params(),
        cost_estimate=cost(2 * seats * rows * width, 20 * rows * width),
        name="dispatch",
    )(where, base, *recv, gain, pos, placing)


def gate_up(where, blocks, wg, wg2, wu, wu2):
    per = blocks[0][0].shape[0]
    depth, ff = wg.shape
    keep = 2 * per

    def kernel(where_ref, a0, a1, a2, a3, b0, b1, b2, b3, wg, wg2, wu, wu2, mine, away):
        first = jnp.concatenate([a0[...], a1[...], a2[...], a3[...]], axis=0)
        last = jnp.concatenate([b0[...], b1[...], b2[...], b3[...]], axis=0)
        for n, (w, w2) in enumerate(((wg, wg2), (wu, wu2))):
            total = dot(first, w[...]) + dot(last, w2[...])
            columns = slice(n * ff, (n + 1) * ff)
            low = where_ref[3] == 0
            mine[:, columns] = jnp.where(low, total[:keep], total[keep:])
            away[:, columns] = jnp.where(low, total[keep:], total[:keep]).astype(BF)

    vmem = pl.BlockSpec(memory_space=pltpu.VMEM)
    return pl.pallas_call(
        kernel,
        in_specs=[pl.BlockSpec(memory_space=pltpu.SMEM)] + [vmem] * 12,
        out_specs=[vmem, vmem],
        out_shape=[
            jax.ShapeDtypeStruct((keep, 2 * ff), F32),
            jax.ShapeDtypeStruct((keep, 2 * ff), BF),
        ],
        compiler_params=params(),
        cost_estimate=cost(16 * per * 2 * depth * ff, 8 * per * 2 * depth + 8 * depth * ff),
        name="gate_up",
    )(where, *[a for a, _ in blocks], *[b for _, b in blocks], wg, wg2, wu, wu2)


def down(where, mine, other, wd, wd2):
    rows, ff = mine.shape
    quarter = wd.shape[1]
    per = rows // 2

    def kernel(where_ref, mine, other, wd, wd2, *outs):
        low = where_ref[3] == 0
        first = jnp.where(low, mine[...], other[...])
        second = jnp.where(low, other[...], mine[...])
        both = jnp.concatenate([first, second], axis=0)
        for n, w in enumerate((wd, wd2)):
            for c in range(2):
                got = dot(both, w[:, c * TILE : (c + 1) * TILE]).astype(BF)
                for k in range(RING):
                    outs[2 * k + n][:, c * TILE : (c + 1) * TILE] = got[k * per : (k + 1) * per]

    vmem = pl.BlockSpec(memory_space=pltpu.VMEM)
    return pl.pallas_call(
        kernel,
        in_specs=[pl.BlockSpec(memory_space=pltpu.SMEM), vmem, vmem, vmem, vmem],
        out_specs=[vmem] * 8,
        out_shape=[jax.ShapeDtypeStruct((per, quarter), BF)] * 8,
        compiler_params=params(),
        cost_estimate=cost(8 * rows * ff * quarter, 4 * ff * quarter + 8 * rows * quarter),
        name="down",
    )(where, mine, other, wd, wd2)


def mix(where, returned, high, low):
    rows, half = returned.shape
    seats, count = high.shape
    quarter = half // 2

    def kernel(where_ref, returned, high, low, out):
        for side in range(2):
            for n in range(2):
                part = returned[side * seats : (side + 1) * seats, n * quarter : (n + 1) * quarter]
                total = None
                for factor in (high, low):
                    got = lax.dot_general(
                        factor[...], part, (((0,), (0,)), ((), ())), preferred_element_type=F32
                    )
                    total = got if total is None else total + got
                at = pl.multiple_of((2 * side + lax.rem(where_ref[1] + n, 2)) * quarter, 128)
                out[:, pl.ds(at, quarter)] = total.astype(BF)

    vmem = pl.BlockSpec(memory_space=pltpu.VMEM)
    return pl.pallas_call(
        kernel,
        in_specs=[pl.BlockSpec(memory_space=pltpu.SMEM)] + [vmem] * 3,
        out_specs=vmem,
        out_shape=jax.ShapeDtypeStruct((count, 2 * half), BF),
        compiler_params=params(),
        cost_estimate=cost(8 * seats * half * count, 2 * rows * half + 4 * count * half),
        name="mix",
    )(where, returned, high, low)


def find_seats(ids, gates):
    top, count = ids.shape
    seats = EXPERTS * SEAT

    def kernel(ids, gates, placing, high, low):
        row = lax.broadcasted_iota(jnp.int32, (count, count), 0)
        column = lax.broadcasted_iota(jnp.int32, (count, count), 1)
        tri = (row <= column).astype(BF)
        seat = lax.broadcasted_iota(jnp.int32, (SEAT, count), 0)
        for expert in range(EXPERTS):
            match = ids[...] == expert
            here = jnp.sum(match.astype(F32), axis=0, keepdims=True)
            gate = jnp.sum(jnp.where(match, gates[...], 0.0), axis=0, keepdims=True)
            upto = dot(jnp.broadcast_to(here, (SEAT, count)).astype(BF), tri)
            found = (here > 0.0) & (upto == (seat + 1).astype(F32)) & (seat < CAP)
            picked = found.astype(F32)
            factor = picked * gate
            first = factor.astype(BF)
            at = slice(expert * SEAT, (expert + 1) * SEAT)
            placing[at] = picked
            high[at] = first.astype(F32)
            low[at] = factor - first.astype(F32)

    vmem = pl.BlockSpec(memory_space=pltpu.VMEM)
    out = pl.pallas_call(
        kernel,
        in_specs=[vmem, vmem],
        out_specs=[vmem] * 3,
        out_shape=[jax.ShapeDtypeStruct((seats, count), F32)] * 3,
        compiler_params=params(),
        cost_estimate=cost(2 * seats * count * count, 32 * seats * count),
        name="find_seats",
    )(ids, gates)
    return [a.astype(BF) for a in out]


def reseat(rows, columns):
    row = lax.broadcasted_iota(jnp.int32, (rows, columns), 0)
    column = lax.broadcasted_iota(jnp.int32, (rows, columns), 1)
    if rows < columns:
        return ((row // CAP == column // SEAT) & (row % CAP == column % SEAT)).astype(BF)
    return ((row // SEAT == column // CAP) & (row % SEAT == column % CAP)).astype(BF)


def pack(rows):
    wide, half = rows.shape
    short = wide // SEAT * CAP
    quarter = half // 2

    def kernel(rows, first, last):
        take = reseat(short, wide)
        first[...] = dot(take, rows[:, :quarter]).astype(BF)
        last[...] = dot(take, rows[:, quarter:]).astype(BF)

    vmem = pl.BlockSpec(memory_space=pltpu.VMEM)
    return pl.pallas_call(
        kernel,
        in_specs=[vmem],
        out_specs=[vmem, vmem],
        out_shape=[jax.ShapeDtypeStruct((short, quarter), BF)] * 2,
        compiler_params=params(),
        cost_estimate=cost(2 * short * wide * half, 4 * wide * half),
        name="pack",
    )(rows)


def add_parts(own, behind, ahead):
    short, quarter = own[0].shape
    wide = short // CAP * SEAT

    def kernel(*refs):
        put = reseat(wide, short)
        for n in range(2):
            total = refs[n][...].astype(F32) + refs[2 + n][...].astype(F32) + refs[4 + n][...].astype(F32)
            refs[6][:, n * quarter : (n + 1) * quarter] = dot(put, total.astype(BF)).astype(BF)

    vmem = pl.BlockSpec(memory_space=pltpu.VMEM)
    return pl.pallas_call(
        kernel,
        in_specs=[vmem] * 6,
        out_specs=vmem,
        out_shape=jax.ShapeDtypeStruct((wide, 2 * quarter), BF),
        compiler_params=params(),
        cost_estimate=cost(4 * short * wide * quarter, 20 * short * quarter),
        name="add_parts",
    )(*own, *behind, *ahead)


def local(attn_partial, residual, gain, expert_ids, gate_vals, w_gate, w_up, w_down):
    count, width = residual.shape
    ff = w_gate.shape[2]
    barrier = lax.optimization_barrier
    where = jnp.stack([lax.axis_index(a) for a in ("x", "core", "y", "zh")]).astype(jnp.int32)
    grid = ("zh", "y", "zl")
    attn = attn_partial[0]
    wg, wu, wd = w_gate[0], w_up[0], w_down[0]
    gain = gain.reshape(1, width)

    with jax.named_scope("routing"):
        token = jnp.arange(count, dtype=jnp.int32)
        anyone = jnp.any(expert_ids < EXPERTS, axis=1)
        tri = (token[:, None] >= token[None, :]).astype(BF)
        ahead = dot(tri, anyone[:, None].astype(BF)).astype(jnp.int32)[:, 0]
        pos = jnp.where(anyone, ahead - 1, ahead[-1] + token - ahead).reshape(1, count)
        base = own_rows(where, attn, residual, pos, FRONT)
        poses = jnp.concatenate([pos] + [shift(pos, -k) for k in (1, 2, 3)], axis=0)
        poses, base = barrier((poses, base))

    with jax.named_scope("weight_swap"):
        wg2 = lax.ppermute(wg, "core", SWAP)
        wu2 = lax.ppermute(wu, "core", SWAP)
        wd2 = lax.ppermute(wd, "core", SWAP)

    with jax.named_scope("front_sum"):
        far = select_rows(where, attn, poses, FRONT, (2,))
        far, poses = barrier((far, poses))
        near = select_rows(where, attn, poses, FRONT, (1, 3))
        near, poses, ids, gates = barrier((near, poses, expert_ids.T, gate_vals.T))
        back = [back_rows(where, attn, poses, FRONT, 0, PIECES[0] * TILE)]
        seats = find_seats(ids, gates)
        behind, ahead, (back, seats) = ring_sum(far, near[:2], near[2:], (back, seats))
        placing, high, low = seats
    def head_sum(n, after):
        operand, after = barrier((back[n], after))
        with jax.named_scope("head_sum"):
            summed = lax.psum_scatter(operand, "x", scatter_dimension=0, tiled=True)
        return summed[0], after

    with jax.named_scope("rows_out"):
        front, message = dispatch(where, base, (*behind, *ahead), gain, poses, placing)
        summed0, message = head_sum(0, message)
        late_poses, message = barrier((poses, message))
        left = PIECES[0] * TILE
        for tiles in PIECES[1:]:
            back.append(back_rows(where, attn, late_poses, FRONT, left, tiles * TILE))
            left += tiles * TILE
        whole = lax.all_to_all(message, grid, split_axis=0, concat_axis=0, tiled=True)
        whole, back = barrier((whole, back))
        rows = ring_gather(*pack(whole))
    with jax.named_scope("gate_up"):
        mine, away = gate_up(where, rows, wg, wg2, wu, wu2)
        summed1, away = head_sum(1, away)
        mine = mine + lax.ppermute(away, "zh", SWAP).astype(F32)
        middle = (jax.nn.silu(mine[:, :ff]) * mine[:, ff:]).astype(BF)
        other = lax.ppermute(middle, "zh", SWAP)
    with jax.named_scope("rows_back"):
        outs = down(where, middle, other, wd, wd2)
        total = add_parts(outs[:2], *ring_sum(outs[4:6], outs[6:8], outs[2:4])[:2])
        summed2, total = head_sum(2, total)
        returned = lax.all_to_all(total, grid, split_axis=0, concat_axis=0, tiled=True)
    with jax.named_scope("hidden"):
        hidden, left = None, 0
        for tiles, summed in zip(PIECES, (summed0, summed1, summed2)):
            if left + tiles * TILE == width:
                returned, hidden = barrier((returned, hidden))
            hidden = finish_hidden(where, front, residual, summed, poses, left, hidden)
            left += tiles * TILE
    with jax.named_scope("mix"):
        moe_out = mix(where, returned, high, low)
    return hidden, moe_out


def solution(mesh):
    grid = Mesh(mesh.devices.reshape(2, 2, 4, 2, 4), ("zh", "core", "y", "zl", "x"))
    group = ("zh", "core", "y", "zl")
    token = P(group + ("x",), None)
    placed = (
        P("x", group, None),
        token,
        P(),
        token,
        token,
        P(("y", "zl"), ("zh", "core"), "x"),
        P(("y", "zl"), ("zh", "core"), "x"),
        P(("y", "zl"), "x", ("zh", "core")),
    )
    return jax.shard_map(
        local, mesh=grid, in_specs=placed, out_specs=(token, token), check_vma=False
    )
```

time: 234 us -> 199 us (0.85)
  Pallas kernels: 0 us -> 42.9 us
  waiting for transfers between devices: 110 us -> 69.2 us
  matrix products: 34.8 us -> 0.14 us
  starting transfers between devices: 22.8 us -> 50.7 us
  blocking collectives: 23.5 us -> 0 us
  between operations: 1.17 us -> 14.1 us
  local copies, waits for them, and re-layouts: 23.7 us -> 14.4 us
  other arithmetic: 14.2 us -> 5.43 us
    ppermute x15 -> x21, waiting for transfers between devices: 98.6 us -> 29.9 us  [shift(): lax.ppermute(value, 'x', [(j, (j + steps) % RING) for j in range(RING)])]
    pallas_call x0 -> x16, Pallas kernels: none -> 42.9 us  [the longest x3 12.4 us: back_rows(): pl.pallas_call(kernel, in_specs=[pl.BlockSpec(memory_space=pltpu.SMEM), p...]
    dot_general x21 -> x1, matrix products: 34.8 us -> 0.14 us  [dot(): return jnp.dot(a, b, preferred_element_type=F32)]
    all_to_all x1 -> x0, blocking collectives: 23.5 us -> none  [local(): got = lax.all_to_all(rows, grid, split_axis=0, concat_axis=0, tiled=True)]
    ppermute x15 -> x21, starting transfers between devices: 16.1 us -> 34.4 us  [shift(): lax.ppermute(value, 'x', [(j, (j + steps) % RING) for j in range(RING)])]
    all_to_all x1 -> x2, waiting for transfers between devices: 0.01 us -> 15.6 us  [the longest x1 7.89 us: local(): lax.all_to_all(message, grid, split_axis=0, concat_axis=0, tiled=True)]
    rev x2 -> x0, local copies, waits for them, and re-layouts: 10.1 us -> none  [the longest x1 6.96 us: local(): rows = jnp.where(core == 0, rows, rows[:, :, :, :, ::-1])]
    all_to_all x1 -> x2, starting transfers between devices: 3.85 us -> 13.8 us  [the longest x1 8.04 us: local(): lax.all_to_all(message, grid, split_axis=0, concat_axis=0, tiled=True)]
  transfers between devices with their start and end apart: 21 -> 31, of which waited for: 10 -> 15; matrix products, arithmetic and copies ran while one was open for 17% -> 1% of each run, Pallas kernels for 0% -> 18%
where the time goes in v2:
time: 199 us; the launch traced here: 197 us
  waiting for transfers between devices  69.2 us (35%)
  starting transfers between devices  50.7 us (25%)
  Pallas kernels  42.9 us (22%)
  local copies, waits for them, and re-layouts  14.4 us (7%)
  between operations  14.1 us (7%)
  other arithmetic  5.43 us (3%)
    ppermute x21, starting transfers between devices, shift(): lax.ppermute(value, 'x', [(j, (j + steps) % RING) for j in range(RING)])  34.4 us
    ppermute x21, waiting for transfers between devices, shift(): lax.ppermute(value, 'x', [(j, (j + steps) % RING) for j in range(RING)])  29.9 us
    unnamed x54, local copies, waits for them, and re-layouts  13.8 us
    pallas_call x3, Pallas kernels, back_rows(): pl.pallas_call(kernel, in_specs=[pl.BlockSpec(memory_space=pltpu.SMEM), p...  12.4 us
    ppermute x1, waiting for transfers between devices, local(): mine = mine + lax.ppermute(away, 'zh', SWAP).astype(F32)  11 us
    all_to_all x1, starting transfers between devices, local(): lax.all_to_all(message, grid, split_axis=0, concat_axis=0, tiled=True)  8.04 us
    all_to_all x1, waiting for transfers between devices, local(): lax.all_to_all(message, grid, split_axis=0, concat_axis=0, tiled=True)  7.89 us
    all_to_all x1, waiting for transfers between devices, local(): lax.all_to_all(total, grid, split_axis=0, concat_axis=0, tiled=True)  7.75 us
  transfers between devices with their start and end apart: 31, of which 15 were waited for; matrix products, arithmetic and copies ran while one was open for 1% of the time, Pallas kernels for 18%

profile of v2, /device:TPU:0, one launch (start us, length us, event | category | flops | bytes accessed | tf_op | source)
XLA Modules:
  0.0 196.9 jit_solution(7693448618534782213)
XLA Ops:
  9.3 1.6 collective-permute-start.2
  11.0 2.7 %collective-permute-start.1 = (s32[1,128]{1,0:T(1,128)S(1)}, s32[1,128]{1,0:T(1,128)S(1)}, u32[]{:S(2)}, u32[]{:S(2)}) collective-permute-start(s32[1,128]{1,0:T(1,128)S(1)} %select_bitcast_fusion.pos), channel_id=1, source_target_pairs={{0,2},{1,3},{2,0},{3,1},{4,6},{5,7},{6,4},{7,5},{8,10},{9,11},{10,... | collective-permute-start | bytes 1544 | tf_op jit(solution)/shard_map/routing/ppermute | solution.py:22
  13.7 1.4 collective-permute-start
  15.7 4.0 %own_rows.1.base = f32[40,7168]{1,0:T(8,128)} custom-call(s32[4]{0:T(128)} %pad_add_fusion.1.where_ref, bf16[512,7168]{1,0:T(8,128)(2,1)} %bitcast.44, bf16[128,7168]{1,0:T(8,128)(2,1)} %residual.5, s32[1,128]{1,0:T(1,128)} %copy-done.26), custom_call_target="tpu_custom_call" | custom-call | flops 146800640 | bytes 4816896 | tf_op jit(solution)/shard_map/routing/own_rows/pallas_call | solution.py:125
  19.8 1.2 pad_add_fusion.poses.pos
  21.0 3.1 %select_rows.2 = (bf16[40,3584]{1,0:T(8,128)(2,1)}, bf16[40,3584]{1,0:T(8,128)(2,1)}) custom-call(s32[4]{0:T(128)} %pad_add_fusion.1.where_ref, bf16[512,7168]{1,0:T(8,128)(2,1)} %bitcast.45, s32[4,128]{1,0:T(4,128)} %pad_add_fusion.poses.pos), custom_call_target="tpu_custom_call" | custom-call | flops 73400320 | bytes 3670016 | tf_op jit(solution)/shard_map/front_sum/select_rows/pallas_call | solution.py:89
  24.8 2.6 %collective-permute-start.4 = (bf16[40,3584]{1,0:T(8,128)(2,1)}, bf16[40,3584]{1,0:T(8,128)(2,1)S(1)}, u32[]{:S(2)}, u32[]{:S(2)}) collective-permute-start(bf16[40,3584]{1,0:T(8,128)(2,1)} %get-tuple-element.67), channel_id=1, source_target_pairs={{0,3},{1,0},{2,1},{3,2},{4,7},{5,4},{6,5},{7,6},{8,11},{9,8},{10,9... | collective-permute-start | bytes 860168 | tf_op jit(solution)/shard_map/front_sum/ppermute | solution.py:22
  27.5 3.7 %select_rows.3 = (bf16[40,3584]{1,0:T(8,128)(2,1)}, bf16[40,3584]{1,0:T(8,128)(2,1)}, bf16[40,3584]{1,0:T(8,128)(2,1)}, bf16[40,3584]{1,0:T(8,128)(2,1)}) custom-call(s32[4]{0:T(128)} %pad_add_fusion.1.where_ref, bf16[512,7168]{1,0:T(8,128)(2,1)} %bitcast.46, s32[4,128]{1,0:T(4,128)} %pad_add_fusion.poses.pos), custom_call_target="tpu_custom_call" | custom-call | flops 146800640 | bytes 7340032 | tf_op jit(solution)/shard_map/front_sum/select_rows/pallas_call | solution.py:89
  33.3 3.2 %collective-permute-start.7 = (bf16[40,3584]{1,0:T(8,128)(2,1)}, bf16[40,3584]{1,0:T(8,128)(2,1)S(1)}, u32[]{:S(2)}, u32[]{:S(2)}) collective-permute-start(bf16[40,3584]{1,0:T(8,128)(2,1)} %get-tuple-element.76), channel_id=1, source_target_pairs={{0,3},{1,0},{2,1},{3,2},{4,7},{5,4},{6,5},{7,6},{8,11},{9,8},{10,9... | collective-permute-start | bytes 860168 | tf_op jit(solution)/shard_map/front_sum/ppermute | solution.py:22
  36.5 3.8 %back_rows.3 = bf16[4,88,1792]{2,1,0:T(8,128)(2,1)} custom-call(s32[4]{0:T(128)} %pad_add_fusion.1.where_ref, bf16[512,7168]{1,0:T(8,128)(2,1)} %bitcast.47, s32[4,128]{1,0:T(4,128)} %pad_add_fusion.poses.pos), custom_call_target="tpu_custom_call" | custom-call | flops 161480704 | bytes 3096576 | tf_op jit(solution)/shard_map/front_sum/back_rows/pallas_call | solution.py:154
  40.6 3.3 %collective-permute-start.8 = (bf16[40,3584]{1,0:T(8,128)(2,1)S(1)}, bf16[40,3584]{1,0:T(8,128)(2,1)S(1)}, u32[]{:S(2)}, u32[]{:S(2)}) collective-permute-start(bf16[40,3584]{1,0:T(8,128)(2,1)S(1)} %add_convert_fusion.2), channel_id=1, source_target_pairs={{0,3},{1,0},{2,1},{3,2},{4,7},{5,4},{6,5},{7,6},{8,11},{9,8},{10,9... | collective-permute-start | bytes 860168 | tf_op jit(solution)/shard_map/front_sum/ppermute | solution.py:22
  45.4 3.0 %collective-permute-done.5.r0 = bf16[40,3584]{1,0:T(8,128)(2,1)S(1)} collective-permute-done((bf16[40,3584]{1,0:T(8,128)(2,1)S(1)}, bf16[40,3584]{1,0:T(8,128)(2,1)S(1)}, u32[]{:S(2)}, u32[]{:S(2)}) %collective-permute-start.5) | collective-permute-done | bytes 286752 | tf_op jit(solution)/shard_map/front_sum/ppermute | solution.py:22
  53.0 1.7 dispatch.1
  56.3 8.0 %all-to-all-start = ((bf16[16,8,3584]{2,1,0:T(8,128)(2,1)}), bf16[16,8,3584]{2,1,0:T(8,128)(2,1)S(1)}, u32[]{:S(2)}, u32[]{:S(2)}) async-start(bf16[16,8,3584]{2,1,0:T(8,128)(2,1)} %bitcast.35), calls=%async_computation | async-start | bytes 1835008 | tf_op jit(solution)/shard_map/rows_out/all_to_all | solution.py:483
  64.4 4.3 %back_rows.4 = bf16[4,88,2688]{2,1,0:T(8,128)(2,1)} custom-call(s32[4]{0:T(128)} %pad_add_fusion.1.where_ref, bf16[512,7168]{1,0:T(8,128)(2,1)} %bitcast.48, s32[4,128]{1,0:T(4,128)} %pad_add_fusion.poses.pos), custom_call_target="tpu_custom_call" | custom-call | flops 242221056 | bytes 4644864 | tf_op jit(solution)/shard_map/rows_out/back_rows/pallas_call | solution.py:154
  68.7 4.3 %back_rows.5 = bf16[4,88,2688]{2,1,0:T(8,128)(2,1)} custom-call(s32[4]{0:T(128)} %pad_add_fusion.1.where_ref, bf16[512,7168]{1,0:T(8,128)(2,1)} %bitcast.49, s32[4,128]{1,0:T(4,128)} %pad_add_fusion.poses.pos), custom_call_target="tpu_custom_call" | custom-call | flops 242221056 | bytes 4644864 | tf_op jit(solution)/shard_map/rows_out/back_rows/pallas_call | solution.py:154
  73.0 7.9 %all-to-all-done = bf16[16,8,3584]{2,1,0:T(8,128)(2,1)S(1)} async-done(((bf16[16,8,3584]{2,1,0:T(8,128)(2,1)}), bf16[16,8,3584]{2,1,0:T(8,128)(2,1)S(1)}, u32[]{:S(2)}, u32[]{:S(2)}) %all-to-all-start) | async-done | bytes 917536 | tf_op jit(solution)/shard_map/rows_out/all_to_all | solution.py:483
  81.3 3.5 %collective-permute-start.11 = (bf16[80,1792]{1,0:T(8,128)(2,1)S(1)}, bf16[80,1792]{1,0:T(8,128)(2,1)S(1)}, u32[]{:S(2)}, u32[]{:S(2)}) collective-permute-start(bf16[80,1792]{1,0:T(8,128)(2,1)S(1)} %get-tuple-element.88.a0), channel_id=1, source_target_pairs={{0,3},{1,0},{2,1},{3,2},{4,7},{5,4},{6,5},{7,6},{8,11},{9,8},{10,9... | collective-permute-start | bytes 860168 | tf_op jit(solution)/shard_map/rows_out/ppermute | solution.py:22
  84.7 1.9 collective-permute-start.13
  86.7 3.5 %collective-permute-done.9.a1 = bf16[80,1792]{1,0:T(8,128)(2,1)S(1)} collective-permute-done((bf16[80,1792]{1,0:T(8,128)(2,1)S(1)}, bf16[80,1792]{1,0:T(8,128)(2,1)S(1)}, u32[]{:S(2)}, u32[]{:S(2)}) %collective-permute-start.9) | collective-permute-done | bytes 286752 | tf_op jit(solution)/shard_map/rows_out/ppermute | solution.py:22
  90.2 1.8 collective-permute-done.11.a3
  92.0 1.8 collective-permute-start.10
  93.8 1.9 collective-permute-done.13.b3
  95.7 3.7 %collective-permute-start.14 = (bf16[80,1792]{1,0:T(8,128)(2,1)S(1)}, bf16[80,1792]{1,0:T(8,128)(2,1)S(1)}, u32[]{:S(2)}, u32[]{:S(2)}) collective-permute-start(bf16[80,1792]{1,0:T(8,128)(2,1)S(1)} %collective-permute-done.13.b3), channel_id=1, source_target_pairs={{0,3},{1,0},{2,1},{3,2},{4,7},{5,4},{6,5},{7,6},{8,11},{9,8},{10,9... | collective-permute-start | bytes 860168 | tf_op jit(solution)/shard_map/rows_out/ppermute | solution.py:22
  99.4 1.8 collective-permute-done.12.b1
  101.2 3.1 %collective-permute-done.10.a2 = bf16[80,1792]{1,0:T(8,128)(2,1)S(1)} collective-permute-done((bf16[80,1792]{1,0:T(8,128)(2,1)S(1)}, bf16[80,1792]{1,0:T(8,128)(2,1)S(1)}, u32[]{:S(2)}, u32[]{:S(2)}) %collective-permute-start.10) | collective-permute-done | bytes 286752 | tf_op jit(solution)/shard_map/rows_out/ppermute | solution.py:22
  104.3 1.5 copy-done.3
  105.8 4.6 %gate_up.1 = (f32[160,1024]{1,0:T(8,128)S(1)}, bf16[160,1024]{1,0:T(8,128)(2,1)S(1)}) custom-call(s32[4]{0:T(128)S(1)} %copy-done.18, bf16[80,1792]{1,0:T(8,128)(2,1)S(1)} %get-tuple-element.88.a0, bf16[80,1792]{1,0:T(8,128)(2,1)S(1)} %collective-permute-done.9.a1, bf16[80,1792]{1,0:T(8,128)(2,1)S(1)} %collective-permute-done.10.a2, ...), custom_call_target="tpu_custom_call" | custom-call | flops 2348810240 | bytes 9633792 | tf_op jit(solution)/shard_map/gate_up/gate_up/pallas_call | solution.py:275
  111.2 1.4 copy-done.22
  113.5 11.0 %collective-permute-done.17 = bf16[160,1024]{1,0:T(8,128)(2,1)S(1)} collective-permute-done((bf16[160,1024]{1,0:T(8,128)(2,1)}, bf16[160,1024]{1,0:T(8,128)(2,1)S(1)}, u32[]{:S(2)}, u32[]{:S(2)}) %collective-permute-start.17) | collective-permute-done | bytes 327712 | tf_op jit(solution)/shard_map/gate_up/ppermute | solution.py:489
  125.6 6.5 %collective-permute-done.18.other = bf16[160,512]{1,0:T(8,128)(2,1)S(1)} collective-permute-done((bf16[160,512]{1,0:T(8,128)(2,1)S(1)}, bf16[160,512]{1,0:T(8,128)(2,1)S(1)}, u32[]{:S(2)}, u32[]{:S(2)}) %collective-permute-start.18) | collective-permute-done | bytes 163872 | tf_op jit(solution)/shard_map/gate_up/ppermute | solution.py:491
  132.0 2.1 %down.1 = (bf16[80,1792]{1,0:T(8,128)(2,1)S(1)}, bf16[80,1792]{1,0:T(8,128)(2,1)S(1)}, bf16[80,1792]{1,0:T(8,128)(2,1)S(1)}, bf16[80,1792]{1,0:T(8,128)(2,1)S(1)...) custom-call(s32[4]{0:T(128)S(1)} %copy-done.18, ...), custom_call_target="tpu_custom_call" | custom-call | flops 1174405120 | bytes 5963776 | tf_op jit(solution)/shard_map/rows_back/down/pallas_call | solution.py:306
  134.2 1.6 collective-permute-start.22
  135.8 1.7 collective-permute-start.23
  137.5 1.9 collective-permute-start.24
  139.4 5.7 %collective-permute-done.20 = bf16[80,1792]{1,0:T(8,128)(2,1)S(1)} collective-permute-done((bf16[80,1792]{1,0:T(8,128)(2,1)S(1)}, bf16[80,1792]{1,0:T(8,128)(2,1)S(1)}, u32[]{:S(2)}, u32[]{:S(2)}) %collective-permute-start.20) | collective-permute-done | bytes 286752 | tf_op jit(solution)/shard_map/rows_back/ppermute | solution.py:22
  145.3 4.7 %collective-permute-done.24 = bf16[80,1792]{1,0:T(8,128)(2,1)S(1)} collective-permute-done((bf16[80,1792]{1,0:T(8,128)(2,1)S(1)}, bf16[80,1792]{1,0:T(8,128)(2,1)S(1)}, u32[]{:S(2)}, u32[]{:S(2)}) %collective-permute-start.24) | collective-permute-done | bytes 286752 | tf_op jit(solution)/shard_map/rows_back/ppermute | solution.py:22
  150.1 2.3 %collective-permute-start.25 = (bf16[80,1792]{1,0:T(8,128)(2,1)S(1)}, bf16[80,1792]{1,0:T(8,128)(2,1)S(1)}, u32[]{:S(2)}, u32[]{:S(2)}) collective-permute-start(bf16[80,1792]{1,0:T(8,128)(2,1)S(1)} %add_convert_fusion), channel_id=1, source_target_pairs={{0,3},{1,0},{2,1},{3,2},{4,7},{5,4},{6,5},{7,6},{8,11},{9,8},{10,9... | collective-permute-start | bytes 860168 | tf_op jit(solution)/shard_map/rows_back/ppermute | solution.py:22
  152.4 2.9 %collective-permute-done.21.refs_2_ = bf16[80,1792]{1,0:T(8,128)(2,1)S(1)} collective-permute-done((bf16[80,1792]{1,0:T(8,128)(2,1)S(1)}, bf16[80,1792]{1,0:T(8,128)(2,1)S(1)}, u32[]{:S(2)}, u32[]{:S(2)}) %collective-permute-start.21) | collective-permute-done | bytes 286752 | tf_op jit(solution)/shard_map/rows_back/ppermute | solution.py:22
  155.3 1.5 collective-permute-done.25.refs_5_
  156.8 1.4 add_parts.1
  158.2 5.7 %all-to-all-start.1 = ((bf16[16,8,3584]{2,1,0:T(8,128)(2,1)}), bf16[16,8,3584]{2,1,0:T(8,128)(2,1)S(1)}, u32[]{:S(2)}, u32[]{:S(2)}) async-start(bf16[16,8,3584]{2,1,0:T(8,128)(2,1)} %bitcast.18), calls=%async_computation.1 | async-start | bytes 1835008 | tf_op jit(solution)/shard_map/rows_back/all_to_all | solution.py:496
  165.0 1.7 finish_hidden.3.refs_0_
  167.7 2.4 %finish_hidden.4.refs_0_ = bf16[128,7168]{1,0:T(8,128)(2,1)} custom-call(bf16[40,7168]{1,0:T(8,128)(2,1)S(1)} %get-tuple-element.80.front, bf16[128,7168]{1,0:T(8,128)(2,1)S(1)} %copy-done, bf16[88,2688]{1,0:T(8,128)(2,1)S(1)} %bitcast.36, s32[4,128]{1,0:T(4,128)S(1)} %copy-done.13, ...), custom_call_target="tpu_custom_call", output_to_operand_aliasing={{}: (4, {})} | custom-call | flops 176160768 | bytes 2752512 | tf_op jit(solution)/shard_map/hidden/finish_hidden/pallas_call | solution.py:193
  170.1 7.7 %all-to-all-done.1 = bf16[16,8,3584]{2,1,0:T(8,128)(2,1)S(1)} async-done(((bf16[16,8,3584]{2,1,0:T(8,128)(2,1)}), bf16[16,8,3584]{2,1,0:T(8,128)(2,1)S(1)}, u32[]{:S(2)}, u32[]{:S(2)}) %all-to-all-start.1) | async-done | bytes 917536 | tf_op jit(solution)/shard_map/rows_back/all_to_all | solution.py:496
  177.9 2.9 %mix.1 = bf16[128,7168]{1,0:T(8,128)(2,1)} custom-call(s32[4]{0:T(128)S(1)} %copy-done.18, bf16[128,3584]{1,0:T(8,128)(2,1)S(1)} %bitcast.30, bf16[64,128]{1,0:T(8,128)(2,1)S(1)} %copy-done.14, bf16[64,128]{1,0:T(8,128)(2,1)S(1)} %copy-done.15), custom_call_target="tpu_custom_call" | custom-call | flops 234881024 | bytes 2752512 | tf_op jit(solution)/shard_map/mix/mix/pallas_call | solution.py:336
  180.8 6.2 %reduce-scatter.10.cloned.1.call-done = bf16[1,88,2688]{2,1,0:T(8,128)(2,1)} async-done(((bf16[4,88,2688]{2,1,0:T(8,128)(2,1)}), bf16[1,88,2688]{2,1,0:T(8,128)(2,1)}) %reduce-scatter.10.cloned.1.call-update) | async-done | bytes 473104
  188.0 2.4 %finish_hidden.5 = bf16[128,7168]{1,0:T(8,128)(2,1)} custom-call(bf16[40,7168]{1,0:T(8,128)(2,1)S(1)} %get-tuple-element.80.front, bf16[128,7168]{1,0:T(8,128)(2,1)S(1)} %copy-done, bf16[88,2688]{1,0:T(8,128)(2,1)S(1)} %bitcast.37, s32[4,128]{1,0:T(4,128)S(1)} %copy-done.13, bf16[128,7168]{1,0:T(8,128)(2,1)} %finish_hidden.4.refs_0_), custom_call_target="tpu_custom_call", output_to_operand_aliasing={{}: (4, {})} | custom-call | flops 176160768 | bytes 2752512 | tf_op jit(solution)/shard_map/hidden/finish_hidden/pallas_call | solution.py:193
  (102 shorter events, 19.9 us)
Async XLA Ops:
  7.2 156.8 %reduce-scatter.8.cloned.1.call-start = ((), (), s32[]{:S(2)}) async-start(), calls=%async_computation.5 | async-start | bytes 1576960 | tf_op jit(solution)/shard_map/rows_out/head_sum/reduce_scatter | solution.py:472
  9.3 6.4 %copy-start.26 = (s32[1,128]{1,0:T(1,128)}, s32[1,128]{1,0:T(1,128)S(1)}, u32[]{:S(2)}) copy-start(s32[1,128]{1,0:T(1,128)S(1)} %select_bitcast_fusion.pos) | copy-start | bytes 1540
  9.3 10.5 %collective-permute-start.2 = (s32[1,128]{1,0:T(1,128)S(1)}, s32[1,128]{1,0:T(1,128)S(1)}, u32[]{:S(2)}, u32[]{:S(2)}) collective-permute-start(s32[1,128]{1,0:T(1,128)S(1)} %select_bitcast_fusion.pos), channel_id=1, source_target_pairs={{0,1},{1,2},{2,3},{3,0},{4,5},{5,6},{6,7},{7,4},{8,9},{9,10},{10,1... | collective-permute-start | bytes 1544 | tf_op jit(solution)/shard_map/routing/ppermute | solution.py:22
  11.0 8.8 %collective-permute-start.1 = (s32[1,128]{1,0:T(1,128)S(1)}, s32[1,128]{1,0:T(1,128)S(1)}, u32[]{:S(2)}, u32[]{:S(2)}) collective-permute-start(s32[1,128]{1,0:T(1,128)S(1)} %select_bitcast_fusion.pos), channel_id=1, source_target_pairs={{0,2},{1,3},{2,0},{3,1},{4,6},{5,7},{6,4},{7,5},{8,10},{9,11},{10,... | collective-permute-start | bytes 1544 | tf_op jit(solution)/shard_map/routing/ppermute | solution.py:22
  13.7 6.1 %collective-permute-start = (s32[1,128]{1,0:T(1,128)S(1)}, s32[1,128]{1,0:T(1,128)S(1)}, u32[]{:S(2)}, u32[]{:S(2)}) collective-permute-start(s32[1,128]{1,0:T(1,128)S(1)} %select_bitcast_fusion.pos), channel_id=1, source_target_pairs={{0,3},{1,0},{2,1},{3,2},{4,7},{5,4},{6,5},{7,6},{8,11},{9,8},{10,9... | collective-permute-start | bytes 1544 | tf_op jit(solution)/shard_map/routing/ppermute | solution.py:22
  24.2 7.1 %copy-start.20 = (s32[128,8]{0,1:T(8,128)S(1)}, s32[128,8]{0,1:T(8,128)}, u32[]{:S(2)}) copy-start(s32[128,8]{0,1:T(8,128)} %param.11) | copy-start | bytes 12292
  24.2 7.1 %copy-start.21 = (f32[128,8]{0,1:T(8,128)S(1)}, f32[128,8]{0,1:T(8,128)}, u32[]{:S(2)}) copy-start(f32[128,8]{0,1:T(8,128)} %param.12) | copy-start | bytes 12292
  24.2 16.2 %collective-permute-start.3 = (bf16[40,3584]{1,0:T(8,128)(2,1)}, bf16[40,3584]{1,0:T(8,128)(2,1)S(1)}, u32[]{:S(2)}, u32[]{:S(2)}) collective-permute-start(bf16[40,3584]{1,0:T(8,128)(2,1)} %get-tuple-element.66), channel_id=1, source_target_pairs={{0,1},{1,2},{2,3},{3,0},{4,5},{5,6},{6,7},{7,4},{8,9},{9,10},{10,1... | collective-permute-start | bytes 860168 | tf_op jit(solution)/shard_map/front_sum/ppermute | solution.py:22
  24.8 15.5 %collective-permute-start.4 = (bf16[40,3584]{1,0:T(8,128)(2,1)}, bf16[40,3584]{1,0:T(8,128)(2,1)S(1)}, u32[]{:S(2)}, u32[]{:S(2)}) collective-permute-start(bf16[40,3584]{1,0:T(8,128)(2,1)} %get-tuple-element.67), channel_id=1, source_target_pairs={{0,3},{1,0},{2,1},{3,2},{4,7},{5,4},{6,5},{7,6},{8,11},{9,8},{10,9... | collective-permute-start | bytes 860168 | tf_op jit(solution)/shard_map/front_sum/ppermute | solution.py:22
  33.3 7.1 %copy-start.25 = (bf16[40,3584]{1,0:T(8,128)(2,1)S(1)}, bf16[40,3584]{1,0:T(8,128)(2,1)}, u32[]{:S(2)}) copy-start(bf16[40,3584]{1,0:T(8,128)(2,1)} %get-tuple-element.65) | copy-start | bytes 860164
  33.3 7.3 %copy-start.24 = (bf16[40,3584]{1,0:T(8,128)(2,1)S(1)}, bf16[40,3584]{1,0:T(8,128)(2,1)}, u32[]{:S(2)}) copy-start(bf16[40,3584]{1,0:T(8,128)(2,1)} %get-tuple-element.77) | copy-start | bytes 860164
  33.3 10.6 %collective-permute-start.6 = (bf16[40,3584]{1,0:T(8,128)(2,1)}, bf16[40,3584]{1,0:T(8,128)(2,1)S(1)}, u32[]{:S(2)}, u32[]{:S(2)}) collective-permute-start(bf16[40,3584]{1,0:T(8,128)(2,1)} %get-tuple-element.75), channel_id=1, source_target_pairs={{0,1},{1,2},{2,3},{3,0},{4,5},{5,6},{6,7},{7,4},{8,9},{9,10},{10,1... | collective-permute-start | bytes 860168 | tf_op jit(solution)/shard_map/front_sum/ppermute | solution.py:22
  33.3 11.4 %collective-permute-start.7 = (bf16[40,3584]{1,0:T(8,128)(2,1)}, bf16[40,3584]{1,0:T(8,128)(2,1)S(1)}, u32[]{:S(2)}, u32[]{:S(2)}) collective-permute-start(bf16[40,3584]{1,0:T(8,128)(2,1)} %get-tuple-element.76), channel_id=1, source_target_pairs={{0,3},{1,0},{2,1},{3,2},{4,7},{5,4},{6,5},{7,6},{8,11},{9,8},{10,9... | collective-permute-start | bytes 860168 | tf_op jit(solution)/shard_map/front_sum/ppermute | solution.py:22
  40.3 8.0 %copy-start.1 = (f32[40,7168]{1,0:T(8,128)S(1)}, f32[40,7168]{1,0:T(8,128)}, u32[]{:S(2)}) copy-start(f32[40,7168]{1,0:T(8,128)} %own_rows.1.base) | copy-start | bytes 3440644
  40.4 7.9 %collective-permute-start.5 = (bf16[40,3584]{1,0:T(8,128)(2,1)S(1)}, bf16[40,3584]{1,0:T(8,128)(2,1)S(1)}, u32[]{:S(2)}, u32[]{:S(2)}) collective-permute-start(bf16[40,3584]{1,0:T(8,128)(2,1)S(1)} %add_convert_fusion.3), channel_id=1, source_target_pairs={{0,1},{1,2},{2,3},{3,0},{4,5},{5,6},{6,7},{7,4},{8,9},{9,10},{10,1... | collective-permute-start | bytes 860168 | tf_op jit(solution)/shard_map/front_sum/ppermute | solution.py:22
  40.6 15.1 %copy-start.2 = (bf16[1,1792,512]{2,1,0:T(8,128)(2,1)S(1)}, bf16[1,1792,512]{2,1,0:T(8,128)(2,1)}, u32[]{:S(2)}) copy-start(bf16[1,1792,512]{2,1,0:T(8,128)(2,1)} %param.13) | copy-start | bytes 5505028
  40.6 7.7 %collective-permute-start.8 = (bf16[40,3584]{1,0:T(8,128)(2,1)S(1)}, bf16[40,3584]{1,0:T(8,128)(2,1)S(1)}, u32[]{:S(2)}, u32[]{:S(2)}) collective-permute-start(bf16[40,3584]{1,0:T(8,128)(2,1)S(1)} %add_convert_fusion.2), channel_id=1, source_target_pairs={{0,3},{1,0},{2,1},{3,2},{4,7},{5,4},{6,5},{7,6},{8,11},{9,8},{10,9... | collective-permute-start | bytes 860168 | tf_op jit(solution)/shard_map/front_sum/ppermute | solution.py:22
  55.7 45.5 %collective-permute-start.15 = (bf16[1792,512]{1,0:T(8,128)(2,1)S(1)}, bf16[1792,512]{1,0:T(8,128)(2,1)}, u32[]{:S(2)}, u32[]{:S(2)}) collective-permute-start(bf16[1792,512]{1,0:T(8,128)(2,1)S(1)} %bitcast.31), channel_id=1, source_target_pairs={{0,32},{32,0},{1,33},{33,1},{2,34},{34,2},{3,35},{35,3},{4,36},{36... | collective-permute-start | bytes 5505032 | tf_op jit(solution)/shard_map/weight_swap/ppermute | solution.py:456
  55.8 45.4 %collective-permute-start.16 = (bf16[1792,512]{1,0:T(8,128)(2,1)}, bf16[1792,512]{1,0:T(8,128)(2,1)}, u32[]{:S(2)}, u32[]{:S(2)}) collective-permute-start(bf16[1792,512]{1,0:T(8,128)(2,1)} %bitcast.33), channel_id=1, source_target_pairs={{0,32},{32,0},{1,33},{33,1},{2,34},{34,2},{3,35},{35,3},{4,36},{36... | collective-permute-start | bytes 5505032 | tf_op jit(solution)/shard_map/weight_swap/ppermute | solution.py:457
  56.3 24.6 %all-to-all-start = ((bf16[16,8,3584]{2,1,0:T(8,128)(2,1)}), bf16[16,8,3584]{2,1,0:T(8,128)(2,1)S(1)}, u32[]{:S(2)}, u32[]{:S(2)}) async-start(bf16[16,8,3584]{2,1,0:T(8,128)(2,1)} %bitcast.35), calls=%async_computation | async-start | bytes 1835008 | tf_op jit(solution)/shard_map/rows_out/all_to_all | solution.py:483
  64.3 102.4 %reduce-scatter.12.cloned.1.call-start = ((), (), s32[]{:S(2)}) async-start(), calls=%async_computation.7 | async-start | bytes 2365440
  68.6 35.6 %copy-start.18 = (s32[4]{0:T(128)S(1)}, s32[4]{0:T(128)}, u32[]{:S(2)}) copy-start(s32[4]{0:T(128)} %pad_add_fusion.1.where_ref) | copy-start | bytes 52
  81.2 9.0 %collective-permute-start.9 = (bf16[80,1792]{1,0:T(8,128)(2,1)S(1)}, bf16[80,1792]{1,0:T(8,128)(2,1)S(1)}, u32[]{:S(2)}, u32[]{:S(2)}) collective-permute-start(bf16[80,1792]{1,0:T(8,128)(2,1)S(1)} %get-tuple-element.88.a0), channel_id=1, source_target_pairs={{0,1},{1,2},{2,3},{3,0},{4,5},{5,6},{6,7},{7,4},{8,9},{9,10},{10,1... | collective-permute-start | bytes 860168 | tf_op jit(solution)/shard_map/rows_out/ppermute | solution.py:22
  81.3 10.8 %collective-permute-start.11 = (bf16[80,1792]{1,0:T(8,128)(2,1)S(1)}, bf16[80,1792]{1,0:T(8,128)(2,1)S(1)}, u32[]{:S(2)}, u32[]{:S(2)}) collective-permute-start(bf16[80,1792]{1,0:T(8,128)(2,1)S(1)} %get-tuple-element.88.a0), channel_id=1, source_target_pairs={{0,3},{1,0},{2,1},{3,2},{4,7},{5,4},{6,5},{7,6},{8,11},{9,8},{10,9... | collective-permute-start | bytes 860168 | tf_op jit(solution)/shard_map/rows_out/ppermute | solution.py:22
  84.7 11.0 %collective-permute-start.13 = (bf16[80,1792]{1,0:T(8,128)(2,1)S(1)}, bf16[80,1792]{1,0:T(8,128)(2,1)S(1)}, u32[]{:S(2)}, u32[]{:S(2)}) collective-permute-start(bf16[80,1792]{1,0:T(8,128)(2,1)S(1)} %get-tuple-element.89.b0), channel_id=1, source_target_pairs={{0,3},{1,0},{2,1},{3,2},{4,7},{5,4},{6,5},{7,6},{8,11},{9,8},{10,9... | collective-permute-start | bytes 860168 | tf_op jit(solution)/shard_map/rows_out/ppermute | solution.py:22
  90.2 11.0 %collective-permute-start.12 = (bf16[80,1792]{1,0:T(8,128)(2,1)S(1)}, bf16[80,1792]{1,0:T(8,128)(2,1)S(1)}, u32[]{:S(2)}, u32[]{:S(2)}) collective-permute-start(bf16[80,1792]{1,0:T(8,128)(2,1)S(1)} %get-tuple-element.89.b0), channel_id=1, source_target_pairs={{0,1},{1,2},{2,3},{3,0},{4,5},{5,6},{6,7},{7,4},{8,9},{9,10},{10,1... | collective-permute-start | bytes 860168 | tf_op jit(solution)/shard_map/rows_out/ppermute | solution.py:22
  92.0 12.2 %collective-permute-start.10 = (bf16[80,1792]{1,0:T(8,128)(2,1)S(1)}, bf16[80,1792]{1,0:T(8,128)(2,1)S(1)}, u32[]{:S(2)}, u32[]{:S(2)}) collective-permute-start(bf16[80,1792]{1,0:T(8,128)(2,1)S(1)} %collective-permute-done.9.a1), channel_id=1, source_target_pairs={{0,1},{1,2},{2,3},{3,0},{4,5},{5,6},{6,7},{7,4},{8,9},{9,10},{10,1... | collective-permute-start | bytes 860168 | tf_op jit(solution)/shard_map/rows_out/ppermute | solution.py:22
  95.7 8.5 %collective-permute-start.14 = (bf16[80,1792]{1,0:T(8,128)(2,1)S(1)}, bf16[80,1792]{1,0:T(8,128)(2,1)S(1)}, u32[]{:S(2)}, u32[]{:S(2)}) collective-permute-start(bf16[80,1792]{1,0:T(8,128)(2,1)S(1)} %collective-permute-done.13.b3), channel_id=1, source_target_pairs={{0,3},{1,0},{2,1},{3,2},{4,7},{5,4},{6,5},{7,6},{8,11},{9,8},{10,9... | collective-permute-start | bytes 860168 | tf_op jit(solution)/shard_map/rows_out/ppermute | solution.py:22
  104.3 1.5 copy-start.3
  111.1 1.5 copy-start.22
  111.1 75.9 %reduce-scatter.10.cloned.1.call-start = ((), (), s32[]{:S(2)}) async-start(), calls=%async_computation.6 | async-start | bytes 2365440
  112.6 13.0 %collective-permute-start.19 = (bf16[512,1792]{1,0:T(8,128)(2,1)S(1)}, bf16[512,1792]{1,0:T(8,128)(2,1)S(1)}, u32[]{:S(2)}, u32[]{:S(2)}) collective-permute-start(bf16[512,1792]{1,0:T(8,128)(2,1)S(1)} %bitcast.42), channel_id=1, source_target_pairs={{0,32},{32,0},{1,33},{33,1},{2,34},{34,2},{3,35},{35,3},{4,36},{36... | collective-permute-start | bytes 5505032 | tf_op jit(solution)/shard_map/weight_swap/ppermute | solution.py:458
  112.6 11.8 %collective-permute-start.17 = (bf16[160,1024]{1,0:T(8,128)(2,1)}, bf16[160,1024]{1,0:T(8,128)(2,1)S(1)}, u32[]{:S(2)}, u32[]{:S(2)}) collective-permute-start(bf16[160,1024]{1,0:T(8,128)(2,1)} %copy-done.23), channel_id=1, source_target_pairs={{0,64},{64,0},{1,65},{65,1},{2,66},{66,2},{3,67},{67,3},{4,68},{68... | collective-permute-start | bytes 983048 | tf_op jit(solution)/shard_map/gate_up/ppermute | solution.py:489
  124.6 7.4 %collective-permute-start.18 = (bf16[160,512]{1,0:T(8,128)(2,1)S(1)}, bf16[160,512]{1,0:T(8,128)(2,1)S(1)}, u32[]{:S(2)}, u32[]{:S(2)}) collective-permute-start(bf16[160,512]{1,0:T(8,128)(2,1)S(1)} %fusion.1.mine), channel_id=1, source_target_pairs={{0,64},{64,0},{1,65},{65,1},{2,66},{66,2},{3,67},{67,3},{4,68},{68... | collective-permute-start | bytes 491528 | tf_op jit(solution)/shard_map/gate_up/ppermute | solution.py:491
  134.1 11.0 %collective-permute-start.20 = (bf16[80,1792]{1,0:T(8,128)(2,1)S(1)}, bf16[80,1792]{1,0:T(8,128)(2,1)S(1)}, u32[]{:S(2)}, u32[]{:S(2)}) collective-permute-start(bf16[80,1792]{1,0:T(8,128)(2,1)S(1)} %get-tuple-element.97), channel_id=1, source_target_pairs={{0,1},{1,2},{2,3},{3,0},{4,5},{5,6},{6,7},{7,4},{8,9},{9,10},{10,1... | collective-permute-start | bytes 860168 | tf_op jit(solution)/shard_map/rows_back/ppermute | solution.py:22
  134.2 18.2 %collective-permute-start.22 = (bf16[80,1792]{1,0:T(8,128)(2,1)S(1)}, bf16[80,1792]{1,0:T(8,128)(2,1)S(1)}, u32[]{:S(2)}, u32[]{:S(2)}) collective-permute-start(bf16[80,1792]{1,0:T(8,128)(2,1)S(1)} %get-tuple-element.98), channel_id=1, source_target_pairs={{0,1},{1,2},{2,3},{3,0},{4,5},{5,6},{6,7},{7,4},{8,9},{9,10},{10,1... | collective-permute-start | bytes 860168 | tf_op jit(solution)/shard_map/rows_back/ppermute | solution.py:22
  135.8 16.6 %collective-permute-start.23 = (bf16[80,1792]{1,0:T(8,128)(2,1)S(1)}, bf16[80,1792]{1,0:T(8,128)(2,1)S(1)}, u32[]{:S(2)}, u32[]{:S(2)}) collective-permute-start(bf16[80,1792]{1,0:T(8,128)(2,1)S(1)} %get-tuple-element.99), channel_id=1, source_target_pairs={{0,3},{1,0},{2,1},{3,2},{4,7},{5,4},{6,5},{7,6},{8,11},{9,8},{10,9... | collective-permute-start | bytes 860168 | tf_op jit(solution)/shard_map/rows_back/ppermute | solution.py:22
  137.5 12.5 %collective-permute-start.24 = (bf16[80,1792]{1,0:T(8,128)(2,1)S(1)}, bf16[80,1792]{1,0:T(8,128)(2,1)S(1)}, u32[]{:S(2)}, u32[]{:S(2)}) collective-permute-start(bf16[80,1792]{1,0:T(8,128)(2,1)S(1)} %get-tuple-element.101), channel_id=1, source_target_pairs={{0,3},{1,0},{2,1},{3,2},{4,7},{5,4},{6,5},{7,6},{8,11},{9,8},{10,9... | collective-permute-start | bytes 860168 | tf_op jit(solution)/shard_map/rows_back/ppermute | solution.py:22
  145.2 10.1 %collective-permute-start.21 = (bf16[80,1792]{1,0:T(8,128)(2,1)S(1)}, bf16[80,1792]{1,0:T(8,128)(2,1)S(1)}, u32[]{:S(2)}, u32[]{:S(2)}) collective-permute-start(bf16[80,1792]{1,0:T(8,128)(2,1)S(1)} %add_convert_fusion.1), channel_id=1, source_target_pairs={{0,1},{1,2},{2,3},{3,0},{4,5},{5,6},{6,7},{7,4},{8,9},{9,10},{10,1... | collective-permute-start | bytes 860168 | tf_op jit(solution)/shard_map/rows_back/ppermute | solution.py:22
  150.1 6.7 %collective-permute-start.25 = (bf16[80,1792]{1,0:T(8,128)(2,1)S(1)}, bf16[80,1792]{1,0:T(8,128)(2,1)S(1)}, u32[]{:S(2)}, u32[]{:S(2)}) collective-permute-start(bf16[80,1792]{1,0:T(8,128)(2,1)S(1)} %add_convert_fusion), channel_id=1, source_target_pairs={{0,3},{1,0},{2,1},{3,2},{4,7},{5,4},{6,5},{7,6},{8,11},{9,8},{10,9... | collective-permute-start | bytes 860168 | tf_op jit(solution)/shard_map/rows_back/ppermute | solution.py:22
  158.2 5.8 %copy-start = (bf16[128,7168]{1,0:T(8,128)(2,1)S(1)}, bf16[128,7168]{1,0:T(8,128)(2,1)}, u32[]{:S(2)}) copy-start(bf16[128,7168]{1,0:T(8,128)(2,1)} %residual.5) | copy-start | bytes 5505028
  158.2 5.8 %copy-start.13 = (s32[4,128]{1,0:T(4,128)S(1)}, s32[4,128]{1,0:T(4,128)}, u32[]{:S(2)}) copy-start(s32[4,128]{1,0:T(4,128)} %pad_add_fusion.poses.pos) | copy-start | bytes 6148
  158.2 19.6 %all-to-all-start.1 = ((bf16[16,8,3584]{2,1,0:T(8,128)(2,1)}), bf16[16,8,3584]{2,1,0:T(8,128)(2,1)S(1)}, u32[]{:S(2)}, u32[]{:S(2)}) async-start(bf16[16,8,3584]{2,1,0:T(8,128)(2,1)} %bitcast.18), calls=%async_computation.1 | async-start | bytes 1835008 | tf_op jit(solution)/shard_map/rows_back/all_to_all | solution.py:496
  164.0 1.0 copy-start.7
  166.7 1.1 copy-start.5
  167.7 10.1 %copy-start.14 = (bf16[64,128]{1,0:T(8,128)(2,1)S(1)}, bf16[64,128]{1,0:T(8,128)(2,1)}, u32[]{:S(2)}) copy-start(bf16[64,128]{1,0:T(8,128)(2,1)} %convert_element_type.60.high) | copy-start | bytes 49156
  167.7 10.1 %copy-start.15 = (bf16[64,128]{1,0:T(8,128)(2,1)S(1)}, bf16[64,128]{1,0:T(8,128)(2,1)}, u32[]{:S(2)}) copy-start(bf16[64,128]{1,0:T(8,128)(2,1)} %convert_element_type.61.low) | copy-start | bytes 49156
  187.0 1.0 copy-start.6
  (10 other events, 7.8 us)
Sparse Core Ops, SparseCore 0:
  55.8 27.0 reduce-scatter.7
  111.2 26.0 reduce-scatter.11
  158.3 28.6 reduce-scatter.9

commit v3 on v2

--- a/solution.py
+++ b/solution.py
@@ -12,10 +12,9 @@
 SWAP = [(0, 1), (1, 0)]
 TILE = 896
 SEAT = 8
-PIECES = (2, 3, 3)
+PIECES = (3, 3, 2)
 F32, BF = jnp.float32, jnp.bfloat16
 VMEM_LIMIT = 14 * 1024 * 1024
-VMEM_ALL = 57 * 1024 * 1024
 
 
 def shift(value, steps):
@@ -56,109 +55,95 @@
     return (index == pos).astype(BF)
 
 
-def fetch(source, target, sem):
-    copy = pltpu.make_async_copy(source, target, sem)
-    copy.start()
-    return copy
+def block_of(where_ref, distance, count):
+    block = lax.rem(where_ref[0] + distance, RING)
+    return block, pl.ds(pl.multiple_of(block * count, count), count)
+
+
+def load(attn, after):
+    def kernel(attn, after, out, sem):
+        copy = pltpu.make_async_copy(attn, out, sem)
+        copy.start()
+        copy.wait()
+
+    return pl.pallas_call(
+        kernel,
+        in_specs=[pl.BlockSpec(memory_space=pl.ANY), pl.BlockSpec(memory_space=pl.ANY)],
+        out_specs=pl.BlockSpec(memory_space=pltpu.VMEM),
+        out_shape=jax.ShapeDtypeStruct(attn.shape, BF),
+        scratch_shapes=[pltpu.SemaphoreType.DMA(())],
+        compiler_params=params(),
+        cost_estimate=cost(0, 4 * attn.size),
+        name="load",
+    )(attn, after)
 
 
 def select_rows(where, attn, poses, rows, distances):
     count = poses.shape[1]
-    width = attn.shape[1]
-    number = len(distances)
-    half = width // 2
-
-    def kernel(where_ref, attn_ref, poses, *refs):
-        held, sems = refs[-2:]
-        copies = []
-        for n, k in enumerate(distances):
-            block = pl.multiple_of(lax.rem(where_ref[0] + k, RING) * count, count)
-            for c in range(2):
-                at = pl.ds(c * half, half)
-                copies.append(
-                    fetch(attn_ref.at[pl.ds(block, count), at], held.at[n, :, at], sems.at[n, c])
-                )
+    half = attn.shape[1] // 2
+    number = 2 * len(distances)
+
+    def kernel(where_ref, attn, poses, *outs):
         for n, k in enumerate(distances):
             pick = onehot(0, rows, poses[k : k + 1, :])
+            _, at = block_of(where_ref, k, count)
             for c in range(2):
-                copies[2 * n + c].wait()
-                at = slice(c * half, (c + 1) * half)
-                refs[2 * n + c][...] = dot(pick, held[n, :, at]).astype(BF)
-
-    vmem = pl.BlockSpec(memory_space=pltpu.VMEM)
-    return pl.pallas_call(
-        kernel,
-        in_specs=[pl.BlockSpec(memory_space=pltpu.SMEM), pl.BlockSpec(memory_space=pl.ANY), vmem],
-        out_specs=[vmem] * (2 * number),
-        out_shape=[jax.ShapeDtypeStruct((rows, half), BF)] * (2 * number),
-        scratch_shapes=[
-            pltpu.VMEM((number, count, width), BF),
-            pltpu.SemaphoreType.DMA((number, 2)),
-        ],
-        compiler_params=params(VMEM_ALL),
-        cost_estimate=cost(2 * number * rows * count * width, 4 * number * count * width),
+                outs[2 * n + c][...] = dot(pick, attn[at, c * half : (c + 1) * half]).astype(BF)
+
+    vmem = pl.BlockSpec(memory_space=pltpu.VMEM)
+    return pl.pallas_call(
+        kernel,
+        in_specs=[pl.BlockSpec(memory_space=pltpu.SMEM), vmem, vmem],
+        out_specs=[vmem] * number,
+        out_shape=[jax.ShapeDtypeStruct((rows, half), BF)] * number,
+        compiler_params=params(),
+        cost_estimate=cost(2 * number * rows * count * half, 2 * number * count * half),
         name="select_rows",
     )(where, attn, poses)
 
 
 def own_rows(where, attn, residual, pos, rows):
-    count = pos.shape[1]
-    width = attn.shape[1]
-    quarter = width // 4
-
-    def kernel(where_ref, attn_ref, residual_ref, pos, out, held, sems):
-        block = pl.multiple_of(where_ref[0] * count, count)
-        copies = []
-        for c in range(4):
-            at = pl.ds(c * quarter, quarter)
-            copies.append(fetch(attn_ref.at[pl.ds(block, count), at], held.at[0, :, at], sems.at[0, c]))
-            copies.append(fetch(residual_ref.at[:, at], held.at[1, :, at], sems.at[1, c]))
+    count, width = residual.shape
+
+    def kernel(where_ref, attn, residual, pos, out):
         pick = onehot(0, rows, pos[:1, :])
-        for c in range(4):
-            at = slice(c * quarter, (c + 1) * quarter)
-            copies[2 * c].wait()
-            copies[2 * c + 1].wait()
-            out[:, at] = dot(pick, held[0, :, at]) + dot(pick, held[1, :, at])
-
-    vmem = pl.BlockSpec(memory_space=pltpu.VMEM)
-    hbm = pl.BlockSpec(memory_space=pl.ANY)
-    return pl.pallas_call(
-        kernel,
-        in_specs=[pl.BlockSpec(memory_space=pltpu.SMEM), hbm, hbm, vmem],
+        _, at = block_of(where_ref, 0, count)
+        out[...] = dot(pick, attn[at, :]) + dot(pick, residual[...])
+
+    vmem = pl.BlockSpec(memory_space=pltpu.VMEM)
+    return pl.pallas_call(
+        kernel,
+        in_specs=[pl.BlockSpec(memory_space=pltpu.SMEM), vmem, vmem, vmem],
         out_specs=vmem,
         out_shape=jax.ShapeDtypeStruct((rows, width), F32),
-        scratch_shapes=[pltpu.VMEM((2, count, width), BF), pltpu.SemaphoreType.DMA((2, 4))],
-        compiler_params=params(VMEM_ALL),
+        compiler_params=params(),
         cost_estimate=cost(4 * rows * count * width, 4 * count * width + 4 * rows * width),
         name="own_rows",
     )(where, attn, residual, pos)
 
 
-def back_rows(where, attn, poses, first, left, width):
+def back_rows(where, attn, poses, first, left, widths):
     count = poses.shape[1]
     rows = count - first
 
-    def kernel(where_ref, attn_ref, poses, out, held, sems):
-        blocks, copies = [], []
+    def kernel(where_ref, attn, poses, *outs):
         for k in range(RING):
-            blocks.append(lax.rem(where_ref[0] + k, RING))
-            at = pl.multiple_of(blocks[k] * count, count)
-            copies.append(
-                fetch(attn_ref.at[pl.ds(at, count), pl.ds(left, width)], held.at[k], sems.at[k])
-            )
-        for k in range(RING):
-            copies[k].wait()
-            out[blocks[k]] = dot(onehot(first, rows, poses[k : k + 1, :]), held[k]).astype(BF)
-
-    vmem = pl.BlockSpec(memory_space=pltpu.VMEM)
-    return pl.pallas_call(
-        kernel,
-        in_specs=[pl.BlockSpec(memory_space=pltpu.SMEM), pl.BlockSpec(memory_space=pl.ANY), vmem],
-        out_specs=vmem,
-        out_shape=jax.ShapeDtypeStruct((RING, rows, width), BF),
-        scratch_shapes=[pltpu.VMEM((RING, count, width), BF), pltpu.SemaphoreType.DMA((RING,))],
-        compiler_params=params(VMEM_ALL),
-        cost_estimate=cost(8 * rows * count * width, 8 * count * width + 8 * rows * width),
+            block, at = block_of(where_ref, k, count)
+            pick = onehot(first, rows, poses[k : k + 1, :])
+            start = left
+            for out, width in zip(outs, widths):
+                out[block] = dot(pick, attn[at, start : start + width]).astype(BF)
+                start += width
+
+    vmem = pl.BlockSpec(memory_space=pltpu.VMEM)
+    wide = sum(widths)
+    return pl.pallas_call(
+        kernel,
+        in_specs=[pl.BlockSpec(memory_space=pltpu.SMEM), vmem, vmem],
+        out_specs=[vmem] * len(widths),
+        out_shape=[jax.ShapeDtypeStruct((RING, rows, width), BF) for width in widths],
+        compiler_params=params(),
+        cost_estimate=cost(8 * rows * count * wide, 8 * count * wide + 8 * rows * wide),
         name="back_rows",
     )(where, attn, poses)
 
@@ -210,15 +195,12 @@
 
     half = width // 2
 
-    def kernel(where_ref, base, r0, r1, r2, r3, gain, pos, placing, front, out, held, came, sems):
-        copies = [fetch(r, came.at[n], sems.at[n]) for n, r in enumerate((r0, r1, r2, r3))]
+    def kernel(where_ref, base, r0, r1, r2, r3, gain, pos, placing, front, out, held):
         pick = onehot(0, rows, pos[:1, :])
         square = jnp.zeros((rows, 1), F32)
-        for n in range(2):
-            copies[n].wait()
-            copies[n + 2].wait()
+        for n, (a, b) in enumerate(((r0, r2), (r1, r3))):
             at = slice(n * half, (n + 1) * half)
-            total = base[:, at] + came[n].astype(F32) + came[n + 2].astype(F32)
+            total = base[:, at] + a[...].astype(F32) + b[...].astype(F32)
             rounded = total.astype(BF)
             front[:, at] = rounded
             total = rounded.astype(F32)
@@ -237,19 +219,13 @@
     vmem = pl.BlockSpec(memory_space=pltpu.VMEM)
     return pl.pallas_call(
         kernel,
-        in_specs=[pl.BlockSpec(memory_space=pltpu.SMEM), vmem]
-        + [pl.BlockSpec(memory_space=pl.ANY)] * 4
-        + [vmem] * 3,
+        in_specs=[pl.BlockSpec(memory_space=pltpu.SMEM)] + [vmem] * 8,
         out_specs=[vmem] * 2,
         out_shape=[
             jax.ShapeDtypeStruct((rows, width), BF),
             jax.ShapeDtypeStruct((2 * seats, width // 2), BF),
         ],
-        scratch_shapes=[
-            pltpu.VMEM((rows, width), BF),
-            pltpu.VMEM((4, rows, half), BF),
-            pltpu.SemaphoreType.DMA((4,)),
-        ],
+        scratch_shapes=[pltpu.VMEM((rows, width), BF)],
         compiler_params=params(),
         cost_estimate=cost(2 * seats * rows * width, 20 * rows * width),
         name="dispatch",
@@ -448,61 +424,63 @@
         tri = (token[:, None] >= token[None, :]).astype(BF)
         ahead = dot(tri, anyone[:, None].astype(BF)).astype(jnp.int32)[:, 0]
         pos = jnp.where(anyone, ahead - 1, ahead[-1] + token - ahead).reshape(1, count)
-        base = own_rows(where, attn, residual, pos, FRONT)
+        attn = load(attn, pos)
         poses = jnp.concatenate([pos] + [shift(pos, -k) for k in (1, 2, 3)], axis=0)
-        poses, base = barrier((poses, base))
 
     with jax.named_scope("weight_swap"):
         wg2 = lax.ppermute(wg, "core", SWAP)
         wu2 = lax.ppermute(wu, "core", SWAP)
         wd2 = lax.ppermute(wd, "core", SWAP)
 
+    back, summed = [], {}
+
+    def head_sum(n, after):
+        operand, after = barrier((back[n], after))
+        with jax.named_scope("head_sum"):
+            summed[n] = lax.psum_scatter(operand, "x", scatter_dimension=0, tiled=True)[0]
+        return after
+
     with jax.named_scope("front_sum"):
+        attn, poses = barrier((attn, poses))
         far = select_rows(where, attn, poses, FRONT, (2,))
         far, poses = barrier((far, poses))
         near = select_rows(where, attn, poses, FRONT, (1, 3))
         near, poses, ids, gates = barrier((near, poses, expert_ids.T, gate_vals.T))
-        back = [back_rows(where, attn, poses, FRONT, 0, PIECES[0] * TILE)]
+        pieces = [tiles * TILE for tiles in PIECES]
+        back += back_rows(where, attn, poses, FRONT, 0, pieces[:1])
         seats = find_seats(ids, gates)
-        behind, ahead, (back, seats) = ring_sum(far, near[:2], near[2:], (back, seats))
+        base = own_rows(where, attn, residual, poses, FRONT)
+        beside = (back[0], seats, wg2, wu2, wd2)
+        behind, ahead, (_, seats, wg2, wu2, wd2) = ring_sum(far, near[:2], near[2:], beside)
         placing, high, low = seats
-    def head_sum(n, after):
-        operand, after = barrier((back[n], after))
-        with jax.named_scope("head_sum"):
-            summed = lax.psum_scatter(operand, "x", scatter_dimension=0, tiled=True)
-        return summed[0], after
-
     with jax.named_scope("rows_out"):
+        behind, ahead = head_sum(0, (behind, ahead))
         front, message = dispatch(where, base, (*behind, *ahead), gain, poses, placing)
-        summed0, message = head_sum(0, message)
         late_poses, message = barrier((poses, message))
-        left = PIECES[0] * TILE
-        for tiles in PIECES[1:]:
-            back.append(back_rows(where, attn, late_poses, FRONT, left, tiles * TILE))
-            left += tiles * TILE
+        back += back_rows(where, attn, late_poses, FRONT, pieces[0], pieces[1:])
         whole = lax.all_to_all(message, grid, split_axis=0, concat_axis=0, tiled=True)
-        whole, back = barrier((whole, back))
+        whole, back[1:] = barrier((whole, back[1:]))
         rows = ring_gather(*pack(whole))
     with jax.named_scope("gate_up"):
+        rows = head_sum(1, rows)
         mine, away = gate_up(where, rows, wg, wg2, wu, wu2)
-        summed1, away = head_sum(1, away)
         mine = mine + lax.ppermute(away, "zh", SWAP).astype(F32)
         middle = (jax.nn.silu(mine[:, :ff]) * mine[:, ff:]).astype(BF)
         other = lax.ppermute(middle, "zh", SWAP)
     with jax.named_scope("rows_back"):
         outs = down(where, middle, other, wd, wd2)
-        total = add_parts(outs[:2], *ring_sum(outs[4:6], outs[6:8], outs[2:4])[:2])
-        summed2, total = head_sum(2, total)
+        came = head_sum(2, ring_sum(outs[4:6], outs[6:8], outs[2:4])[:2])
+        total = add_parts(outs[:2], *came)
         returned = lax.all_to_all(total, grid, split_axis=0, concat_axis=0, tiled=True)
     with jax.named_scope("hidden"):
-        hidden, left = None, 0
-        for tiles, summed in zip(PIECES, (summed0, summed1, summed2)):
-            if left + tiles * TILE == width:
-                returned, hidden = barrier((returned, hidden))
-            hidden = finish_hidden(where, front, residual, summed, poses, left, hidden)
-            left += tiles * TILE
+        hidden = finish_hidden(where, front, residual, summed[0], poses, 0)
+        hidden = finish_hidden(where, front, residual, summed[1], poses, pieces[0], hidden)
+        returned, hidden = barrier((returned, hidden))
     with jax.named_scope("mix"):
         moe_out = mix(where, returned, high, low)
+    with jax.named_scope("hidden"):
+        moe_out, hidden = barrier((moe_out, hidden))
+        hidden = finish_hidden(where, front, residual, summed[2], poses, sum(pieces[:2]), hidden)
     return hidden, moe_out
 
 

time: 199 us -> 182 us (0.915)
  local copies, waits for them, and re-layouts: 14.4 us -> 32.7 us
  Pallas kernels: 42.9 us -> 27.4 us
  waiting for transfers between devices: 69.2 us -> 55.3 us
  starting transfers between devices: 50.7 us -> 47.3 us
    unnamed x54 -> x96, local copies, waits for them, and re-layouts: 13.8 us -> 32.1 us
    pallas_call x7, Pallas kernels: 25 us -> 8.55 us  [the longest x2 2.86 us: back_rows(): pl.pallas_call(kernel, in_specs=[pl.BlockSpec(memory_space=pltpu.SMEM), v...]
    unnamed x5, waiting for transfers between devices: 6.26 us -> 0.07 us
    ppermute x21, starting transfers between devices: 34.4 us -> 31.8 us  [shift(): lax.ppermute(value, 'x', [(j, (j + steps) % RING) for j in range(RING)])]
    ppermute x1, waiting for transfers between devices: 11 us -> 8.62 us  [local(): mine = mine + lax.ppermute(away, 'zh', SWAP).astype(F32)]
    all_to_all x1, waiting for transfers between devices: 7.75 us -> 5.66 us  [local(): lax.all_to_all(total, grid, split_axis=0, concat_axis=0, tiled=True)]
  transfers between devices with their start and end apart: 31 -> 31, of which waited for: 15 -> 17; matrix products, arithmetic and copies ran while one was open for 1% -> 2% of each run, Pallas kernels for 18% -> 14%
where the time goes in v3:
time: 182 us; the launch traced here: 181 us
  waiting for transfers between devices  55.3 us (30%)
  starting transfers between devices  47.3 us (26%)
  local copies, waits for them, and re-layouts  32.7 us (18%)
  Pallas kernels  27.4 us (15%)
  between operations  14.2 us (8%)
  other arithmetic  3.74 us (2%)
    unnamed x96, local copies, waits for them, and re-layouts  32.1 us
    ppermute x21, starting transfers between devices, shift(): lax.ppermute(value, 'x', [(j, (j + steps) % RING) for j in range(RING)])  31.8 us
    ppermute x21, waiting for transfers between devices, shift(): lax.ppermute(value, 'x', [(j, (j + steps) % RING) for j in range(RING)])  28.6 us
    ppermute x1, waiting for transfers between devices, local(): mine = mine + lax.ppermute(away, 'zh', SWAP).astype(F32)  8.62 us
    all_to_all x1, starting transfers between devices, local(): lax.all_to_all(message, grid, split_axis=0, concat_axis=0, tiled=True)  8.18 us
    all_to_all x1, waiting for transfers between devices, local(): lax.all_to_all(message, grid, split_axis=0, concat_axis=0, tiled=True)  6.7 us
    pallas_call x3, Pallas kernels, finish_hidden(): pl.pallas_call(kernel, grid=(wide // TILE,), in_specs=in_specs, out_specs...  6.47 us
    all_to_all x1, waiting for transfers between devices, local(): lax.all_to_all(total, grid, split_axis=0, concat_axis=0, tiled=True)  5.66 us
  transfers between devices with their start and end apart: 31, of which 17 were waited for; matrix products, arithmetic and copies ran while one was open for 2% of the time, Pallas kernels for 14%

profile of v3, /device:TPU:0, one launch (start us, length us, event | category | flops | bytes accessed | tf_op | source)
XLA Modules:
  0.0 180.7 jit_solution(12442905309295975121)
XLA Ops:
  10.0 2.9 %collective-permute-start = (s32[1,128]{1,0:T(1,128)S(1)}, s32[1,128]{1,0:T(1,128)S(1)}, u32[]{:S(2)}, u32[]{:S(2)}) collective-permute-start(s32[1,128]{1,0:T(1,128)S(1)} %select_bitcast_fusion.after), channel_id=1, source_target_pairs={{0,3},{1,0},{2,1},{3,2},{4,7},{5,4},{6,5},{7,6},{8,11},{9,8},{10,9... | collective-permute-start | bytes 1544 | tf_op jit(solution)/shard_map/routing/ppermute | solution.py:21
  15.3 3.1 %copy-done.5 = bf16[1,512,7168]{2,1,0:T(8,128)(2,1)S(1)} copy-done((bf16[1,512,7168]{2,1,0:T(8,128)(2,1)S(1)}, bf16[1,512,7168]{2,1,0:T(8,128)(2,1)}, u32[]{:S(2)}) %copy-start.5) | copy-done | bytes 7340056
  20.2 1.3 collective-permute-start.3
  21.5 2.0 %collective-permute-start.4 = (bf16[40,3584]{1,0:T(8,128)(2,1)S(1)}, bf16[40,3584]{1,0:T(8,128)(2,1)S(1)}, u32[]{:S(2)}, u32[]{:S(2)}) collective-permute-start(bf16[40,3584]{1,0:T(8,128)(2,1)S(1)} %get-tuple-element.87), channel_id=1, source_target_pairs={{0,3},{1,0},{2,1},{3,2},{4,7},{5,4},{6,5},{7,6},{8,11},{9,8},{10,9... | collective-permute-start | bytes 860168 | tf_op jit(solution)/shard_map/front_sum/ppermute | solution.py:21
  23.5 1.8 select_rows.3
  27.2 1.2 back_rows.2
  28.5 1.3 copy-done.4
  29.8 1.1 collective-permute-start.10
  31.9 2.4 %collective-permute-start.11 = (bf16[40,3584]{1,0:T(8,128)(2,1)S(1)}, bf16[40,3584]{1,0:T(8,128)(2,1)S(1)}, u32[]{:S(2)}, u32[]{:S(2)}) collective-permute-start(bf16[40,3584]{1,0:T(8,128)(2,1)S(1)} %add_convert_fusion.2), channel_id=1, source_target_pairs={{0,3},{1,0},{2,1},{3,2},{4,7},{5,4},{6,5},{7,6},{8,11},{9,8},{10,9... | collective-permute-start | bytes 860168 | tf_op jit(solution)/shard_map/front_sum/ppermute | solution.py:21
  34.5 5.3 %collective-permute-done.10.r2 = bf16[40,3584]{1,0:T(8,128)(2,1)S(1)} collective-permute-done((bf16[40,3584]{1,0:T(8,128)(2,1)}, bf16[40,3584]{1,0:T(8,128)(2,1)S(1)}, u32[]{:S(2)}, u32[]{:S(2)}) %collective-permute-start.10) | collective-permute-done | bytes 286752 | tf_op jit(solution)/shard_map/front_sum/ppermute | solution.py:21
  39.8 2.3 %collective-permute-done.9.r1 = bf16[40,3584]{1,0:T(8,128)(2,1)S(1)} collective-permute-done((bf16[40,3584]{1,0:T(8,128)(2,1)}, bf16[40,3584]{1,0:T(8,128)(2,1)S(1)}, u32[]{:S(2)}, u32[]{:S(2)}) %collective-permute-start.9) | collective-permute-done | bytes 286752 | tf_op jit(solution)/shard_map/front_sum/ppermute | solution.py:21
  43.1 2.6 %collective-permute-done.8.r0 = bf16[40,3584]{1,0:T(8,128)(2,1)S(1)} collective-permute-done((bf16[40,3584]{1,0:T(8,128)(2,1)S(1)}, bf16[40,3584]{1,0:T(8,128)(2,1)S(1)}, u32[]{:S(2)}, u32[]{:S(2)}) %collective-permute-start.8) | collective-permute-done | bytes 286752 | tf_op jit(solution)/shard_map/front_sum/ppermute | solution.py:21
  45.7 3.1 %copy-done.1 = bf16[512,7168]{1,0:T(8,128)(2,1)S(1)} copy-done((bf16[512,7168]{1,0:T(8,128)(2,1)S(1)}, bf16[512,7168]{1,0:T(8,128)(2,1)}, u32[]{:S(2)}) %copy-start.1) | copy-done | bytes 7340056
  48.8 1.1 own_rows.1.base
  50.0 1.4 dispatch.1
  52.3 8.2 %all-to-all-start = ((bf16[16,8,3584]{2,1,0:T(8,128)(2,1)}), bf16[16,8,3584]{2,1,0:T(8,128)(2,1)S(1)}, u32[]{:S(2)}, u32[]{:S(2)}) async-start(bf16[16,8,3584]{2,1,0:T(8,128)(2,1)} %bitcast.36), calls=%async_computation | async-start | bytes 1835008 | tf_op jit(solution)/shard_map/rows_out/all_to_all | solution.py:461
  60.5 3.1 %copy-done.2 = bf16[512,7168]{1,0:T(8,128)(2,1)S(1)} copy-done((bf16[512,7168]{1,0:T(8,128)(2,1)S(1)}, bf16[512,7168]{1,0:T(8,128)(2,1)}, u32[]{:S(2)}) %copy-start.2) | copy-done | bytes 7340056
  63.7 1.6 back_rows.3
  65.3 1.2 copy-done.6
  67.6 6.7 %all-to-all-done = bf16[16,8,3584]{2,1,0:T(8,128)(2,1)S(1)} async-done(((bf16[16,8,3584]{2,1,0:T(8,128)(2,1)}), bf16[16,8,3584]{2,1,0:T(8,128)(2,1)S(1)}, u32[]{:S(2)}, u32[]{:S(2)}) %all-to-all-start) | async-done | bytes 917536 | tf_op jit(solution)/shard_map/rows_out/all_to_all | solution.py:461
  74.7 3.2 %collective-permute-start.15 = (bf16[80,1792]{1,0:T(8,128)(2,1)S(1)}, bf16[80,1792]{1,0:T(8,128)(2,1)S(1)}, u32[]{:S(2)}, u32[]{:S(2)}) collective-permute-start(bf16[80,1792]{1,0:T(8,128)(2,1)S(1)} %get-tuple-element.118.b0), channel_id=1, source_target_pairs={{0,3},{1,0},{2,1},{3,2},{4,7},{5,4},{6,5},{7,6},{8,11},{9,8},{10,9... | collective-permute-start | bytes 860168 | tf_op jit(solution)/shard_map/rows_out/ppermute | solution.py:21
  78.6 3.2 %collective-permute-start.17 = (bf16[80,1792]{1,0:T(8,128)(2,1)S(1)}, bf16[80,1792]{1,0:T(8,128)(2,1)S(1)}, u32[]{:S(2)}, u32[]{:S(2)}) collective-permute-start(bf16[80,1792]{1,0:T(8,128)(2,1)S(1)} %get-tuple-element.114.a0), channel_id=1, source_target_pairs={{0,3},{1,0},{2,1},{3,2},{4,7},{5,4},{6,5},{7,6},{8,11},{9,8},{10,9... | collective-permute-start | bytes 860168 | tf_op jit(solution)/shard_map/rows_out/ppermute | solution.py:21
  82.6 3.1 %collective-permute-done.12.a1 = bf16[80,1792]{1,0:T(8,128)(2,1)S(1)} collective-permute-done((bf16[80,1792]{1,0:T(8,128)(2,1)S(1)}, bf16[80,1792]{1,0:T(8,128)(2,1)S(1)}, u32[]{:S(2)}, u32[]{:S(2)}) %collective-permute-start.12) | collective-permute-done | bytes 286752 | tf_op jit(solution)/shard_map/rows_out/ppermute | solution.py:21
  85.7 3.2 %collective-permute-start.16 = (bf16[80,1792]{1,0:T(8,128)(2,1)S(1)}, bf16[80,1792]{1,0:T(8,128)(2,1)S(1)}, u32[]{:S(2)}, u32[]{:S(2)}) collective-permute-start(bf16[80,1792]{1,0:T(8,128)(2,1)S(1)} %collective-permute-done.15.b3), channel_id=1, source_target_pairs={{0,3},{1,0},{2,1},{3,2},{4,7},{5,4},{6,5},{7,6},{8,11},{9,8},{10,9... | collective-permute-start | bytes 860168 | tf_op jit(solution)/shard_map/rows_out/ppermute | solution.py:21
  88.9 1.5 collective-permute-done.13.b1
  91.8 1.7 collective-permute-done.14.a2
  95.2 1.5 copy-done.7
  96.7 1.5 copy-done.8
  102.8 4.6 %gate_up.1 = (f32[160,1024]{1,0:T(8,128)S(1)}, bf16[160,1024]{1,0:T(8,128)(2,1)S(1)}) custom-call(s32[4]{0:T(128)S(1)} %copy-done.42, bf16[80,1792]{1,0:T(8,128)(2,1)S(1)} %copy-done.15, bf16[80,1792]{1,0:T(8,128)(2,1)S(1)} %collective-permute-done.12.a1, bf16[80,1792]{1,0:T(8,128)(2,1)S(1)} %copy-done.25, bf16[80,1792]{1,0:T(8,128)(2,1)S(1)} %copy-done.21, ...), custom_call_target="tpu_custom_call" | custom-call | flops 2348810240 | bytes 9633792 | tf_op jit(solution)/shard_map/gate_up/gate_up/pallas_call | solution.py:251
  107.4 1.2 collective-permute-start.18
  108.6 8.6 %collective-permute-done.18 = bf16[160,1024]{1,0:T(8,128)(2,1)S(1)} collective-permute-done((bf16[160,1024]{1,0:T(8,128)(2,1)S(1)}, bf16[160,1024]{1,0:T(8,128)(2,1)S(1)}, u32[]{:S(2)}, u32[]{:S(2)}) %collective-permute-start.18) | collective-permute-done | bytes 327712 | tf_op jit(solution)/shard_map/gate_up/ppermute | solution.py:467
  117.4 1.3 collective-permute-start.19
  118.7 5.6 %collective-permute-done.19.other = bf16[160,512]{1,0:T(8,128)(2,1)S(1)} collective-permute-done((bf16[160,512]{1,0:T(8,128)(2,1)S(1)}, bf16[160,512]{1,0:T(8,128)(2,1)S(1)}, u32[]{:S(2)}, u32[]{:S(2)}) %collective-permute-start.19) | collective-permute-done | bytes 163872 | tf_op jit(solution)/shard_map/gate_up/ppermute | solution.py:469
  124.3 3.0 %down.1 = (bf16[80,1792]{1,0:T(8,128)(2,1)S(1)}, bf16[80,1792]{1,0:T(8,128)(2,1)S(1)}, bf16[80,1792]{1,0:T(8,128)(2,1)S(1)}, bf16[80,1792]{1,0:T(8,128)(2,1)S(1)...) custom-call(s32[4]{0:T(128)S(1)} %copy-done.42, ...), custom_call_target="tpu_custom_call" | custom-call | flops 1174405120 | bytes 5963776 | tf_op jit(solution)/shard_map/rows_back/down/pallas_call | solution.py:282
  127.4 2.5 %collective-permute-start.24 = (bf16[80,1792]{1,0:T(8,128)(2,1)S(1)}, bf16[80,1792]{1,0:T(8,128)(2,1)S(1)}, u32[]{:S(2)}, u32[]{:S(2)}) collective-permute-start(bf16[80,1792]{1,0:T(8,128)(2,1)S(1)} %get-tuple-element.132), channel_id=1, source_target_pairs={{0,3},{1,0},{2,1},{3,2},{4,7},{5,4},{6,5},{7,6},{8,11},{9,8},{10,9... | collective-permute-start | bytes 860168 | tf_op jit(solution)/shard_map/rows_back/ppermute | solution.py:21
  129.9 3.3 %collective-permute-start.23 = (bf16[80,1792]{1,0:T(8,128)(2,1)S(1)}, bf16[80,1792]{1,0:T(8,128)(2,1)S(1)}, u32[]{:S(2)}, u32[]{:S(2)}) collective-permute-start(bf16[80,1792]{1,0:T(8,128)(2,1)S(1)} %get-tuple-element.130), channel_id=1, source_target_pairs={{0,3},{1,0},{2,1},{3,2},{4,7},{5,4},{6,5},{7,6},{8,11},{9,8},{10,9... | collective-permute-start | bytes 860168 | tf_op jit(solution)/shard_map/rows_back/ppermute | solution.py:21
  133.2 3.2 %collective-permute-done.24 = bf16[80,1792]{1,0:T(8,128)(2,1)S(1)} collective-permute-done((bf16[80,1792]{1,0:T(8,128)(2,1)S(1)}, bf16[80,1792]{1,0:T(8,128)(2,1)S(1)}, u32[]{:S(2)}, u32[]{:S(2)}) %collective-permute-start.24) | collective-permute-done | bytes 286752 | tf_op jit(solution)/shard_map/rows_back/ppermute | solution.py:21
  136.5 3.8 %collective-permute-start.25 = (bf16[80,1792]{1,0:T(8,128)(2,1)S(1)}, bf16[80,1792]{1,0:T(8,128)(2,1)S(1)}, u32[]{:S(2)}, u32[]{:S(2)}) collective-permute-start(bf16[80,1792]{1,0:T(8,128)(2,1)S(1)} %add_convert_fusion), channel_id=1, source_target_pairs={{0,3},{1,0},{2,1},{3,2},{4,7},{5,4},{6,5},{7,6},{8,11},{9,8},{10,9... | collective-permute-start | bytes 860168 | tf_op jit(solution)/shard_map/rows_back/ppermute | solution.py:21
  140.4 2.6 %collective-permute-done.22.refs_3_ = bf16[80,1792]{1,0:T(8,128)(2,1)S(1)} collective-permute-done((bf16[80,1792]{1,0:T(8,128)(2,1)S(1)}, bf16[80,1792]{1,0:T(8,128)(2,1)S(1)}, u32[]{:S(2)}, u32[]{:S(2)}) %collective-permute-start.22) | collective-permute-done | bytes 286752 | tf_op jit(solution)/shard_map/rows_back/ppermute | solution.py:21
  143.0 1.4 collective-permute-done.25.refs_5_
  145.1 3.1 %collective-permute-done.21.refs_2_ = bf16[80,1792]{1,0:T(8,128)(2,1)S(1)} collective-permute-done((bf16[80,1792]{1,0:T(8,128)(2,1)S(1)}, bf16[80,1792]{1,0:T(8,128)(2,1)S(1)}, u32[]{:S(2)}, u32[]{:S(2)}) %collective-permute-start.21) | collective-permute-done | bytes 286752 | tf_op jit(solution)/shard_map/rows_back/ppermute | solution.py:21
  150.9 1.4 add_parts.1
  152.3 3.8 %all-to-all-start.1 = ((bf16[16,8,3584]{2,1,0:T(8,128)(2,1)}), bf16[16,8,3584]{2,1,0:T(8,128)(2,1)S(1)}, u32[]{:S(2)}, u32[]{:S(2)}) async-start(bf16[16,8,3584]{2,1,0:T(8,128)(2,1)} %bitcast.18), calls=%async_computation.2 | async-start | bytes 1835008 | tf_op jit(solution)/shard_map/rows_back/all_to_all | solution.py:474
  157.1 2.4 %finish_hidden.3.refs_0_ = bf16[128,7168]{1,0:T(8,128)(2,1)} custom-call(bf16[40,7168]{1,0:T(8,128)(2,1)S(1)} %get-tuple-element.103.front, bf16[128,7168]{1,0:T(8,128)(2,1)S(1)} %copy-done.3, bf16[88,2688]{1,0:T(8,128)(2,1)S(1)} %bitcast.37, s32[4,128]{1,0:T(4,128)S(1)} %copy-done.34), custom_call_target="tpu_custom_call" | custom-call | flops 176160768 | bytes 2752512 | tf_op jit(solution)/shard_map/hidden/finish_hidden/pallas_call | solution.py:178
  160.5 2.4 %finish_hidden.4.refs_0_ = bf16[128,7168]{1,0:T(8,128)(2,1)} custom-call(bf16[40,7168]{1,0:T(8,128)(2,1)S(1)} %get-tuple-element.103.front, bf16[128,7168]{1,0:T(8,128)(2,1)S(1)} %copy-done.3, bf16[88,2688]{1,0:T(8,128)(2,1)S(1)} %bitcast.38, s32[4,128]{1,0:T(4,128)S(1)} %copy-done.34, ...), custom_call_target="tpu_custom_call", output_to_operand_aliasing={{}: (4, {})} | custom-call | flops 176160768 | bytes 2752512 | tf_op jit(solution)/shard_map/hidden/finish_hidden/pallas_call | solution.py:178
  162.9 5.7 %all-to-all-done.1 = bf16[16,8,3584]{2,1,0:T(8,128)(2,1)S(1)} async-done(((bf16[16,8,3584]{2,1,0:T(8,128)(2,1)}), bf16[16,8,3584]{2,1,0:T(8,128)(2,1)S(1)}, u32[]{:S(2)}, u32[]{:S(2)}) %all-to-all-start.1) | async-done | bytes 917536 | tf_op jit(solution)/shard_map/rows_back/all_to_all | solution.py:474
  168.6 2.9 %mix.1 = bf16[128,7168]{1,0:T(8,128)(2,1)} custom-call(s32[4]{0:T(128)S(1)} %copy-done.43, bf16[128,3584]{1,0:T(8,128)(2,1)S(1)} %bitcast.31, bf16[64,128]{1,0:T(8,128)(2,1)S(1)} %copy-done.35, bf16[64,128]{1,0:T(8,128)(2,1)S(1)} %copy-done.36), custom_call_target="tpu_custom_call" | custom-call | flops 234881024 | bytes 2752512 | tf_op jit(solution)/shard_map/mix/mix/pallas_call | solution.py:312
  172.5 1.7 finish_hidden.5
  (144 shorter events, 29.4 us)
Async XLA Ops:
  7.2 148.9 %reduce-scatter.12.cloned.1.call-start = ((), (), s32[]{:S(2)}) async-start(), calls=%async_computation.7 | async-start | bytes 2365440
  7.2 24.6 %collective-permute-start.5 = (bf16[1792,512]{1,0:T(8,128)(2,1)}, bf16[1792,512]{1,0:T(8,128)(2,1)}, u32[]{:S(2)}, u32[]{:S(2)}) collective-permute-start(bf16[1792,512]{1,0:T(8,128)(2,1)} %bitcast.32), channel_id=1, source_target_pairs={{0,32},{32,0},{1,33},{33,1},{2,34},{34,2},{3,35},{35,3},{4,36},{36... | collective-permute-start | bytes 5505032 | tf_op jit(solution)/shard_map/weight_swap/ppermute | solution.py:431
  7.3 24.5 %collective-permute-start.6 = (bf16[1792,512]{1,0:T(8,128)(2,1)}, bf16[1792,512]{1,0:T(8,128)(2,1)}, u32[]{:S(2)}, u32[]{:S(2)}) collective-permute-start(bf16[1792,512]{1,0:T(8,128)(2,1)} %bitcast.34), channel_id=1, source_target_pairs={{0,32},{32,0},{1,33},{33,1},{2,34},{34,2},{3,35},{35,3},{4,36},{36... | collective-permute-start | bytes 5505032 | tf_op jit(solution)/shard_map/weight_swap/ppermute | solution.py:432
  7.8 24.0 %collective-permute-start.7 = (bf16[512,1792]{1,0:T(8,128)(2,1)}, bf16[512,1792]{1,0:T(8,128)(2,1)}, u32[]{:S(2)}, u32[]{:S(2)}) collective-permute-start(bf16[512,1792]{1,0:T(8,128)(2,1)} %bitcast.43), channel_id=1, source_target_pairs={{0,32},{32,0},{1,33},{33,1},{2,34},{34,2},{3,35},{35,3},{4,36},{36... | collective-permute-start | bytes 5505032 | tf_op jit(solution)/shard_map/weight_swap/ppermute | solution.py:433
  10.0 4.2 %collective-permute-start = (s32[1,128]{1,0:T(1,128)S(1)}, s32[1,128]{1,0:T(1,128)S(1)}, u32[]{:S(2)}, u32[]{:S(2)}) collective-permute-start(s32[1,128]{1,0:T(1,128)S(1)} %select_bitcast_fusion.after), channel_id=1, source_target_pairs={{0,3},{1,0},{2,1},{3,2},{4,7},{5,4},{6,5},{7,6},{8,11},{9,8},{10,9... | collective-permute-start | bytes 1544 | tf_op jit(solution)/shard_map/routing/ppermute | solution.py:21
  12.9 6.0 %collective-permute-start.1 = (s32[1,128]{1,0:T(1,128)S(1)}, s32[1,128]{1,0:T(1,128)S(1)}, u32[]{:S(2)}, u32[]{:S(2)}) collective-permute-start(s32[1,128]{1,0:T(1,128)S(1)} %select_bitcast_fusion.after), channel_id=1, source_target_pairs={{0,2},{1,3},{2,0},{3,1},{4,6},{5,7},{6,4},{7,5},{8,10},{9,11},{10,... | collective-permute-start | bytes 1544 | tf_op jit(solution)/shard_map/routing/ppermute | solution.py:21
  14.2 5.0 %collective-permute-start.2 = (s32[1,128]{1,0:T(1,128)S(1)}, s32[1,128]{1,0:T(1,128)S(1)}, u32[]{:S(2)}, u32[]{:S(2)}) collective-permute-start(s32[1,128]{1,0:T(1,128)S(1)} %select_bitcast_fusion.after), channel_id=1, source_target_pairs={{0,1},{1,2},{2,3},{3,0},{4,5},{5,6},{6,7},{7,4},{8,9},{9,10},{10,1... | collective-permute-start | bytes 1544 | tf_op jit(solution)/shard_map/routing/ppermute | solution.py:21
  15.3 12.0 %copy-start.38 = (s32[4]{0:T(128)}, s32[4]{0:T(128)S(1)}, u32[]{:S(2)}) copy-start(s32[4]{0:T(128)S(1)} %pad_add_fusion.1.where_ref) | copy-start | bytes 52
  18.9 8.4 %copy-start = (bf16[512,7168]{1,0:T(8,128)(2,1)}, bf16[512,7168]{1,0:T(8,128)(2,1)S(1)}, u32[]{:S(2)}) copy-start(bf16[512,7168]{1,0:T(8,128)(2,1)S(1)} %load.1.attn) | copy-start | bytes 22020100
  19.2 8.1 %copy-start.30 = (s32[4,128]{1,0:T(4,128)}, s32[4,128]{1,0:T(4,128)S(1)}, u32[]{:S(2)}) copy-start(s32[4,128]{1,0:T(4,128)S(1)} %pad_add_fusion.poses.pos) | copy-start | bytes 6148
  20.1 5.1 %copy-start.45 = (s32[128,8]{0,1:T(8,128)S(1)}, s32[128,8]{0,1:T(8,128)}, u32[]{:S(2)}) copy-start(s32[128,8]{0,1:T(8,128)} %param.11) | copy-start | bytes 12292
  20.1 5.1 %copy-start.46 = (f32[128,8]{0,1:T(8,128)S(1)}, f32[128,8]{0,1:T(8,128)}, u32[]{:S(2)}) copy-start(f32[128,8]{0,1:T(8,128)} %param.12) | copy-start | bytes 12292
  20.2 9.6 %collective-permute-start.3 = (bf16[40,3584]{1,0:T(8,128)(2,1)S(1)}, bf16[40,3584]{1,0:T(8,128)(2,1)S(1)}, u32[]{:S(2)}, u32[]{:S(2)}) collective-permute-start(bf16[40,3584]{1,0:T(8,128)(2,1)S(1)} %get-tuple-element.86), channel_id=1, source_target_pairs={{0,1},{1,2},{2,3},{3,0},{4,5},{5,6},{6,7},{7,4},{8,9},{9,10},{10,1... | collective-permute-start | bytes 860168 | tf_op jit(solution)/shard_map/front_sum/ppermute | solution.py:21
  21.5 9.4 %collective-permute-start.4 = (bf16[40,3584]{1,0:T(8,128)(2,1)S(1)}, bf16[40,3584]{1,0:T(8,128)(2,1)S(1)}, u32[]{:S(2)}, u32[]{:S(2)}) collective-permute-start(bf16[40,3584]{1,0:T(8,128)(2,1)S(1)} %get-tuple-element.87), channel_id=1, source_target_pairs={{0,3},{1,0},{2,1},{3,2},{4,7},{5,4},{6,5},{7,6},{8,11},{9,8},{10,9... | collective-permute-start | bytes 860168 | tf_op jit(solution)/shard_map/front_sum/ppermute | solution.py:21
  29.8 15.9 %copy-start.3 = (bf16[128,7168]{1,0:T(8,128)(2,1)S(1)}, bf16[128,7168]{1,0:T(8,128)(2,1)}, u32[]{:S(2)}) copy-start(bf16[128,7168]{1,0:T(8,128)(2,1)} %residual.7) | copy-start | bytes 5505028
  29.8 10.0 %collective-permute-start.10 = (bf16[40,3584]{1,0:T(8,128)(2,1)}, bf16[40,3584]{1,0:T(8,128)(2,1)S(1)}, u32[]{:S(2)}, u32[]{:S(2)}) collective-permute-start(bf16[40,3584]{1,0:T(8,128)(2,1)} %get-tuple-element.95), channel_id=1, source_target_pairs={{0,3},{1,0},{2,1},{3,2},{4,7},{5,4},{6,5},{7,6},{8,11},{9,8},{10,9... | collective-permute-start | bytes 860168 | tf_op jit(solution)/shard_map/front_sum/ppermute | solution.py:21
  30.9 11.2 %collective-permute-start.9 = (bf16[40,3584]{1,0:T(8,128)(2,1)}, bf16[40,3584]{1,0:T(8,128)(2,1)S(1)}, u32[]{:S(2)}, u32[]{:S(2)}) collective-permute-start(bf16[40,3584]{1,0:T(8,128)(2,1)} %get-tuple-element.94), channel_id=1, source_target_pairs={{0,1},{1,2},{2,3},{3,0},{4,5},{5,6},{6,7},{7,4},{8,9},{9,10},{10,1... | collective-permute-start | bytes 860168 | tf_op jit(solution)/shard_map/front_sum/ppermute | solution.py:21
  31.9 13.8 %copy-start.31 = (s32[4,128]{1,0:T(4,128)S(1)}, s32[4,128]{1,0:T(4,128)}, u32[]{:S(2)}) copy-start(s32[4,128]{1,0:T(4,128)} %copy-done.30) | copy-start | bytes 6148
  31.9 13.8 %copy-start.39 = (s32[4]{0:T(128)S(1)}, s32[4]{0:T(128)}, u32[]{:S(2)}) copy-start(s32[4]{0:T(128)} %copy-done.38) | copy-start | bytes 52
  31.9 11.1 %collective-permute-start.11 = (bf16[40,3584]{1,0:T(8,128)(2,1)S(1)}, bf16[40,3584]{1,0:T(8,128)(2,1)S(1)}, u32[]{:S(2)}, u32[]{:S(2)}) collective-permute-start(bf16[40,3584]{1,0:T(8,128)(2,1)S(1)} %add_convert_fusion.2), channel_id=1, source_target_pairs={{0,3},{1,0},{2,1},{3,2},{4,7},{5,4},{6,5},{7,6},{8,11},{9,8},{10,9... | collective-permute-start | bytes 860168 | tf_op jit(solution)/shard_map/front_sum/ppermute | solution.py:21
  34.4 11.3 %collective-permute-start.8 = (bf16[40,3584]{1,0:T(8,128)(2,1)S(1)}, bf16[40,3584]{1,0:T(8,128)(2,1)S(1)}, u32[]{:S(2)}, u32[]{:S(2)}) collective-permute-start(bf16[40,3584]{1,0:T(8,128)(2,1)S(1)} %add_convert_fusion.3), channel_id=1, source_target_pairs={{0,1},{1,2},{2,3},{3,0},{4,5},{5,6},{6,7},{7,4},{8,9},{9,10},{10,1... | collective-permute-start | bytes 860168 | tf_op jit(solution)/shard_map/front_sum/ppermute | solution.py:21
  52.3 8.2 %copy-start.33 = (s32[4,128]{1,0:T(4,128)S(1)}, s32[4,128]{1,0:T(4,128)}, u32[]{:S(2)}) copy-start(s32[4,128]{1,0:T(4,128)} %copy-done.30) | copy-start | bytes 6148
  52.3 8.3 %copy-start.41 = (s32[4]{0:T(128)S(1)}, s32[4]{0:T(128)}, u32[]{:S(2)}) copy-start(s32[4]{0:T(128)} %copy-done.38) | copy-start | bytes 52
  52.3 22.0 %all-to-all-start = ((bf16[16,8,3584]{2,1,0:T(8,128)(2,1)}), bf16[16,8,3584]{2,1,0:T(8,128)(2,1)S(1)}, u32[]{:S(2)}, u32[]{:S(2)}) async-start(bf16[16,8,3584]{2,1,0:T(8,128)(2,1)} %bitcast.36), calls=%async_computation | async-start | bytes 1835008 | tf_op jit(solution)/shard_map/rows_out/all_to_all | solution.py:461
  60.5 99.0 %reduce-scatter.10.cloned.1.call-start = ((), (), s32[]{:S(2)}) async-start(), calls=%async_computation.6 | async-start | bytes 2365440
  74.6 11.0 %collective-permute-start.12 = (bf16[80,1792]{1,0:T(8,128)(2,1)S(1)}, bf16[80,1792]{1,0:T(8,128)(2,1)S(1)}, u32[]{:S(2)}, u32[]{:S(2)}) collective-permute-start(bf16[80,1792]{1,0:T(8,128)(2,1)S(1)} %get-tuple-element.114.a0), channel_id=1, source_target_pairs={{0,1},{1,2},{2,3},{3,0},{4,5},{5,6},{6,7},{7,4},{8,9},{9,10},{10,1... | collective-permute-start | bytes 860168 | tf_op jit(solution)/shard_map/rows_out/ppermute | solution.py:21
  74.7 11.0 %collective-permute-start.15 = (bf16[80,1792]{1,0:T(8,128)(2,1)S(1)}, bf16[80,1792]{1,0:T(8,128)(2,1)S(1)}, u32[]{:S(2)}, u32[]{:S(2)}) collective-permute-start(bf16[80,1792]{1,0:T(8,128)(2,1)S(1)} %get-tuple-element.118.b0), channel_id=1, source_target_pairs={{0,3},{1,0},{2,1},{3,2},{4,7},{5,4},{6,5},{7,6},{8,11},{9,8},{10,9... | collective-permute-start | bytes 860168 | tf_op jit(solution)/shard_map/rows_out/ppermute | solution.py:21
  77.9 12.5 %collective-permute-start.13 = (bf16[80,1792]{1,0:T(8,128)(2,1)S(1)}, bf16[80,1792]{1,0:T(8,128)(2,1)S(1)}, u32[]{:S(2)}, u32[]{:S(2)}) collective-permute-start(bf16[80,1792]{1,0:T(8,128)(2,1)S(1)} %get-tuple-element.118.b0), channel_id=1, source_target_pairs={{0,1},{1,2},{2,3},{3,0},{4,5},{5,6},{6,7},{7,4},{8,9},{9,10},{10,1... | collective-permute-start | bytes 860168 | tf_op jit(solution)/shard_map/rows_out/ppermute | solution.py:21
  78.6 12.5 %collective-permute-start.17 = (bf16[80,1792]{1,0:T(8,128)(2,1)S(1)}, bf16[80,1792]{1,0:T(8,128)(2,1)S(1)}, u32[]{:S(2)}, u32[]{:S(2)}) collective-permute-start(bf16[80,1792]{1,0:T(8,128)(2,1)S(1)} %get-tuple-element.114.a0), channel_id=1, source_target_pairs={{0,3},{1,0},{2,1},{3,2},{4,7},{5,4},{6,5},{7,6},{8,11},{9,8},{10,9... | collective-permute-start | bytes 860168 | tf_op jit(solution)/shard_map/rows_out/ppermute | solution.py:21
  82.6 12.6 %copy-start.17 = (bf16[80,1792]{1,0:T(8,128)(2,1)S(1)}, bf16[80,1792]{1,0:T(8,128)(2,1)}, u32[]{:S(2)}) copy-start(bf16[80,1792]{1,0:T(8,128)(2,1)} %copy-done.16) | copy-start | bytes 860164
  85.7 9.5 %copy-start.15 = (bf16[80,1792]{1,0:T(8,128)(2,1)S(1)}, bf16[80,1792]{1,0:T(8,128)(2,1)}, u32[]{:S(2)}) copy-start(bf16[80,1792]{1,0:T(8,128)(2,1)} %copy-done.14) | copy-start | bytes 860164
  85.7 7.8 %collective-permute-start.14 = (bf16[80,1792]{1,0:T(8,128)(2,1)S(1)}, bf16[80,1792]{1,0:T(8,128)(2,1)S(1)}, u32[]{:S(2)}, u32[]{:S(2)}) collective-permute-start(bf16[80,1792]{1,0:T(8,128)(2,1)S(1)} %collective-permute-done.12.a1), channel_id=1, source_target_pairs={{0,1},{1,2},{2,3},{3,0},{4,5},{5,6},{6,7},{7,4},{8,9},{9,10},{10,1... | collective-permute-start | bytes 860168 | tf_op jit(solution)/shard_map/rows_out/ppermute | solution.py:21
  85.7 8.6 %collective-permute-start.16 = (bf16[80,1792]{1,0:T(8,128)(2,1)S(1)}, bf16[80,1792]{1,0:T(8,128)(2,1)S(1)}, u32[]{:S(2)}, u32[]{:S(2)}) collective-permute-start(bf16[80,1792]{1,0:T(8,128)(2,1)S(1)} %collective-permute-done.15.b3), channel_id=1, source_target_pairs={{0,3},{1,0},{2,1},{3,2},{4,7},{5,4},{6,5},{7,6},{8,11},{9,8},{10,9... | collective-permute-start | bytes 860168 | tf_op jit(solution)/shard_map/rows_out/ppermute | solution.py:21
  95.0 76.5 %reduce-scatter.8.cloned.1.call-start = ((), (), s32[]{:S(2)}) async-start(), calls=%async_computation.5 | async-start | bytes 1576960 | tf_op jit(solution)/shard_map/rows_back/head_sum/reduce_scatter | solution.py:440
  107.4 17.0 %copy-start.47 = (bf16[1,512,1792]{2,1,0:T(8,128)(2,1)S(1)}, bf16[1,512,1792]{2,1,0:T(8,128)(2,1)}, u32[]{:S(2)}) copy-start(bf16[1,512,1792]{2,1,0:T(8,128)(2,1)} %param.15) | copy-start | bytes 5505028
  107.4 9.8 %collective-permute-start.18 = (bf16[160,1024]{1,0:T(8,128)(2,1)S(1)}, bf16[160,1024]{1,0:T(8,128)(2,1)S(1)}, u32[]{:S(2)}, u32[]{:S(2)}) collective-permute-start(bf16[160,1024]{1,0:T(8,128)(2,1)S(1)} %get-tuple-element.125), channel_id=1, source_target_pairs={{0,64},{64,0},{1,65},{65,1},{2,66},{66,2},{3,67},{67,3},{4,68},{68... | collective-permute-start | bytes 983048 | tf_op jit(solution)/shard_map/gate_up/ppermute | solution.py:467
  117.4 6.9 %collective-permute-start.19 = (bf16[160,512]{1,0:T(8,128)(2,1)S(1)}, bf16[160,512]{1,0:T(8,128)(2,1)S(1)}, u32[]{:S(2)}, u32[]{:S(2)}) collective-permute-start(bf16[160,512]{1,0:T(8,128)(2,1)S(1)} %fusion.1.mine), channel_id=1, source_target_pairs={{0,64},{64,0},{1,65},{65,1},{2,66},{66,2},{3,67},{67,3},{4,68},{68... | collective-permute-start | bytes 491528 | tf_op jit(solution)/shard_map/gate_up/ppermute | solution.py:469
  127.4 9.0 %collective-permute-start.24 = (bf16[80,1792]{1,0:T(8,128)(2,1)S(1)}, bf16[80,1792]{1,0:T(8,128)(2,1)S(1)}, u32[]{:S(2)}, u32[]{:S(2)}) collective-permute-start(bf16[80,1792]{1,0:T(8,128)(2,1)S(1)} %get-tuple-element.132), channel_id=1, source_target_pairs={{0,3},{1,0},{2,1},{3,2},{4,7},{5,4},{6,5},{7,6},{8,11},{9,8},{10,9... | collective-permute-start | bytes 860168 | tf_op jit(solution)/shard_map/rows_back/ppermute | solution.py:21
  129.9 10.3 %collective-permute-start.20 = (bf16[80,1792]{1,0:T(8,128)(2,1)S(1)}, bf16[80,1792]{1,0:T(8,128)(2,1)S(1)}, u32[]{:S(2)}, u32[]{:S(2)}) collective-permute-start(bf16[80,1792]{1,0:T(8,128)(2,1)S(1)} %get-tuple-element.128), channel_id=1, source_target_pairs={{0,1},{1,2},{2,3},{3,0},{4,5},{5,6},{6,7},{7,4},{8,9},{9,10},{10,1... | collective-permute-start | bytes 860168 | tf_op jit(solution)/shard_map/rows_back/ppermute | solution.py:21
  129.9 13.1 %collective-permute-start.22 = (bf16[80,1792]{1,0:T(8,128)(2,1)S(1)}, bf16[80,1792]{1,0:T(8,128)(2,1)S(1)}, u32[]{:S(2)}, u32[]{:S(2)}) collective-permute-start(bf16[80,1792]{1,0:T(8,128)(2,1)S(1)} %get-tuple-element.129), channel_id=1, source_target_pairs={{0,1},{1,2},{2,3},{3,0},{4,5},{5,6},{6,7},{7,4},{8,9},{9,10},{10,1... | collective-permute-start | bytes 860168 | tf_op jit(solution)/shard_map/rows_back/ppermute | solution.py:21
  129.9 13.1 %collective-permute-start.23 = (bf16[80,1792]{1,0:T(8,128)(2,1)S(1)}, bf16[80,1792]{1,0:T(8,128)(2,1)S(1)}, u32[]{:S(2)}, u32[]{:S(2)}) collective-permute-start(bf16[80,1792]{1,0:T(8,128)(2,1)S(1)} %get-tuple-element.130), channel_id=1, source_target_pairs={{0,3},{1,0},{2,1},{3,2},{4,7},{5,4},{6,5},{7,6},{8,11},{9,8},{10,9... | collective-permute-start | bytes 860168 | tf_op jit(solution)/shard_map/rows_back/ppermute | solution.py:21
  136.5 7.9 %collective-permute-start.25 = (bf16[80,1792]{1,0:T(8,128)(2,1)S(1)}, bf16[80,1792]{1,0:T(8,128)(2,1)S(1)}, u32[]{:S(2)}, u32[]{:S(2)}) collective-permute-start(bf16[80,1792]{1,0:T(8,128)(2,1)S(1)} %add_convert_fusion), channel_id=1, source_target_pairs={{0,3},{1,0},{2,1},{3,2},{4,7},{5,4},{6,5},{7,6},{8,11},{9,8},{10,9... | collective-permute-start | bytes 860168 | tf_op jit(solution)/shard_map/rows_back/ppermute | solution.py:21
  140.3 7.9 %collective-permute-start.21 = (bf16[80,1792]{1,0:T(8,128)(2,1)S(1)}, bf16[80,1792]{1,0:T(8,128)(2,1)S(1)}, u32[]{:S(2)}, u32[]{:S(2)}) collective-permute-start(bf16[80,1792]{1,0:T(8,128)(2,1)S(1)} %add_convert_fusion.1), channel_id=1, source_target_pairs={{0,1},{1,2},{2,3},{3,0},{4,5},{5,6},{6,7},{7,4},{8,9},{9,10},{10,1... | collective-permute-start | bytes 860168 | tf_op jit(solution)/shard_map/rows_back/ppermute | solution.py:21
  152.2 3.8 %copy-start.34 = (s32[4,128]{1,0:T(4,128)S(1)}, s32[4,128]{1,0:T(4,128)}, u32[]{:S(2)}) copy-start(s32[4,128]{1,0:T(4,128)} %copy-done.30) | copy-start | bytes 6148
  152.3 16.3 %all-to-all-start.1 = ((bf16[16,8,3584]{2,1,0:T(8,128)(2,1)}), bf16[16,8,3584]{2,1,0:T(8,128)(2,1)S(1)}, u32[]{:S(2)}, u32[]{:S(2)}) async-start(bf16[16,8,3584]{2,1,0:T(8,128)(2,1)} %bitcast.18), calls=%async_computation.2 | async-start | bytes 1835008 | tf_op jit(solution)/shard_map/rows_back/all_to_all | solution.py:474
  160.5 8.1 %copy-start.35 = (bf16[64,128]{1,0:T(8,128)(2,1)S(1)}, bf16[64,128]{1,0:T(8,128)(2,1)}, u32[]{:S(2)}) copy-start(bf16[64,128]{1,0:T(8,128)(2,1)} %convert_element_type.60.high) | copy-start | bytes 49156
  160.5 8.1 %copy-start.36 = (bf16[64,128]{1,0:T(8,128)(2,1)S(1)}, bf16[64,128]{1,0:T(8,128)(2,1)}, u32[]{:S(2)}) copy-start(bf16[64,128]{1,0:T(8,128)(2,1)} %convert_element_type.61.low) | copy-start | bytes 49156
  160.5 8.1 %copy-start.43 = (s32[4]{0:T(128)S(1)}, s32[4]{0:T(128)}, u32[]{:S(2)}) copy-start(s32[4]{0:T(128)} %copy-done.38) | copy-start | bytes 52
  (31 other events, 36.8 us)
Sparse Core Ops, SparseCore 0:
  45.8 27.9 reduce-scatter.11
  95.1 25.4 reduce-scatter.9
  149.1 19.9 reduce-scatter.7

commit v4 on v3

--- a/solution.py
+++ b/solution.py
@@ -469,8 +469,8 @@
         other = lax.ppermute(middle, "zh", SWAP)
     with jax.named_scope("rows_back"):
         outs = down(where, middle, other, wd, wd2)
-        came = head_sum(2, ring_sum(outs[4:6], outs[6:8], outs[2:4])[:2])
-        total = add_parts(outs[:2], *came)
+        total = add_parts(outs[:2], *ring_sum(outs[4:6], outs[6:8], outs[2:4])[:2])
+        total = head_sum(2, total)
         returned = lax.all_to_all(total, grid, split_axis=0, concat_axis=0, tiled=True)
     with jax.named_scope("hidden"):
         hidden = finish_hidden(where, front, residual, summed[0], poses, 0)

time: 182 us -> 180 us (0.989)
  local copies, waits for them, and re-layouts: 32.7 us -> 29.5 us
    unnamed x96 -> x88, local copies, waits for them, and re-layouts: 32.1 us -> 28.9 us
  transfers between devices with their start and end apart: 31 -> 31, of which waited for: 17 -> 18; matrix products, arithmetic and copies ran while one was open for 2% -> 2% of each run, Pallas kernels for 14% -> 14%
where the time goes in v4:
time: 180 us; the launch traced here: 179 us
  waiting for transfers between devices  56.7 us (32%)
  starting transfers between devices  47.2 us (26%)
  local copies, waits for them, and re-layouts  29.5 us (16%)
  Pallas kernels  27.4 us (15%)
  between operations  14.2 us (8%)
  other arithmetic  3.72 us (2%)
    ppermute x21, starting transfers between devices, shift(): lax.ppermute(value, 'x', [(j, (j + steps) % RING) for j in range(RING)])  31.8 us
    ppermute x21, waiting for transfers between devices, shift(): lax.ppermute(value, 'x', [(j, (j + steps) % RING) for j in range(RING)])  29.3 us
    unnamed x88, local copies, waits for them, and re-layouts  28.9 us
    ppermute x1, waiting for transfers between devices, local(): mine = mine + lax.ppermute(away, 'zh', SWAP).astype(F32)  8.6 us
    all_to_all x1, starting transfers between devices, local(): lax.all_to_all(message, grid, split_axis=0, concat_axis=0, tiled=True)  8.18 us
    all_to_all x1, waiting for transfers between devices, local(): lax.all_to_all(message, grid, split_axis=0, concat_axis=0, tiled=True)  6.68 us
    pallas_call x3, Pallas kernels, finish_hidden(): pl.pallas_call(kernel, grid=(wide // TILE,), in_specs=in_specs, out_specs...  6.48 us
    all_to_all x1, waiting for transfers between devices, local(): lax.all_to_all(total, grid, split_axis=0, concat_axis=0, tiled=True)  5.59 us
  transfers between devices with their start and end apart: 31, of which 18 were waited for; matrix products, arithmetic and copies ran while one was open for 2% of the time, Pallas kernels for 14%

profile of v4, /device:TPU:0, one launch (start us, length us, event | category | flops | bytes accessed | tf_op | source)
XLA Modules:
  0.0 178.8 jit_solution(7033907413402176664)
XLA Ops:
  10.0 2.9 %collective-permute-start = (s32[1,128]{1,0:T(1,128)S(1)}, s32[1,128]{1,0:T(1,128)S(1)}, u32[]{:S(2)}, u32[]{:S(2)}) collective-permute-start(s32[1,128]{1,0:T(1,128)S(1)} %select_bitcast_fusion.after), channel_id=1, source_target_pairs={{0,3},{1,0},{2,1},{3,2},{4,7},{5,4},{6,5},{7,6},{8,11},{9,8},{10,9... | collective-permute-start | bytes 1544 | tf_op jit(solution)/shard_map/routing/ppermute | solution.py:21
  15.3 3.1 %copy-done.5 = bf16[1,512,7168]{2,1,0:T(8,128)(2,1)S(1)} copy-done((bf16[1,512,7168]{2,1,0:T(8,128)(2,1)S(1)}, bf16[1,512,7168]{2,1,0:T(8,128)(2,1)}, u32[]{:S(2)}) %copy-start.5) | copy-done | bytes 7340056
  20.2 1.3 collective-permute-start.3
  21.5 2.0 %collective-permute-start.4 = (bf16[40,3584]{1,0:T(8,128)(2,1)S(1)}, bf16[40,3584]{1,0:T(8,128)(2,1)S(1)}, u32[]{:S(2)}, u32[]{:S(2)}) collective-permute-start(bf16[40,3584]{1,0:T(8,128)(2,1)S(1)} %get-tuple-element.84), channel_id=1, source_target_pairs={{0,3},{1,0},{2,1},{3,2},{4,7},{5,4},{6,5},{7,6},{8,11},{9,8},{10,9... | collective-permute-start | bytes 860168 | tf_op jit(solution)/shard_map/front_sum/ppermute | solution.py:21
  23.5 1.8 select_rows.3
  27.2 1.2 back_rows.2
  28.5 1.3 copy-done.4
  31.9 2.4 %collective-permute-start.11 = (bf16[40,3584]{1,0:T(8,128)(2,1)S(1)}, bf16[40,3584]{1,0:T(8,128)(2,1)S(1)}, u32[]{:S(2)}, u32[]{:S(2)}) collective-permute-start(bf16[40,3584]{1,0:T(8,128)(2,1)S(1)} %add_convert_fusion.2), channel_id=1, source_target_pairs={{0,3},{1,0},{2,1},{3,2},{4,7},{5,4},{6,5},{7,6},{8,11},{9,8},{10,9... | collective-permute-start | bytes 860168 | tf_op jit(solution)/shard_map/front_sum/ppermute | solution.py:21
  34.5 5.3 %collective-permute-done.10.r2 = bf16[40,3584]{1,0:T(8,128)(2,1)S(1)} collective-permute-done((bf16[40,3584]{1,0:T(8,128)(2,1)}, bf16[40,3584]{1,0:T(8,128)(2,1)S(1)}, u32[]{:S(2)}, u32[]{:S(2)}) %collective-permute-start.10) | collective-permute-done | bytes 286752 | tf_op jit(solution)/shard_map/front_sum/ppermute | solution.py:21
  39.8 2.3 %collective-permute-done.9.r1 = bf16[40,3584]{1,0:T(8,128)(2,1)S(1)} collective-permute-done((bf16[40,3584]{1,0:T(8,128)(2,1)}, bf16[40,3584]{1,0:T(8,128)(2,1)S(1)}, u32[]{:S(2)}, u32[]{:S(2)}) %collective-permute-start.9) | collective-permute-done | bytes 286752 | tf_op jit(solution)/shard_map/front_sum/ppermute | solution.py:21
  43.1 2.6 %collective-permute-done.8.r0 = bf16[40,3584]{1,0:T(8,128)(2,1)S(1)} collective-permute-done((bf16[40,3584]{1,0:T(8,128)(2,1)S(1)}, bf16[40,3584]{1,0:T(8,128)(2,1)S(1)}, u32[]{:S(2)}, u32[]{:S(2)}) %collective-permute-start.8) | collective-permute-done | bytes 286752 | tf_op jit(solution)/shard_map/front_sum/ppermute | solution.py:21
  45.7 3.1 %copy-done.1 = bf16[512,7168]{1,0:T(8,128)(2,1)S(1)} copy-done((bf16[512,7168]{1,0:T(8,128)(2,1)S(1)}, bf16[512,7168]{1,0:T(8,128)(2,1)}, u32[]{:S(2)}) %copy-start.1) | copy-done | bytes 7340056
  48.8 1.1 own_rows.1.base
  50.0 1.4 dispatch.1
  52.3 8.2 %all-to-all-start = ((bf16[16,8,3584]{2,1,0:T(8,128)(2,1)}), bf16[16,8,3584]{2,1,0:T(8,128)(2,1)S(1)}, u32[]{:S(2)}, u32[]{:S(2)}) async-start(bf16[16,8,3584]{2,1,0:T(8,128)(2,1)} %bitcast.36), calls=%async_computation | async-start | bytes 1835008 | tf_op jit(solution)/shard_map/rows_out/all_to_all | solution.py:461
  60.5 3.1 %copy-done.2 = bf16[512,7168]{1,0:T(8,128)(2,1)S(1)} copy-done((bf16[512,7168]{1,0:T(8,128)(2,1)S(1)}, bf16[512,7168]{1,0:T(8,128)(2,1)}, u32[]{:S(2)}) %copy-start.2) | copy-done | bytes 7340056
  63.7 1.6 back_rows.3
  65.3 1.2 copy-done.6
  67.6 6.7 %all-to-all-done = bf16[16,8,3584]{2,1,0:T(8,128)(2,1)S(1)} async-done(((bf16[16,8,3584]{2,1,0:T(8,128)(2,1)}), bf16[16,8,3584]{2,1,0:T(8,128)(2,1)S(1)}, u32[]{:S(2)}, u32[]{:S(2)}) %all-to-all-start) | async-done | bytes 917536 | tf_op jit(solution)/shard_map/rows_out/all_to_all | solution.py:461
  74.7 3.2 %collective-permute-start.15 = (bf16[80,1792]{1,0:T(8,128)(2,1)S(1)}, bf16[80,1792]{1,0:T(8,128)(2,1)S(1)}, u32[]{:S(2)}, u32[]{:S(2)}) collective-permute-start(bf16[80,1792]{1,0:T(8,128)(2,1)S(1)} %get-tuple-element.115.b0), channel_id=1, source_target_pairs={{0,3},{1,0},{2,1},{3,2},{4,7},{5,4},{6,5},{7,6},{8,11},{9,8},{10,9... | collective-permute-start | bytes 860168 | tf_op jit(solution)/shard_map/rows_out/ppermute | solution.py:21
  78.6 3.2 %collective-permute-start.17 = (bf16[80,1792]{1,0:T(8,128)(2,1)S(1)}, bf16[80,1792]{1,0:T(8,128)(2,1)S(1)}, u32[]{:S(2)}, u32[]{:S(2)}) collective-permute-start(bf16[80,1792]{1,0:T(8,128)(2,1)S(1)} %get-tuple-element.111.a0), channel_id=1, source_target_pairs={{0,3},{1,0},{2,1},{3,2},{4,7},{5,4},{6,5},{7,6},{8,11},{9,8},{10,9... | collective-permute-start | bytes 860168 | tf_op jit(solution)/shard_map/rows_out/ppermute | solution.py:21
  82.6 3.1 %collective-permute-done.12.a1 = bf16[80,1792]{1,0:T(8,128)(2,1)S(1)} collective-permute-done((bf16[80,1792]{1,0:T(8,128)(2,1)S(1)}, bf16[80,1792]{1,0:T(8,128)(2,1)S(1)}, u32[]{:S(2)}, u32[]{:S(2)}) %collective-permute-start.12) | collective-permute-done | bytes 286752 | tf_op jit(solution)/shard_map/rows_out/ppermute | solution.py:21
  85.7 3.2 %collective-permute-start.16 = (bf16[80,1792]{1,0:T(8,128)(2,1)S(1)}, bf16[80,1792]{1,0:T(8,128)(2,1)S(1)}, u32[]{:S(2)}, u32[]{:S(2)}) collective-permute-start(bf16[80,1792]{1,0:T(8,128)(2,1)S(1)} %collective-permute-done.15.b3), channel_id=1, source_target_pairs={{0,3},{1,0},{2,1},{3,2},{4,7},{5,4},{6,5},{7,6},{8,11},{9,8},{10,9... | collective-permute-start | bytes 860168 | tf_op jit(solution)/shard_map/rows_out/ppermute | solution.py:21
  88.9 1.5 collective-permute-done.13.b1
  91.9 1.6 collective-permute-done.14.a2
  95.2 1.5 copy-done.7
  96.7 1.5 copy-done.8
  102.7 4.6 %gate_up.1 = (f32[160,1024]{1,0:T(8,128)S(1)}, bf16[160,1024]{1,0:T(8,128)(2,1)S(1)}) custom-call(s32[4]{0:T(128)S(1)} %copy-done.38, bf16[80,1792]{1,0:T(8,128)(2,1)S(1)} %copy-done.15, bf16[80,1792]{1,0:T(8,128)(2,1)S(1)} %collective-permute-done.12.a1, bf16[80,1792]{1,0:T(8,128)(2,1)S(1)} %copy-done.23, bf16[80,1792]{1,0:T(8,128)(2,1)S(1)} %copy-done.21, ...), custom_call_target="tpu_custom_call" | custom-call | flops 2348810240 | bytes 9633792 | tf_op jit(solution)/shard_map/gate_up/gate_up/pallas_call | solution.py:251
  107.3 1.2 collective-permute-start.18
  108.6 8.6 %collective-permute-done.18 = bf16[160,1024]{1,0:T(8,128)(2,1)S(1)} collective-permute-done((bf16[160,1024]{1,0:T(8,128)(2,1)S(1)}, bf16[160,1024]{1,0:T(8,128)(2,1)S(1)}, u32[]{:S(2)}, u32[]{:S(2)}) %collective-permute-start.18) | collective-permute-done | bytes 327712 | tf_op jit(solution)/shard_map/gate_up/ppermute | solution.py:467
  117.4 1.3 collective-permute-start.19
  118.7 5.6 %collective-permute-done.19.other = bf16[160,512]{1,0:T(8,128)(2,1)S(1)} collective-permute-done((bf16[160,512]{1,0:T(8,128)(2,1)S(1)}, bf16[160,512]{1,0:T(8,128)(2,1)S(1)}, u32[]{:S(2)}, u32[]{:S(2)}) %collective-permute-start.19) | collective-permute-done | bytes 163872 | tf_op jit(solution)/shard_map/gate_up/ppermute | solution.py:469
  124.3 3.0 %down.1 = (bf16[80,1792]{1,0:T(8,128)(2,1)S(1)}, bf16[80,1792]{1,0:T(8,128)(2,1)S(1)}, bf16[80,1792]{1,0:T(8,128)(2,1)S(1)}, bf16[80,1792]{1,0:T(8,128)(2,1)S(1)...) custom-call(s32[4]{0:T(128)S(1)} %copy-done.38, ...), custom_call_target="tpu_custom_call" | custom-call | flops 1174405120 | bytes 5963776 | tf_op jit(solution)/shard_map/rows_back/down/pallas_call | solution.py:282
  127.3 2.5 %collective-permute-start.24 = (bf16[80,1792]{1,0:T(8,128)(2,1)S(1)}, bf16[80,1792]{1,0:T(8,128)(2,1)S(1)}, u32[]{:S(2)}, u32[]{:S(2)}) collective-permute-start(bf16[80,1792]{1,0:T(8,128)(2,1)S(1)} %get-tuple-element.131), channel_id=1, source_target_pairs={{0,3},{1,0},{2,1},{3,2},{4,7},{5,4},{6,5},{7,6},{8,11},{9,8},{10,9... | collective-permute-start | bytes 860168 | tf_op jit(solution)/shard_map/rows_back/ppermute | solution.py:21
  129.8 3.3 %collective-permute-start.23 = (bf16[80,1792]{1,0:T(8,128)(2,1)S(1)}, bf16[80,1792]{1,0:T(8,128)(2,1)S(1)}, u32[]{:S(2)}, u32[]{:S(2)}) collective-permute-start(bf16[80,1792]{1,0:T(8,128)(2,1)S(1)} %get-tuple-element.129), channel_id=1, source_target_pairs={{0,3},{1,0},{2,1},{3,2},{4,7},{5,4},{6,5},{7,6},{8,11},{9,8},{10,9... | collective-permute-start | bytes 860168 | tf_op jit(solution)/shard_map/rows_back/ppermute | solution.py:21
  133.1 3.3 %collective-permute-done.24 = bf16[80,1792]{1,0:T(8,128)(2,1)S(1)} collective-permute-done((bf16[80,1792]{1,0:T(8,128)(2,1)S(1)}, bf16[80,1792]{1,0:T(8,128)(2,1)S(1)}, u32[]{:S(2)}, u32[]{:S(2)}) %collective-permute-start.24) | collective-permute-done | bytes 286752 | tf_op jit(solution)/shard_map/rows_back/ppermute | solution.py:21
  136.4 3.8 %collective-permute-start.25 = (bf16[80,1792]{1,0:T(8,128)(2,1)S(1)}, bf16[80,1792]{1,0:T(8,128)(2,1)S(1)}, u32[]{:S(2)}, u32[]{:S(2)}) collective-permute-start(bf16[80,1792]{1,0:T(8,128)(2,1)S(1)} %add_convert_fusion), channel_id=1, source_target_pairs={{0,3},{1,0},{2,1},{3,2},{4,7},{5,4},{6,5},{7,6},{8,11},{9,8},{10,9... | collective-permute-start | bytes 860168 | tf_op jit(solution)/shard_map/rows_back/ppermute | solution.py:21
  140.3 2.6 %collective-permute-done.22.refs_3_ = bf16[80,1792]{1,0:T(8,128)(2,1)S(1)} collective-permute-done((bf16[80,1792]{1,0:T(8,128)(2,1)S(1)}, bf16[80,1792]{1,0:T(8,128)(2,1)S(1)}, u32[]{:S(2)}, u32[]{:S(2)}) %collective-permute-start.22) | collective-permute-done | bytes 286752 | tf_op jit(solution)/shard_map/rows_back/ppermute | solution.py:21
  143.0 1.4 collective-permute-done.25.refs_5_
  144.3 3.8 %collective-permute-done.21.refs_2_ = bf16[80,1792]{1,0:T(8,128)(2,1)S(1)} collective-permute-done((bf16[80,1792]{1,0:T(8,128)(2,1)S(1)}, bf16[80,1792]{1,0:T(8,128)(2,1)S(1)}, u32[]{:S(2)}, u32[]{:S(2)}) %collective-permute-start.21) | collective-permute-done | bytes 286752 | tf_op jit(solution)/shard_map/rows_back/ppermute | solution.py:21
  148.1 1.4 add_parts.1
  149.5 3.7 %all-to-all-start.1 = ((bf16[16,8,3584]{2,1,0:T(8,128)(2,1)}), bf16[16,8,3584]{2,1,0:T(8,128)(2,1)S(1)}, u32[]{:S(2)}, u32[]{:S(2)}) async-start(bf16[16,8,3584]{2,1,0:T(8,128)(2,1)} %bitcast.18), calls=%async_computation.2 | async-start | bytes 1835008 | tf_op jit(solution)/shard_map/rows_back/all_to_all | solution.py:474
  153.3 1.1 copy-done.11
  154.4 2.4 %finish_hidden.3.refs_0_ = bf16[128,7168]{1,0:T(8,128)(2,1)} custom-call(bf16[40,7168]{1,0:T(8,128)(2,1)S(1)} %get-tuple-element.100.front, bf16[128,7168]{1,0:T(8,128)(2,1)S(1)} %copy-done.3, bf16[88,2688]{1,0:T(8,128)(2,1)S(1)} %bitcast.37, s32[4,128]{1,0:T(4,128)S(1)} %copy-done.30), custom_call_target="tpu_custom_call" | custom-call | flops 176160768 | bytes 2752512 | tf_op jit(solution)/shard_map/hidden/finish_hidden/pallas_call | solution.py:178
  157.8 2.4 %finish_hidden.4.refs_0_ = bf16[128,7168]{1,0:T(8,128)(2,1)} custom-call(bf16[40,7168]{1,0:T(8,128)(2,1)S(1)} %get-tuple-element.100.front, bf16[128,7168]{1,0:T(8,128)(2,1)S(1)} %copy-done.3, bf16[88,2688]{1,0:T(8,128)(2,1)S(1)} %bitcast.38, s32[4,128]{1,0:T(4,128)S(1)} %copy-done.30, ...), custom_call_target="tpu_custom_call", output_to_operand_aliasing={{}: (4, {})} | custom-call | flops 176160768 | bytes 2752512 | tf_op jit(solution)/shard_map/hidden/finish_hidden/pallas_call | solution.py:178
  160.2 5.6 %all-to-all-done.1 = bf16[16,8,3584]{2,1,0:T(8,128)(2,1)S(1)} async-done(((bf16[16,8,3584]{2,1,0:T(8,128)(2,1)}), bf16[16,8,3584]{2,1,0:T(8,128)(2,1)S(1)}, u32[]{:S(2)}, u32[]{:S(2)}) %all-to-all-start.1) | async-done | bytes 917536 | tf_op jit(solution)/shard_map/rows_back/all_to_all | solution.py:474
  165.8 2.9 %mix.1 = bf16[128,7168]{1,0:T(8,128)(2,1)} custom-call(s32[4]{0:T(128)S(1)} %copy-done.39, bf16[128,3584]{1,0:T(8,128)(2,1)S(1)} %bitcast.31, bf16[64,128]{1,0:T(8,128)(2,1)S(1)} %copy-done.31, bf16[64,128]{1,0:T(8,128)(2,1)S(1)} %copy-done.32), custom_call_target="tpu_custom_call" | custom-call | flops 234881024 | bytes 2752512 | tf_op jit(solution)/shard_map/mix/mix/pallas_call | solution.py:312
  170.5 1.7 finish_hidden.5
  (136 shorter events, 27.1 us)
Async XLA Ops:
  7.2 146.1 %reduce-scatter.12.cloned.1.call-start = ((), (), s32[]{:S(2)}) async-start(), calls=%async_computation.7 | async-start | bytes 2365440
  7.2 24.6 %collective-permute-start.5 = (bf16[1792,512]{1,0:T(8,128)(2,1)}, bf16[1792,512]{1,0:T(8,128)(2,1)}, u32[]{:S(2)}, u32[]{:S(2)}) collective-permute-start(bf16[1792,512]{1,0:T(8,128)(2,1)} %bitcast.32), channel_id=1, source_target_pairs={{0,32},{32,0},{1,33},{33,1},{2,34},{34,2},{3,35},{35,3},{4,36},{36... | collective-permute-start | bytes 5505032 | tf_op jit(solution)/shard_map/weight_swap/ppermute | solution.py:431
  7.3 24.5 %collective-permute-start.6 = (bf16[1792,512]{1,0:T(8,128)(2,1)}, bf16[1792,512]{1,0:T(8,128)(2,1)}, u32[]{:S(2)}, u32[]{:S(2)}) collective-permute-start(bf16[1792,512]{1,0:T(8,128)(2,1)} %bitcast.34), channel_id=1, source_target_pairs={{0,32},{32,0},{1,33},{33,1},{2,34},{34,2},{3,35},{35,3},{4,36},{36... | collective-permute-start | bytes 5505032 | tf_op jit(solution)/shard_map/weight_swap/ppermute | solution.py:432
  7.8 24.0 %collective-permute-start.7 = (bf16[512,1792]{1,0:T(8,128)(2,1)}, bf16[512,1792]{1,0:T(8,128)(2,1)}, u32[]{:S(2)}, u32[]{:S(2)}) collective-permute-start(bf16[512,1792]{1,0:T(8,128)(2,1)} %bitcast.43), channel_id=1, source_target_pairs={{0,32},{32,0},{1,33},{33,1},{2,34},{34,2},{3,35},{35,3},{4,36},{36... | collective-permute-start | bytes 5505032 | tf_op jit(solution)/shard_map/weight_swap/ppermute | solution.py:433
  10.0 4.2 %collective-permute-start = (s32[1,128]{1,0:T(1,128)S(1)}, s32[1,128]{1,0:T(1,128)S(1)}, u32[]{:S(2)}, u32[]{:S(2)}) collective-permute-start(s32[1,128]{1,0:T(1,128)S(1)} %select_bitcast_fusion.after), channel_id=1, source_target_pairs={{0,3},{1,0},{2,1},{3,2},{4,7},{5,4},{6,5},{7,6},{8,11},{9,8},{10,9... | collective-permute-start | bytes 1544 | tf_op jit(solution)/shard_map/routing/ppermute | solution.py:21
  12.9 6.0 %collective-permute-start.1 = (s32[1,128]{1,0:T(1,128)S(1)}, s32[1,128]{1,0:T(1,128)S(1)}, u32[]{:S(2)}, u32[]{:S(2)}) collective-permute-start(s32[1,128]{1,0:T(1,128)S(1)} %select_bitcast_fusion.after), channel_id=1, source_target_pairs={{0,2},{1,3},{2,0},{3,1},{4,6},{5,7},{6,4},{7,5},{8,10},{9,11},{10,... | collective-permute-start | bytes 1544 | tf_op jit(solution)/shard_map/routing/ppermute | solution.py:21
  14.2 5.0 %collective-permute-start.2 = (s32[1,128]{1,0:T(1,128)S(1)}, s32[1,128]{1,0:T(1,128)S(1)}, u32[]{:S(2)}, u32[]{:S(2)}) collective-permute-start(s32[1,128]{1,0:T(1,128)S(1)} %select_bitcast_fusion.after), channel_id=1, source_target_pairs={{0,1},{1,2},{2,3},{3,0},{4,5},{5,6},{6,7},{7,4},{8,9},{9,10},{10,1... | collective-permute-start | bytes 1544 | tf_op jit(solution)/shard_map/routing/ppermute | solution.py:21
  15.3 12.0 %copy-start.34 = (s32[4]{0:T(128)}, s32[4]{0:T(128)S(1)}, u32[]{:S(2)}) copy-start(s32[4]{0:T(128)S(1)} %pad_add_fusion.1.where_ref) | copy-start | bytes 52
  18.9 8.4 %copy-start = (bf16[512,7168]{1,0:T(8,128)(2,1)}, bf16[512,7168]{1,0:T(8,128)(2,1)S(1)}, u32[]{:S(2)}) copy-start(bf16[512,7168]{1,0:T(8,128)(2,1)S(1)} %load.1.attn) | copy-start | bytes 22020100
  19.2 8.0 %copy-start.26 = (s32[4,128]{1,0:T(4,128)}, s32[4,128]{1,0:T(4,128)S(1)}, u32[]{:S(2)}) copy-start(s32[4,128]{1,0:T(4,128)S(1)} %pad_add_fusion.poses.pos) | copy-start | bytes 6148
  20.1 5.1 %copy-start.41 = (s32[128,8]{0,1:T(8,128)S(1)}, s32[128,8]{0,1:T(8,128)}, u32[]{:S(2)}) copy-start(s32[128,8]{0,1:T(8,128)} %param.11) | copy-start | bytes 12292
  20.1 5.1 %copy-start.42 = (f32[128,8]{0,1:T(8,128)S(1)}, f32[128,8]{0,1:T(8,128)}, u32[]{:S(2)}) copy-start(f32[128,8]{0,1:T(8,128)} %param.12) | copy-start | bytes 12292
  20.2 9.6 %collective-permute-start.3 = (bf16[40,3584]{1,0:T(8,128)(2,1)S(1)}, bf16[40,3584]{1,0:T(8,128)(2,1)S(1)}, u32[]{:S(2)}, u32[]{:S(2)}) collective-permute-start(bf16[40,3584]{1,0:T(8,128)(2,1)S(1)} %get-tuple-element.83), channel_id=1, source_target_pairs={{0,1},{1,2},{2,3},{3,0},{4,5},{5,6},{6,7},{7,4},{8,9},{9,10},{10,1... | collective-permute-start | bytes 860168 | tf_op jit(solution)/shard_map/front_sum/ppermute | solution.py:21
  21.5 9.4 %collective-permute-start.4 = (bf16[40,3584]{1,0:T(8,128)(2,1)S(1)}, bf16[40,3584]{1,0:T(8,128)(2,1)S(1)}, u32[]{:S(2)}, u32[]{:S(2)}) collective-permute-start(bf16[40,3584]{1,0:T(8,128)(2,1)S(1)} %get-tuple-element.84), channel_id=1, source_target_pairs={{0,3},{1,0},{2,1},{3,2},{4,7},{5,4},{6,5},{7,6},{8,11},{9,8},{10,9... | collective-permute-start | bytes 860168 | tf_op jit(solution)/shard_map/front_sum/ppermute | solution.py:21
  29.8 15.9 %copy-start.3 = (bf16[128,7168]{1,0:T(8,128)(2,1)S(1)}, bf16[128,7168]{1,0:T(8,128)(2,1)}, u32[]{:S(2)}) copy-start(bf16[128,7168]{1,0:T(8,128)(2,1)} %residual.7) | copy-start | bytes 5505028
  29.8 10.0 %collective-permute-start.10 = (bf16[40,3584]{1,0:T(8,128)(2,1)}, bf16[40,3584]{1,0:T(8,128)(2,1)S(1)}, u32[]{:S(2)}, u32[]{:S(2)}) collective-permute-start(bf16[40,3584]{1,0:T(8,128)(2,1)} %get-tuple-element.92), channel_id=1, source_target_pairs={{0,3},{1,0},{2,1},{3,2},{4,7},{5,4},{6,5},{7,6},{8,11},{9,8},{10,9... | collective-permute-start | bytes 860168 | tf_op jit(solution)/shard_map/front_sum/ppermute | solution.py:21
  30.9 11.2 %collective-permute-start.9 = (bf16[40,3584]{1,0:T(8,128)(2,1)}, bf16[40,3584]{1,0:T(8,128)(2,1)S(1)}, u32[]{:S(2)}, u32[]{:S(2)}) collective-permute-start(bf16[40,3584]{1,0:T(8,128)(2,1)} %get-tuple-element.91), channel_id=1, source_target_pairs={{0,1},{1,2},{2,3},{3,0},{4,5},{5,6},{6,7},{7,4},{8,9},{9,10},{10,1... | collective-permute-start | bytes 860168 | tf_op jit(solution)/shard_map/front_sum/ppermute | solution.py:21
  31.9 13.8 %copy-start.27 = (s32[4,128]{1,0:T(4,128)S(1)}, s32[4,128]{1,0:T(4,128)}, u32[]{:S(2)}) copy-start(s32[4,128]{1,0:T(4,128)} %copy-done.26) | copy-start | bytes 6148
  31.9 13.8 %copy-start.35 = (s32[4]{0:T(128)S(1)}, s32[4]{0:T(128)}, u32[]{:S(2)}) copy-start(s32[4]{0:T(128)} %copy-done.34) | copy-start | bytes 52
  31.9 11.1 %collective-permute-start.11 = (bf16[40,3584]{1,0:T(8,128)(2,1)S(1)}, bf16[40,3584]{1,0:T(8,128)(2,1)S(1)}, u32[]{:S(2)}, u32[]{:S(2)}) collective-permute-start(bf16[40,3584]{1,0:T(8,128)(2,1)S(1)} %add_convert_fusion.2), channel_id=1, source_target_pairs={{0,3},{1,0},{2,1},{3,2},{4,7},{5,4},{6,5},{7,6},{8,11},{9,8},{10,9... | collective-permute-start | bytes 860168 | tf_op jit(solution)/shard_map/front_sum/ppermute | solution.py:21
  34.4 11.3 %collective-permute-start.8 = (bf16[40,3584]{1,0:T(8,128)(2,1)S(1)}, bf16[40,3584]{1,0:T(8,128)(2,1)S(1)}, u32[]{:S(2)}, u32[]{:S(2)}) collective-permute-start(bf16[40,3584]{1,0:T(8,128)(2,1)S(1)} %add_convert_fusion.3), channel_id=1, source_target_pairs={{0,1},{1,2},{2,3},{3,0},{4,5},{5,6},{6,7},{7,4},{8,9},{9,10},{10,1... | collective-permute-start | bytes 860168 | tf_op jit(solution)/shard_map/front_sum/ppermute | solution.py:21
  52.3 8.2 %copy-start.29 = (s32[4,128]{1,0:T(4,128)S(1)}, s32[4,128]{1,0:T(4,128)}, u32[]{:S(2)}) copy-start(s32[4,128]{1,0:T(4,128)} %copy-done.26) | copy-start | bytes 6148
  52.3 8.3 %copy-start.37 = (s32[4]{0:T(128)S(1)}, s32[4]{0:T(128)}, u32[]{:S(2)}) copy-start(s32[4]{0:T(128)} %copy-done.34) | copy-start | bytes 52
  52.3 22.0 %all-to-all-start = ((bf16[16,8,3584]{2,1,0:T(8,128)(2,1)}), bf16[16,8,3584]{2,1,0:T(8,128)(2,1)S(1)}, u32[]{:S(2)}, u32[]{:S(2)}) async-start(bf16[16,8,3584]{2,1,0:T(8,128)(2,1)} %bitcast.36), calls=%async_computation | async-start | bytes 1835008 | tf_op jit(solution)/shard_map/rows_out/all_to_all | solution.py:461
  60.5 96.3 %reduce-scatter.10.cloned.1.call-start = ((), (), s32[]{:S(2)}) async-start(), calls=%async_computation.6 | async-start | bytes 2365440
  74.6 11.1 %collective-permute-start.12 = (bf16[80,1792]{1,0:T(8,128)(2,1)S(1)}, bf16[80,1792]{1,0:T(8,128)(2,1)S(1)}, u32[]{:S(2)}, u32[]{:S(2)}) collective-permute-start(bf16[80,1792]{1,0:T(8,128)(2,1)S(1)} %get-tuple-element.111.a0), channel_id=1, source_target_pairs={{0,1},{1,2},{2,3},{3,0},{4,5},{5,6},{6,7},{7,4},{8,9},{9,10},{10,1... | collective-permute-start | bytes 860168 | tf_op jit(solution)/shard_map/rows_out/ppermute | solution.py:21
  74.7 11.0 %collective-permute-start.15 = (bf16[80,1792]{1,0:T(8,128)(2,1)S(1)}, bf16[80,1792]{1,0:T(8,128)(2,1)S(1)}, u32[]{:S(2)}, u32[]{:S(2)}) collective-permute-start(bf16[80,1792]{1,0:T(8,128)(2,1)S(1)} %get-tuple-element.115.b0), channel_id=1, source_target_pairs={{0,3},{1,0},{2,1},{3,2},{4,7},{5,4},{6,5},{7,6},{8,11},{9,8},{10,9... | collective-permute-start | bytes 860168 | tf_op jit(solution)/shard_map/rows_out/ppermute | solution.py:21
  77.9 12.5 %collective-permute-start.13 = (bf16[80,1792]{1,0:T(8,128)(2,1)S(1)}, bf16[80,1792]{1,0:T(8,128)(2,1)S(1)}, u32[]{:S(2)}, u32[]{:S(2)}) collective-permute-start(bf16[80,1792]{1,0:T(8,128)(2,1)S(1)} %get-tuple-element.115.b0), channel_id=1, source_target_pairs={{0,1},{1,2},{2,3},{3,0},{4,5},{5,6},{6,7},{7,4},{8,9},{9,10},{10,1... | collective-permute-start | bytes 860168 | tf_op jit(solution)/shard_map/rows_out/ppermute | solution.py:21
  78.6 12.5 %collective-permute-start.17 = (bf16[80,1792]{1,0:T(8,128)(2,1)S(1)}, bf16[80,1792]{1,0:T(8,128)(2,1)S(1)}, u32[]{:S(2)}, u32[]{:S(2)}) collective-permute-start(bf16[80,1792]{1,0:T(8,128)(2,1)S(1)} %get-tuple-element.111.a0), channel_id=1, source_target_pairs={{0,3},{1,0},{2,1},{3,2},{4,7},{5,4},{6,5},{7,6},{8,11},{9,8},{10,9... | collective-permute-start | bytes 860168 | tf_op jit(solution)/shard_map/rows_out/ppermute | solution.py:21
  82.6 12.6 %copy-start.17 = (bf16[80,1792]{1,0:T(8,128)(2,1)S(1)}, bf16[80,1792]{1,0:T(8,128)(2,1)}, u32[]{:S(2)}) copy-start(bf16[80,1792]{1,0:T(8,128)(2,1)} %copy-done.16) | copy-start | bytes 860164
  85.7 9.5 %copy-start.15 = (bf16[80,1792]{1,0:T(8,128)(2,1)S(1)}, bf16[80,1792]{1,0:T(8,128)(2,1)}, u32[]{:S(2)}) copy-start(bf16[80,1792]{1,0:T(8,128)(2,1)} %copy-done.14) | copy-start | bytes 860164
  85.7 7.8 %collective-permute-start.14 = (bf16[80,1792]{1,0:T(8,128)(2,1)S(1)}, bf16[80,1792]{1,0:T(8,128)(2,1)S(1)}, u32[]{:S(2)}, u32[]{:S(2)}) collective-permute-start(bf16[80,1792]{1,0:T(8,128)(2,1)S(1)} %collective-permute-done.12.a1), channel_id=1, source_target_pairs={{0,1},{1,2},{2,3},{3,0},{4,5},{5,6},{6,7},{7,4},{8,9},{9,10},{10,1... | collective-permute-start | bytes 860168 | tf_op jit(solution)/shard_map/rows_out/ppermute | solution.py:21
  85.7 8.6 %collective-permute-start.16 = (bf16[80,1792]{1,0:T(8,128)(2,1)S(1)}, bf16[80,1792]{1,0:T(8,128)(2,1)S(1)}, u32[]{:S(2)}, u32[]{:S(2)}) collective-permute-start(bf16[80,1792]{1,0:T(8,128)(2,1)S(1)} %collective-permute-done.15.b3), channel_id=1, source_target_pairs={{0,3},{1,0},{2,1},{3,2},{4,7},{5,4},{6,5},{7,6},{8,11},{9,8},{10,9... | collective-permute-start | bytes 860168 | tf_op jit(solution)/shard_map/rows_out/ppermute | solution.py:21
  95.0 74.6 %reduce-scatter.8.cloned.1.call-start = ((), (), s32[]{:S(2)}) async-start(), calls=%async_computation.5 | async-start | bytes 1576960 | tf_op jit(solution)/shard_map/rows_back/head_sum/reduce_scatter | solution.py:440
  107.3 16.9 %copy-start.43 = (bf16[1,512,1792]{2,1,0:T(8,128)(2,1)S(1)}, bf16[1,512,1792]{2,1,0:T(8,128)(2,1)}, u32[]{:S(2)}) copy-start(bf16[1,512,1792]{2,1,0:T(8,128)(2,1)} %param.15) | copy-start | bytes 5505028
  107.3 9.8 %collective-permute-start.18 = (bf16[160,1024]{1,0:T(8,128)(2,1)S(1)}, bf16[160,1024]{1,0:T(8,128)(2,1)S(1)}, u32[]{:S(2)}, u32[]{:S(2)}) collective-permute-start(bf16[160,1024]{1,0:T(8,128)(2,1)S(1)} %get-tuple-element.122), channel_id=1, source_target_pairs={{0,64},{64,0},{1,65},{65,1},{2,66},{66,2},{3,67},{67,3},{4,68},{68... | collective-permute-start | bytes 983048 | tf_op jit(solution)/shard_map/gate_up/ppermute | solution.py:467
  117.4 6.9 %collective-permute-start.19 = (bf16[160,512]{1,0:T(8,128)(2,1)S(1)}, bf16[160,512]{1,0:T(8,128)(2,1)S(1)}, u32[]{:S(2)}, u32[]{:S(2)}) collective-permute-start(bf16[160,512]{1,0:T(8,128)(2,1)S(1)} %fusion.1.mine), channel_id=1, source_target_pairs={{0,64},{64,0},{1,65},{65,1},{2,66},{66,2},{3,67},{67,3},{4,68},{68... | collective-permute-start | bytes 491528 | tf_op jit(solution)/shard_map/gate_up/ppermute | solution.py:469
  127.3 9.0 %collective-permute-start.24 = (bf16[80,1792]{1,0:T(8,128)(2,1)S(1)}, bf16[80,1792]{1,0:T(8,128)(2,1)S(1)}, u32[]{:S(2)}, u32[]{:S(2)}) collective-permute-start(bf16[80,1792]{1,0:T(8,128)(2,1)S(1)} %get-tuple-element.131), channel_id=1, source_target_pairs={{0,3},{1,0},{2,1},{3,2},{4,7},{5,4},{6,5},{7,6},{8,11},{9,8},{10,9... | collective-permute-start | bytes 860168 | tf_op jit(solution)/shard_map/rows_back/ppermute | solution.py:21
  129.8 10.4 %collective-permute-start.20 = (bf16[80,1792]{1,0:T(8,128)(2,1)S(1)}, bf16[80,1792]{1,0:T(8,128)(2,1)S(1)}, u32[]{:S(2)}, u32[]{:S(2)}) collective-permute-start(bf16[80,1792]{1,0:T(8,128)(2,1)S(1)} %get-tuple-element.127), channel_id=1, source_target_pairs={{0,1},{1,2},{2,3},{3,0},{4,5},{5,6},{6,7},{7,4},{8,9},{9,10},{10,1... | collective-permute-start | bytes 860168 | tf_op jit(solution)/shard_map/rows_back/ppermute | solution.py:21
  129.8 13.2 %collective-permute-start.22 = (bf16[80,1792]{1,0:T(8,128)(2,1)S(1)}, bf16[80,1792]{1,0:T(8,128)(2,1)S(1)}, u32[]{:S(2)}, u32[]{:S(2)}) collective-permute-start(bf16[80,1792]{1,0:T(8,128)(2,1)S(1)} %get-tuple-element.128), channel_id=1, source_target_pairs={{0,1},{1,2},{2,3},{3,0},{4,5},{5,6},{6,7},{7,4},{8,9},{9,10},{10,1... | collective-permute-start | bytes 860168 | tf_op jit(solution)/shard_map/rows_back/ppermute | solution.py:21
  129.8 13.2 %collective-permute-start.23 = (bf16[80,1792]{1,0:T(8,128)(2,1)S(1)}, bf16[80,1792]{1,0:T(8,128)(2,1)S(1)}, u32[]{:S(2)}, u32[]{:S(2)}) collective-permute-start(bf16[80,1792]{1,0:T(8,128)(2,1)S(1)} %get-tuple-element.129), channel_id=1, source_target_pairs={{0,3},{1,0},{2,1},{3,2},{4,7},{5,4},{6,5},{7,6},{8,11},{9,8},{10,9... | collective-permute-start | bytes 860168 | tf_op jit(solution)/shard_map/rows_back/ppermute | solution.py:21
  136.4 7.9 %collective-permute-start.25 = (bf16[80,1792]{1,0:T(8,128)(2,1)S(1)}, bf16[80,1792]{1,0:T(8,128)(2,1)S(1)}, u32[]{:S(2)}, u32[]{:S(2)}) collective-permute-start(bf16[80,1792]{1,0:T(8,128)(2,1)S(1)} %add_convert_fusion), channel_id=1, source_target_pairs={{0,3},{1,0},{2,1},{3,2},{4,7},{5,4},{6,5},{7,6},{8,11},{9,8},{10,9... | collective-permute-start | bytes 860168 | tf_op jit(solution)/shard_map/rows_back/ppermute | solution.py:21
  140.2 7.9 %collective-permute-start.21 = (bf16[80,1792]{1,0:T(8,128)(2,1)S(1)}, bf16[80,1792]{1,0:T(8,128)(2,1)S(1)}, u32[]{:S(2)}, u32[]{:S(2)}) collective-permute-start(bf16[80,1792]{1,0:T(8,128)(2,1)S(1)} %add_convert_fusion.1), channel_id=1, source_target_pairs={{0,1},{1,2},{2,3},{3,0},{4,5},{5,6},{6,7},{7,4},{8,9},{9,10},{10,1... | collective-permute-start | bytes 860168 | tf_op jit(solution)/shard_map/rows_back/ppermute | solution.py:21
  149.5 3.7 %copy-start.30 = (s32[4,128]{1,0:T(4,128)S(1)}, s32[4,128]{1,0:T(4,128)}, u32[]{:S(2)}) copy-start(s32[4,128]{1,0:T(4,128)} %copy-done.26) | copy-start | bytes 6148
  149.5 16.2 %all-to-all-start.1 = ((bf16[16,8,3584]{2,1,0:T(8,128)(2,1)}), bf16[16,8,3584]{2,1,0:T(8,128)(2,1)S(1)}, u32[]{:S(2)}, u32[]{:S(2)}) async-start(bf16[16,8,3584]{2,1,0:T(8,128)(2,1)} %bitcast.18), calls=%async_computation.2 | async-start | bytes 1835008 | tf_op jit(solution)/shard_map/rows_back/all_to_all | solution.py:474
  157.8 8.0 %copy-start.31 = (bf16[64,128]{1,0:T(8,128)(2,1)S(1)}, bf16[64,128]{1,0:T(8,128)(2,1)}, u32[]{:S(2)}) copy-start(bf16[64,128]{1,0:T(8,128)(2,1)} %convert_element_type.60.high) | copy-start | bytes 49156
  157.8 8.0 %copy-start.32 = (bf16[64,128]{1,0:T(8,128)(2,1)S(1)}, bf16[64,128]{1,0:T(8,128)(2,1)}, u32[]{:S(2)}) copy-start(bf16[64,128]{1,0:T(8,128)(2,1)} %convert_element_type.61.low) | copy-start | bytes 49156
  157.8 8.0 %copy-start.39 = (s32[4]{0:T(128)S(1)}, s32[4]{0:T(128)}, u32[]{:S(2)}) copy-start(s32[4]{0:T(128)} %copy-done.34) | copy-start | bytes 52
  (27 other events, 33.6 us)
Sparse Core Ops, SparseCore 0:
  45.8 27.9 reduce-scatter.11
  95.1 25.4 reduce-scatter.9
  149.7 19.8 reduce-scatter.7
